TPU v7x, 512 devices: a whole 4x4x16 slice. The times are simulated.
512 devices in a mesh: group: 32 (over z, y_lo), sample: 16 (over y_hi, x, core).
Axes of the slice: x: 4, y: 4 (y_hi: 2, y_lo: 2; y = y_hi * 2 + y_lo), z: 16, core: 2. Of those that a mesh axis runs over, the one named last changes fastest.
Arguments:
- trainer_flat: bfloat16 [512, 6480], P(('group', 'sample')), may hold values from -0.109375 to 0.109375
- matching: int32 [512], replicated, may hold values from 0 to 511, each once
- prefix_kv: bfloat16 [32, 8192, 128], P('group', 'sample'), may hold values from -500 to 500
- prefix_blocks: int32 [32], P('group'), may hold values from 1 to 64, as said below
- inputs: bfloat16 [4, 32, 128, 2880], P(None, 'group', 'sample'), may hold values from -6 to 6
Outputs:
- attended: bfloat16 [4, 32, 128, 2880], P(None, 'group', 'sample')
Inputs may be any that keep to these rules, and one draw needn't show every extreme that they name: `prefix_blocks`: some prompt's prefix fills all 8192 positions in every draw.
All inputs are finite; a program needn't handle non-finite values.
Results may differ from a plain program's by a relative error of at most 0.025.
Values may be sent and summed in bfloat16 or wider, within the bound.
No kernel may reach another device: no remote copies, remote signals or barrier semaphores. Data moves between devices by JAX's collectives and lax.ppermute only.
A program may use at most 64 MiB of HBM per device.

v0:
```python
import jax
import jax.numpy as jnp
from jax import lax
from jax.sharding import PartitionSpec as P

D = 2880
HEAD = 64
QHEADS = 8


def pick_block(length, wanted):
    width = min(wanted, length)
    while length % width != 0:
        width = width - 1
    return width


def start_state(count):
    return (
        jnp.full((count,), -1e30, jnp.float32),
        jnp.zeros((count,), jnp.float32),
        jnp.zeros((count, HEAD), jnp.float32),
    )


def attend_keys(carry, query_rows, piece, limit, scale):
    length = piece.shape[0]
    block_len = pick_block(length, 2048)

    def step_block(index, state):
        running, total, summed = state
        window = lax.dynamic_slice_in_dim(piece, index * block_len, block_len, 0)
        scores = (
            lax.dot_general(
                query_rows,
                window[:, :HEAD],
                (((1,), (1,)), ((), ())),
                preferred_element_type=jnp.float32,
            )
            * scale
        )
        places = index * block_len + jnp.arange(block_len, dtype=jnp.int32)
        valid = (places < limit)[None, :]
        scores = jnp.where(valid, scores, jnp.float32(-1e30))
        raised = jnp.maximum(running, jnp.max(scores, -1))
        weights = jnp.where(valid, jnp.exp(scores - raised[:, None]), 0.0).astype(jnp.bfloat16)
        factor = jnp.exp(running - raised)
        total = factor * total + jnp.sum(weights, -1, dtype=jnp.float32)
        summed = factor[:, None] * summed + jnp.dot(
            weights, window[:, HEAD:], preferred_element_type=jnp.float32
        )
        return (raised, total, summed)

    return lax.fori_loop(0, length // block_len, step_block, carry)


def shards(trainer_flat, matching, prefix_kv, prefix_blocks, inputs):
    tiles = lax.all_gather(trainer_flat, ("group", "sample"), axis=0, tiled=True)
    count = tiles.shape[0]
    source = jnp.zeros((count,), jnp.int32).at[matching].set(jnp.arange(count, dtype=jnp.int32))
    flat_all = tiles[source].reshape(-1)
    query_width = QHEADS * HEAD
    width_in = query_width + 2 * HEAD
    weight_in = flat_all[: D * width_in].reshape(D, width_in)
    weight_out = flat_all[D * width_in :].reshape(query_width, D)
    scale = HEAD ** (-0.5)
    steps = inputs.shape[0]
    samples = inputs.shape[2]
    rows = steps * samples * QHEADS
    prefix_local = prefix_kv[0]
    limit = prefix_blocks[0] * 128
    projected = jnp.dot(
        inputs[:, 0].reshape(steps * samples, D), weight_in, preferred_element_type=jnp.float32
    )
    query = projected[:, :query_width].astype(jnp.bfloat16)
    own_keys = (
        projected[:, query_width : query_width + HEAD]
        .astype(jnp.bfloat16)
        .reshape(steps, samples, HEAD)
    )
    own_values = (
        projected[:, query_width + HEAD :].astype(jnp.bfloat16).reshape(steps, samples, HEAD)
    )
    own_scores = (
        jnp.einsum(
            "tshd,jsd->tshj",
            query.reshape(steps, samples, QHEADS, HEAD),
            own_keys,
            preferred_element_type=jnp.float32,
        )
        * scale
    )
    earlier = (jnp.arange(steps)[None, :] <= jnp.arange(steps)[:, None])[:, None, None, :]
    own_scores = jnp.where(earlier, own_scores, jnp.float32(-1e30)).reshape(rows, steps)
    query_rows = query.reshape(rows, HEAD)
    peak, total_prefix, summed_prefix = attend_keys(
        start_state(rows),
        query_rows,
        lax.all_gather(prefix_local, "sample", axis=0, tiled=True),
        limit,
        scale,
    )
    peaks = peak[None]
    totals = total_prefix[None]
    sums = summed_prefix[None]
    top = jnp.maximum(jnp.max(peaks, 0), jnp.max(own_scores, -1))
    factor = jnp.exp(peaks - top[None])
    own_weights = jnp.exp(own_scores - top[:, None]).astype(jnp.bfloat16)
    total = jnp.sum(factor * totals, 0) + jnp.sum(own_weights, -1, dtype=jnp.float32)
    summed = jnp.sum(factor[..., None] * sums, 0)
    summed = summed + jnp.einsum(
        "tshj,jsd->tshd",
        own_weights.reshape(steps, samples, QHEADS, steps),
        own_values,
        preferred_element_type=jnp.float32,
    ).reshape(rows, HEAD)
    attended_rows = (
        (summed / total[:, None]).astype(jnp.bfloat16).reshape(steps * samples, query_width)
    )
    output = jnp.dot(attended_rows, weight_out, preferred_element_type=jnp.float32).astype(
        jnp.bfloat16
    )
    return output.reshape(steps, 1, samples, D)


def solution(mesh):
    in_specs = (
        P(("group", "sample"), None),
        P(),
        P("group", "sample", None),
        P("group"),
        P(None, "group", "sample", None),
    )
    out_specs = P(None, "group", "sample", None)
    return jax.shard_map(shards, mesh=mesh, in_specs=in_specs, out_specs=out_specs, check_vma=False)
```

profile of v0, /device:TPU:1, one launch (start us, length us, event | category | flops | bytes accessed | tf_op | source)
XLA Modules:
  0.0 940.1 jit_solution(5019184150910429435)
XLA Ops:
  6.5 0.7 all-gather.7.cloned.1.call-update
  7.3 0.7 all-gather.5.cloned.1.call-update
  8.7 0.7 compare_select_fusion.1
  9.4 2.4 scatter_custom_fusion
  11.9 832.4 %all-gather.7.cloned.1.call-done = bf16[512,1,6480]{2,1,0:T(2,128)(2,1)} async-done(((bf16[1,1,6480]{2,1,0:T(2,128)(2,1)}), bf16[512,1,6480]{2,1,0:T(2,128)(2,1)}) %all-gather.7.cloned.1.call-update) | async-done | bytes 6635536 | tf_op jit(solution)/shard_map/all_gather | solution.py:58
  844.2 8.3 copy.53
  852.5 16.8 %gather_fusion = bf16[512,6480]{1,0:T(8,128)(2,1)} fusion(bf16[512,6480]{1,0:T(8,128)(2,1)} %bitcast.35, s32[1024]{0:T(1024)S(1)} %pad_clamp_fusion), kind=kCustom, calls=%fused_computation | custom fusion | bytes 13273088 | tf_op jit(solution)/shard_map/gather | solution.py:61
  869.4 15.7 %slice.38 = bf16[5184,640]{1,0:T(8,128)(2,1)} reshape(bf16[512,6480]{1,0:T(8,128)(2,1)} %gather_fusion) | data formatting | bytes 13271040 | tf_op jit(solution)/shard_map/slice | solution.py:64
  885.1 2.7 fusion.15
  888.0 15.8 %slice.43 = bf16[1152,2880]{1,0:T(8,128)(2,1)} reshape(bf16[512,6480]{1,0:T(8,128)(2,1)} %gather_fusion) | data formatting | bytes 13271040 | tf_op jit(solution)/shard_map/slice | solution.py:65
  904.4 6.9 all-gather.5.cloned.1.call-done
  911.3 17.7 %while.18 = (s32[]{:T(128)}, f32[256]{0:T(256)S(1)}, f32[256]{0:T(256)S(1)}, f32[256,64]{0,1:T(8,128)S(1)}, s32[]{:T(128)}, /*index=5*/bf16[8192,128]{1,0:T(8,12...) while((s32[]{:T(128)}, f32[256]{0:T(256)S(1)}, ...), condition=%wide.region_4.5_spmd.clone, body=%wide.region_1.4_spmd.clone.sunk | while | flops 140039424 | bytes 7528655 | solution.py:54
  911.3 1.7 fusion.34
  913.0 0.5 convert_reduce_fusion.3
  913.5 2.1 convolution_add_fusion.2
  915.7 1.7 fusion.34
  917.5 0.5 convert_reduce_fusion.3
  918.0 2.1 convolution_add_fusion.2
  920.2 1.7 fusion.34
  921.9 0.5 convert_reduce_fusion.3
  922.4 2.1 convolution_add_fusion.2
  924.6 1.7 fusion.34
  926.8 2.1 convolution_add_fusion.2
  930.1 3.1 fusion.8
  (51 shorter events, 2.6 us)
Async XLA Ops:
  6.5 878.5 %copy-start = (bf16[4,1,8,2880]{3,2,1,0:T(8,128)(2,1)S(1)}, bf16[4,1,8,2880]{3,2,1,0:T(8,128)(2,1)}, u32[]{:S(2)}) copy-start(bf16[4,1,8,2880]{3,2,1,0:T(8,128)(2,1)} %param.11) | copy-start | bytes 552964
  6.5 837.7 %all-gather.7.cloned.1.call-start = ((), (), s32[]{:S(2)}) async-start(), calls=%async_computation.1 | async-start | bytes 13395456 | tf_op jit(solution)/shard_map/all_gather | solution.py:58
  7.3 904.0 %all-gather.5.cloned.1.call-start = ((), (), s32[]{:S(2)}) async-start(), calls=%async_computation | async-start | bytes 2228224 | tf_op jit(solution)/shard_map/all_gather | solution.py:99
Sparse Core Ops, SparseCore 0:
  9.6 834.6 all-gather.6
  847.6 63.6 all-gather.4
where the time goes:
time: 941 us; the launch traced here: 940 us
  waiting for transfers between devices  841 us (89%)
  local copies, waits for them, and re-layouts  60.2 us (6%)
  matrix products  21.9 us (2%)
  between operations  14.2 us (2%)
    all_gather x1, waiting for transfers between devices, shards(): lax.all_gather(trainer_flat, ('group', 'sample'), axis=0, tiled=True)  832 us
  transfers between devices with their start and end apart: 2, of which 2 were waited for; matrix products, arithmetic and copies ran while one was open for 7% of the time, Pallas kernels for 0%

commit v1 on v0

v1 whole, which is shorter than its diff:
```python
import functools

import jax
import jax.numpy as jnp
import numpy as np
from jax import lax
from jax.experimental import pallas as pl
from jax.experimental.pallas import tpu as pltpu
from jax.sharding import PartitionSpec as P

D = 2880
HEAD = 64
QHEADS = 8
AXES = ("group", "sample")
TILE = 6480
IN_ROWS = 2880
IN_SIZE = 2880 * 640
SLOT = 56
USED = 55
ROWS = 32
VMEM = pl.BlockSpec(memory_space=pltpu.VMEM)
SMEM = pl.BlockSpec(memory_space=pltpu.SMEM)
MIB = 1024 * 1024


def device_id(z, y, x, core):
    return z * 32 + (y % 2) * 16 + (y // 2) * 8 + x * 2 + core


Z_GROUPS = [
    [device_id(z, y, x, c) for z in range(16)] for y in range(4) for x in range(4) for c in range(2)
]


def line_groups(x_core):
    along_x = [[device_id(z, y, x, x_core) for x in range(4)] for z in range(16) for y in range(4)]
    along_y = [
        [device_id(z, y, x, 1 - x_core) for y in range(4)] for z in range(16) for x in range(4)
    ]
    return along_x + along_y


def moves(step):
    pairs = []
    for z in range(16):
        for y in range(4):
            for x in range(4):
                for c in range(2):
                    y2, x2, c2 = step(y, x, c)
                    pairs.append((device_id(z, y, x, c), device_id(z, y2 % 4, x2 % 4, c2)))
    return pairs


CORE_SWAP = moves(lambda y, x, c: (y, x, 1 - c))
X_UP = moves(lambda y, x, c: (y, x + 1, c))
X_DOWN = moves(lambda y, x, c: (y, x - 1, c))
Y_FAR = moves(lambda y, x, c: (y + 2, x, c))
RING_UP = moves(lambda y, x, c: (y, x + 1, c) if c else (y + 1, x, c))
RING_DOWN = moves(lambda y, x, c: (y, x - 1, c) if c else (y - 1, x, c))


def form_kernel(matching_ref, tile_ref, out_ref, buf_ref):
    me = lax.axis_index("group") * 16 + lax.axis_index("sample")
    place = matching_ref[me]
    buf_ref[...] = jnp.zeros((64, 128), jnp.float32)
    for r in range(50):
        buf_ref[r : r + 1, :] = tile_ref[:, 128 * r : 128 * r + 128].astype(jnp.float32)
    buf_ref[50:51, :80] = tile_ref[:, 6400:6480].astype(jnp.float32)
    raw = buf_ref[...]
    row = lax.broadcasted_iota(jnp.int32, (64, 128), 0)
    lane = lax.broadcasted_iota(jnp.int32, (64, 128), 1)
    in_len = jnp.clip(IN_SIZE - TILE * place, 0, TILE)
    part = jnp.where(row * 128 + lane < in_len, raw, 0.0)
    shift = 80 * (place & 7)
    lanes = shift & 127
    turned = pltpu.roll(part, lanes, 1)
    above = pltpu.roll(turned, 1, 0)
    shifted = pltpu.roll(jnp.where(lane >= lanes, turned, above), shift >> 7, 0)
    units = []
    lane8 = lax.broadcasted_iota(jnp.int32, (8, 128), 1)
    row8 = lax.broadcasted_iota(jnp.int32, (8, 128), 0)
    for i in range(9):
        base, off = divmod(720 * i, 128)
        window = buf_ref[base : base + 8, :]
        if off:
            window = pltpu.roll(window, 128 - off, 1)
            below = pltpu.roll(window, 7, 0)
            window = jnp.where(lane8 < 128 - off, window, below)
        units.append(jnp.where((row8 < 5) | (lane8 < 80), window, 0.0)[:6])
    for i in range(9):
        buf_ref[1 + 6 * i : 7 + 6 * i, :] = units[i]
    first = 1 + 6 * jnp.clip(2560 - 9 * place, 0, 9)
    out = jnp.where((row >= first) & (row < 55), buf_ref[...], 0.0) + shifted
    out = out[:SLOT].astype(jnp.bfloat16)
    for j in range(out_ref.shape[0]):
        out_ref[j] = out


def merge_kernel(in_ref, out_ref, buf_ref):
    for j in range(16):
        buf_ref[SLOT * j : SLOT * j + SLOT, :] = in_ref[j].astype(jnp.float32)
    for r in range(USED):
        low = buf_ref[pl.ds(r, 8, stride=SLOT), :]
        high = buf_ref[pl.ds(r + 8 * SLOT, 8, stride=SLOT), :]
        both = jnp.concatenate([low, high], 0).astype(jnp.bfloat16)
        for k in range(out_ref.shape[0]):
            out_ref[k, r] = both


def read_weights(refs, rows):
    columns = []
    for r in rows:
        columns.append(jnp.concatenate([ref[:, r].reshape(-1, 128) for ref in refs], 0))
    return jnp.concatenate(columns, 1)


def chip_place():
    group, sample = lax.axis_index("group"), lax.axis_index("sample")
    core = sample & 1
    x = (sample >> 1) & 3
    y = (sample >> 3) * 2 + (group & 1)
    return y, x, core


def ring_offset(piece):
    return jnp.where(piece == 0, 0, jnp.where(piece == 1, 3, piece - 1))


def slot_places(matching_row):
    y0, x0, core0 = chip_place()
    slot = lax.broadcasted_iota(jnp.int32, (1, 512), 1)
    core = core0 ^ (slot >> 8)
    offset = ring_offset((slot >> 6) & 3)
    line = (slot >> 4) & 3
    y = jnp.where(core == 0, (y0 + offset) & 3, line)
    x = jnp.where(core == 0, line, (x0 + offset) & 3)
    device = (slot & 15) * 32 + (y & 1) * 16 + (y >> 1) * 8 + x * 2 + core
    rows = lax.broadcasted_iota(jnp.int32, (512, 512), 0)
    chosen = jnp.where(rows == device, 1.0, 0.0).astype(jnp.bfloat16)
    row = lax.broadcasted_iota(jnp.int32, (8, 512), 0)
    digits = jnp.where(row == 0, matching_row >> 4, jnp.where(row == 1, matching_row & 15, 0))
    picked = jnp.dot(
        digits.astype(jnp.float32).astype(jnp.bfloat16), chosen, preferred_element_type=jnp.float32
    ).astype(jnp.int32)
    return picked[0:1] * 16 + picked[1:2]


def pick_kernel(x_ref, matching_ref, xg_ref, place_ref, xs_ref, a_ref):
    place = slot_places(matching_ref[...])
    place_ref[...] = place
    xs_ref[:, 2816:] = jnp.zeros((ROWS, 256), jnp.float32)
    xs_ref[:, :D] = x_ref[...].astype(jnp.float32).reshape(ROWS, D)
    xs = xs_ref[...]
    for i in range(11):
        moved = xs if i == 0 else pltpu.roll(xs, 3072 - i, 1)
        a_ref[ROWS * i : ROWS * i + ROWS, :] = moved.astype(jnp.bfloat16)
    start = jnp.where(place <= 284, 10 * place + (place >> 3), -1)
    total = None
    for k in range(12):
        rows = lax.broadcasted_iota(jnp.int32, (256, 512), 0) + 256 * k
        chosen = jnp.where(rows == start, 1.0, 0.0).astype(jnp.bfloat16)
        term = jnp.dot(
            a_ref[:, 256 * k : 256 * k + 256], chosen, preferred_element_type=jnp.float32
        )
        total = term if total is None else total + term
    xg_ref[...] = total.astype(jnp.bfloat16)


def project(xg_ref, halves):
    blocks = []
    for cols in ((0, 1), (2, 3), (4,)):
        total = None
        for half in range(2):
            for i in range(11):
                term = jnp.dot(
                    xg_ref[ROWS * i : ROWS * i + ROWS, 256 * half : 256 * half + 256],
                    read_weights(halves[half], [5 * i + b for b in cols]),
                    preferred_element_type=jnp.float32,
                )
                total = term if total is None else total + term
        blocks.append(total)
    return jnp.concatenate(blocks, 1)


CHUNK = 1024
SHARD = 512


def tail_kernel(
    limit_ref, xg_ref, place_ref, m0, m1, m2, m3, m4, o0, o1, o2, o3, o4, near_ref, far_ref, out_ref,
    s_ref, w_ref, og_ref, acc_ref,
):
    halves = ((m0, m1, m2, m3, m4), (o0, o1, o2, o3, o4))
    projected = project(xg_ref, halves)
    y0, x0, core0 = chip_place()
    rounded = projected.astype(jnp.bfloat16)
    own_kv = rounded[:, 512:640]
    heads = []
    zero = jnp.zeros((ROWS, HEAD), jnp.float32)
    for h in range(QHEADS):
        heads.append(jnp.concatenate([projected[:, HEAD * h : HEAD * h + HEAD], zero], 1))
    query = jnp.concatenate(heads, 0).astype(jnp.bfloat16)
    count = QHEADS * ROWS
    scale = np.float32(HEAD**-0.5 * np.log2(np.e))
    contract = (((1,), (1,)), ((), ()))
    limit = limit_ref[0] * 128

    own = lax.dot_general(query, own_kv, contract, preferred_element_type=jnp.float32)
    row = lax.broadcasted_iota(jnp.int32, (count, ROWS), 0)
    col = lax.broadcasted_iota(jnp.int32, (count, ROWS), 1)
    allowed = ((row & 7) == (col & 7)) & ((col >> 3) <= ((row >> 3) & 3))
    own = jnp.where(allowed, own, -1e30)

    chunks = 16 * SHARD // CHUNK
    def read_keys(k):
        ref = near_ref if k < chunks // 2 else far_ref
        first = CHUNK * (k % (chunks // 2))
        return ref[first : first + CHUNK, :]

    peak = jnp.full((count, 128), -1e30, jnp.float32)
    for k in range(chunks):
        scores = lax.dot_general(
            query, read_keys(k), contract, preferred_element_type=jnp.float32
        )
        bias = []
        for n in range(CHUNK // SHARD * k, CHUNK // SHARD * (k + 1)):
            x = (x0 + (0, 3, 1, 2)[n & 3]) & 3
            shard = ((y0 >> 1) ^ ((n >> 2) & 1)) * 8 + x * 2 + (core0 ^ (n >> 3))
            keys = lax.broadcasted_iota(jnp.int32, (1, SHARD), 1)
            bias.append(jnp.where(keys < limit - SHARD * shard, 0.0, -1e30))
        scores = scores + jnp.concatenate(bias, 1)
        s_ref[:, CHUNK * k : CHUNK * k + CHUNK] = scores
        for n in range(CHUNK // 128):
            peak = jnp.maximum(peak, scores[:, 128 * n : 128 * n + 128])
    top = jnp.maximum(jnp.max(peak, 1, keepdims=True), jnp.max(own, 1, keepdims=True))
    floor = top * scale

    ones = jnp.float32(1)

    def with_ones(piece):
        lane = lax.broadcasted_iota(jnp.int32, piece.shape, 1)
        return jnp.where(lane < HEAD, ones, piece.astype(jnp.float32)).astype(jnp.bfloat16)

    weights = jnp.where(allowed, jnp.exp2(own * scale - floor), 0.0).astype(jnp.bfloat16)
    summed = jnp.dot(weights, with_ones(own_kv), preferred_element_type=jnp.float32)
    for k in range(chunks):
        weights = jnp.exp2(s_ref[:, CHUNK * k : CHUNK * k + CHUNK] * scale - floor)
        summed = summed + jnp.dot(
            weights.astype(jnp.bfloat16),
            with_ones(read_keys(k)),
            preferred_element_type=jnp.float32,
        )
    mixed = summed[:, HEAD:] / summed[:, :HEAD]
    og_ref[...] = jnp.zeros(og_ref.shape, jnp.float32)
    for h in range(QHEADS):
        og_ref[:, 128 + HEAD * h : 128 + HEAD * h + HEAD] = mixed[ROWS * h : ROWS * h + ROWS]

    place = place_ref[...]
    unit = 9 * place - 2560
    base = (unit >> 2) + 1
    shown = jnp.where(place >= 284, base, -1)
    padded = og_ref[...]
    moved = [
        pltpu.roll(padded, 1, 1)[:, 128:640],
        padded[:, 128:640],
        pltpu.roll(padded, 767, 1)[:, 128:640],
    ]
    stacked = jnp.concatenate(moved, 0).astype(jnp.bfloat16)
    chosen = jnp.where(
        lax.broadcasted_iota(jnp.int32, (512, 512), 0) == shown, 1.0, 0.0
    ).astype(jnp.bfloat16)
    picked = jnp.dot(stacked, chosen, preferred_element_type=jnp.float32)
    phase = unit & 3
    for i in range(9):
        for c in range(4):
            wanted = (c - i) % 4
            d = (wanted + i) // 4
            w_ref[ROWS * c : ROWS * c + ROWS, 512 * i : 512 * i + 512] = jnp.where(
                phase == wanted, picked[ROWS * d : ROWS * d + ROWS], 0.0
            ).astype(jnp.bfloat16)
    acc_ref[...] = jnp.zeros(acc_ref.shape, jnp.float32)
    sides = []
    for cols in ((0, 1), (2, 3), (4, 5)):
        total = None
        for i in range(9):
            for half in range(2):
                term = jnp.dot(
                    w_ref[:, 512 * i + 256 * half : 512 * i + 256 * half + 256],
                    read_weights(halves[half], [1 + 6 * i + b for b in cols]),
                    preferred_element_type=jnp.float32,
                )
                total = term if total is None else total + term
        sides.append(total)
    sides.append(jnp.zeros((4 * ROWS, 128), jnp.float32))
    wide = jnp.concatenate(sides, 1)
    for c in range(4):
        first, off = divmod(720 * c, 128)
        block = wide[ROWS * c : ROWS * c + ROWS]
        if off:
            block = pltpu.roll(block, off, 1)
        span = pl.ds(128 * first, 896)
        acc_ref[:, span] = acc_ref[:, span] + block
    out_ref[...] = acc_ref[:, :D].reshape(out_ref.shape).astype(jnp.bfloat16)


def shards(trainer_flat, matching, prefix_kv, prefix_blocks, inputs):
    bf16, f32 = jnp.bfloat16, jnp.float32
    core = lax.axis_index("sample") % 2
    by_place = matching.reshape(16, 2, 2, 4, 2)
    half0 = by_place[..., 0].transpose(2, 1, 3, 0).reshape(1, 256)
    half1 = by_place[..., 1].transpose(3, 2, 1, 0).reshape(1, 256)
    places = jnp.where(
        core == 0, jnp.concatenate([half0, half1], 1), jnp.concatenate([half1, half0], 1)
    )
    x = inputs[:, 0]
    x = inputs[:, 0]
    prefix = prefix_kv[0]
    below = lax.ppermute(prefix, AXES, X_UP)
    above = lax.ppermute(prefix, AXES, X_DOWN)
    across = lax.ppermute(below, AXES, X_UP)
    line_keys = lax.concatenate([prefix, below, above, across], 0)
    far_keys = lax.ppermute(line_keys, AXES, Y_FAR)
    core_keys = lax.concatenate([line_keys, far_keys], 0)
    other_keys = lax.ppermute(core_keys, AXES, CORE_SWAP)

    formed = pl.pallas_call(
        form_kernel,
        out_shape=jax.ShapeDtypeStruct((16, SLOT, 128), bf16),
        in_specs=[SMEM, VMEM],
        out_specs=VMEM,
        scratch_shapes=[pltpu.VMEM((64, 128), f32)],
        name="form",
    )(matching, trainer_flat)
    along_z = lax.all_to_all(formed, AXES, 0, 0, tiled=True, axis_index_groups=Z_GROUPS)
    merged = pl.pallas_call(
        merge_kernel,
        out_shape=jax.ShapeDtypeStruct((4, USED, 16, 128), bf16),
        in_specs=[VMEM],
        out_specs=VMEM,
        scratch_shapes=[pltpu.VMEM((16 * SLOT, 128), f32)],
        name="merge",
    )(along_z)
    lines = lax.all_to_all(merged, AXES, 0, 0, tiled=True, axis_index_groups=line_groups(0))
    low = lax.ppermute(lines, AXES, RING_UP)
    high = lax.ppermute(lines, AXES, RING_DOWN)
    end0 = lax.ppermute(low[:2], AXES, RING_UP)
    end1 = lax.ppermute(high[2:], AXES, RING_DOWN)
    mine = [lines, low, high, end0, end1]
    other = [lax.ppermute(piece, AXES, CORE_SWAP) for piece in mine]
    gathered, places = pl.pallas_call(
        pick_kernel,
        out_shape=(
            jax.ShapeDtypeStruct((11 * ROWS, 512), bf16),
            jax.ShapeDtypeStruct((1, 512), jnp.int32),
        ),
        in_specs=[VMEM] * 2,
        out_specs=(VMEM, VMEM),
        scratch_shapes=[pltpu.VMEM((ROWS, 3072), f32), pltpu.VMEM((11 * ROWS, 3072), bf16)],
        compiler_params=pltpu.CompilerParams(vmem_limit_bytes=40 * MIB),
        name="pick",
    )(x, matching.reshape(1, 512))
    output = pl.pallas_call(
        tail_kernel,
        out_shape=jax.ShapeDtypeStruct(x.shape, bf16),
        in_specs=[SMEM] + [VMEM] * 14,
        out_specs=VMEM,
        scratch_shapes=[
            pltpu.VMEM((QHEADS * ROWS, 16 * SHARD), f32),
            pltpu.VMEM((4 * ROWS, 9 * 512), bf16),
            pltpu.VMEM((ROWS, 768), f32),
            pltpu.VMEM((ROWS, 3072), f32),
        ],
        compiler_params=pltpu.CompilerParams(vmem_limit_bytes=50 * MIB),
        name="tail",
    )(prefix_blocks, gathered, places, *mine, *other, core_keys, other_keys)
    return output[:, None]


def solution(mesh):
    in_specs = (
        P(("group", "sample"), None),
        P(),
        P("group", "sample", None),
        P("group"),
        P(None, "group", "sample", None),
    )
    out_specs = P(None, "group", "sample", None)
    return jax.shard_map(shards, mesh=mesh, in_specs=in_specs, out_specs=out_specs, check_vma=False)
```

time: 941 us -> 104 us (0.11)
  waiting for transfers between devices: 841 us -> 13.6 us
  starting transfers between devices: 0.04 us -> 69.4 us
  local copies, waits for them, and re-layouts: 60.2 us -> 3.01 us
  matrix products: 21.9 us -> 0 us
  Pallas kernels: 0 us -> 15.7 us
  between operations: 14.2 us -> 1.04 us
    all_gather x2 -> x0, waiting for transfers between devices: 839 us -> none  [the longest x1 832 us: shards(): lax.all_gather(trainer_flat, ('group', 'sample'), axis=0, tiled=True)]
    ppermute x0 -> x14, starting transfers between devices: none -> 50.1 us  [the longest x5 15.8 us: shards(): other = [lax.ppermute(piece, AXES, CORE_SWAP) for piece in mine]]
    slice x3 -> x2, local copies, waits for them, and re-layouts: 31.5 us -> 0.06 us  [the longest x1 0.03 us: shards(): end1 = lax.ppermute(high[2:], AXES, RING_DOWN)]
    dot_general x12 -> x0, matrix products: 21.9 us -> none  [the longest x4 8.58 us: step_block(): jnp.dot(weights, window[:, HEAD:], preferred_element_type=jnp.float32)]
    all_to_all x0 -> x2, starting transfers between devices: none -> 19.4 us  [the longest x1 15.9 us: shards(): lax.all_to_all(formed, AXES, 0, 0, tiled=True, axis_index_groups=Z_GROUPS)]
    gather x1 -> x0, local copies, waits for them, and re-layouts: 16.8 us -> none  [shards(): flat_all = tiles[source].reshape(-1)]
    pallas_call x0 -> x4, Pallas kernels: none -> 15.7 us  [the longest x1 10.5 us: shards(): pl.pallas_call(tail_kernel, out_shape=jax.ShapeDtypeStruct(x.shape, bf16)...]
    ppermute x0 -> x14, waiting for transfers between devices: none -> 13.6 us  [the longest x1 5.28 us: shards(): across = lax.ppermute(below, AXES, X_UP)]
  transfers between devices with their start and end apart: 2 -> 16, of which waited for: 2 -> 4; matrix products, arithmetic and copies ran while one was open for 7% -> 0% of each run, Pallas kernels for 0% -> 3%
where the time goes in v1:
time: 104 us; the launch traced here: 103 us
  starting transfers between devices  69.4 us (67%)
  Pallas kernels  15.7 us (15%)
  waiting for transfers between devices  13.6 us (13%)
  local copies, waits for them, and re-layouts  3.01 us (3%)
  between operations  1.04 us (1%)
    all_to_all x1, starting transfers between devices, shards(): lax.all_to_all(formed, AXES, 0, 0, tiled=True, axis_index_groups=Z_GROUPS)  15.9 us
    ppermute x5, starting transfers between devices, shards(): other = [lax.ppermute(piece, AXES, CORE_SWAP) for piece in mine]  15.8 us
    pallas_call x1, Pallas kernels, shards(): pl.pallas_call(tail_kernel, out_shape=jax.ShapeDtypeStruct(x.shape, bf16)...  10.5 us
    ppermute x1, starting transfers between devices, shards(): other_keys = lax.ppermute(core_keys, AXES, CORE_SWAP)  7.89 us
    ppermute x1, waiting for transfers between devices, shards(): across = lax.ppermute(below, AXES, X_UP)  5.28 us
    ppermute x1, starting transfers between devices, shards(): far_keys = lax.ppermute(line_keys, AXES, Y_FAR)  4.82 us
    ppermute x1, waiting for transfers between devices, shards(): low = lax.ppermute(lines, AXES, RING_UP)  4.58 us
    ppermute x1, starting transfers between devices, shards(): high = lax.ppermute(lines, AXES, RING_DOWN)  4.57 us
  transfers between devices with their start and end apart: 16, of which 4 were waited for; matrix products, arithmetic and copies ran while one was open for 0% of the time, Pallas kernels for 3%

profile of v1, /device:TPU:1, one launch (start us, length us, event | category | flops | bytes accessed | tf_op | source)
XLA Modules:
  0.0 102.9 jit_solution(9219758727882438421)
XLA Ops:
  0.0 1.6 %form.1 = bf16[16,56,128]{2,1,0:T(8,128)(2,1)} custom-call(s32[512]{0:T(512)} %matching_ref.1, bf16[1,6480]{1,0:T(2,128)(2,1)} %tile_ref.1), custom_call_target="tpu_custom_call" | custom-call | tf_op jit(solution)/shard_map/form/pallas_call | solution.py:326
  1.6 15.9 %all-to-all-start = ((bf16[16,56,128]{2,1,0:T(8,128)(2,1)}), bf16[16,56,128]{2,1,0:T(8,128)(2,1)S(1)}, u32[]{:S(2)}, u32[]{:S(2)}) async-start(bf16[16,56,128]{2,1,0:T(8,128)(2,1)} %form.1), calls=%async_computation | async-start | bytes 458752 | tf_op jit(solution)/shard_map/all_to_all | solution.py:334
  17.5 3.1 %collective-permute-start.9 = (bf16[512,128]{1,0:T(8,128)(2,1)S(1)}, bf16[512,128]{1,0:T(8,128)(2,1)S(1)}, u32[]{:S(2)}, u32[]{:S(2)}) collective-permute-start(bf16[512,128]{1,0:T(8,128)(2,1)S(1)} %bitcast.9), channel_id=1, source_target_pairs={{0,2},{1,3},{2,4},{3,5},{4,6},{5,7},{6,0},{7,1},{16,18},{17,19},{1... | collective-permute-start | bytes 393224 | tf_op jit(solution)/shard_map/ppermute | solution.py:318
  20.6 3.4 %collective-permute-start.10 = (bf16[512,128]{1,0:T(8,128)(2,1)S(1)}, bf16[512,128]{1,0:T(8,128)(2,1)S(1)}, u32[]{:S(2)}, u32[]{:S(2)}) collective-permute-start(bf16[512,128]{1,0:T(8,128)(2,1)S(1)} %bitcast.10), channel_id=1, source_target_pairs={{0,6},{1,7},{2,0},{3,1},{4,2},{5,3},{6,4},{7,5},{16,22},{17,23},{1... | collective-permute-start | bytes 393224 | tf_op jit(solution)/shard_map/ppermute | solution.py:319
  24.7 1.9 %collective-permute-start.11 = (bf16[512,128]{1,0:T(8,128)(2,1)S(1)}, bf16[512,128]{1,0:T(8,128)(2,1)S(1)}, u32[]{:S(2)}, u32[]{:S(2)}) collective-permute-start(bf16[512,128]{1,0:T(8,128)(2,1)S(1)} %collective-permute-done.9), channel_id=1, source_target_pairs={{0,2},{1,3},{2,4},{3,5},{4,6},{5,7},{6,0},{7,1},{16,18},{17,19},{1... | collective-permute-start | bytes 393224 | tf_op jit(solution)/shard_map/ppermute | solution.py:320
  26.6 5.3 %collective-permute-done.11 = bf16[512,128]{1,0:T(8,128)(2,1)S(1)} collective-permute-done((bf16[512,128]{1,0:T(8,128)(2,1)S(1)}, bf16[512,128]{1,0:T(8,128)(2,1)S(1)}, u32[]{:S(2)}, u32[]{:S(2)}) %collective-permute-start.11) | collective-permute-done | bytes 131104 | tf_op jit(solution)/shard_map/ppermute | solution.py:320
  31.9 4.8 %collective-permute-start.12 = (bf16[2048,128]{1,0:T(8,128)(2,1)S(1)}, bf16[2048,128]{1,0:T(8,128)(2,1)S(1)}, u32[]{:S(2)}, u32[]{:S(2)}) collective-permute-start(bf16[2048,128]{1,0:T(8,128)(2,1)S(1)} %pad_maximum_fusion), channel_id=1, source_target_pairs={{0,8},{1,9},{2,10},{3,11},{4,12},{5,13},{6,14},{7,15},{16,24},{17,... | collective-permute-start | bytes 1572872 | tf_op jit(solution)/shard_map/ppermute | solution.py:322
  37.5 2.0 %merge.1 = bf16[4,55,16,128]{3,2,1,0:T(8,128)(2,1)} custom-call(bf16[16,56,128]{2,1,0:T(8,128)(2,1)} %copy-done.5), custom_call_target="tpu_custom_call" | custom-call | tf_op jit(solution)/shard_map/merge/pallas_call | solution.py:335
  39.5 3.5 %all-to-all-start.1 = ((bf16[4,55,16,128]{3,2,1,0:T(8,128)(2,1)}), bf16[4,55,16,128]{3,2,1,0:T(8,128)(2,1)S(1)}, u32[]{:S(2)}, u32[]{:S(2)}) async-start(bf16[4,55,16,128]{3,2,1,0:T(8,128)(2,1)} %merge.1), calls=%async_computation.1 | async-start | bytes 1802240 | tf_op jit(solution)/shard_map/all_to_all | solution.py:343
  43.1 3.0 %collective-permute-done.12 = bf16[2048,128]{1,0:T(8,128)(2,1)S(1)} collective-permute-done((bf16[2048,128]{1,0:T(8,128)(2,1)S(1)}, bf16[2048,128]{1,0:T(8,128)(2,1)S(1)}, u32[]{:S(2)}, u32[]{:S(2)}) %collective-permute-start.12) | collective-permute-done | bytes 524320 | tf_op jit(solution)/shard_map/ppermute | solution.py:322
  46.2 7.9 %collective-permute-start.13 = (bf16[4096,128]{1,0:T(8,128)(2,1)S(1)}, bf16[4096,128]{1,0:T(8,128)(2,1)S(1)}, u32[]{:S(2)}, u32[]{:S(2)}) collective-permute-start(bf16[4096,128]{1,0:T(8,128)(2,1)S(1)} %constant_dynamic-update-slice_fusion.near_ref), channel_id=1, source_target_pairs={{0,1},{1,0},{2,3},{3,2},{4,5},{5,4},{6,7},{7,6},{16,17},{17,16},{1... | collective-permute-start | bytes 3145736 | tf_op jit(solution)/shard_map/ppermute | solution.py:324
  54.1 1.9 %collective-permute-start = (bf16[4,55,16,128]{3,2,1,0:T(8,128)(2,1)S(1)}, bf16[4,55,16,128]{3,2,1,0:T(8,128)(2,1)S(1)}, u32[]{:S(2)}, u32[]{:S(2)}) collective-permute-start(bf16[4,55,16,128]{3,2,1,0:T(8,128)(2,1)S(1)} %all-to-all-done.1.m0), channel_id=1, source_target_pairs={{0,16},{1,3},{2,18},{3,5},{4,20},{5,7},{6,22},{7,1},{16,8},{17,19}... | collective-permute-start | bytes 2703368 | tf_op jit(solution)/shard_map/ppermute | solution.py:344
  56.0 4.6 %collective-permute-start.1 = (bf16[4,55,16,128]{3,2,1,0:T(8,128)(2,1)S(1)}, bf16[4,55,16,128]{3,2,1,0:T(8,128)(2,1)S(1)}, u32[]{:S(2)}, u32[]{:S(2)}) collective-permute-start(bf16[4,55,16,128]{3,2,1,0:T(8,128)(2,1)S(1)} %all-to-all-done.1.m0), channel_id=1, source_target_pairs={{0,24},{1,7},{2,26},{3,1},{4,28},{5,3},{6,30},{7,5},{16,0},{17,23}... | collective-permute-start | bytes 2703368 | tf_op jit(solution)/shard_map/ppermute | solution.py:345
  60.6 4.4 %collective-permute-start.4 = (bf16[4,55,16,128]{3,2,1,0:T(8,128)(2,1)S(1)}, bf16[4,55,16,128]{3,2,1,0:T(8,128)(2,1)S(1)}, u32[]{:S(2)}, u32[]{:S(2)}) collective-permute-start(bf16[4,55,16,128]{3,2,1,0:T(8,128)(2,1)S(1)} %all-to-all-done.1.m0), channel_id=1, source_target_pairs={{0,1},{1,0},{2,3},{3,2},{4,5},{5,4},{6,7},{7,6},{16,17},{17,16},{1... | collective-permute-start | bytes 2703368 | tf_op jit(solution)/shard_map/ppermute | solution.py:349
  65.0 4.6 %collective-permute-done.m1 = bf16[4,55,16,128]{3,2,1,0:T(8,128)(2,1)S(1)} collective-permute-done((bf16[4,55,16,128]{3,2,1,0:T(8,128)(2,1)S(1)}, bf16[4,55,16,128]{3,2,1,0:T(8,128)(2,1)S(1)}, u32[]{:S(2)}, u32[]{:S(2)}) %collective-permute-start) | collective-permute-done | bytes 901152 | tf_op jit(solution)/shard_map/ppermute | solution.py:344
  69.6 2.1 %collective-permute-start.2 = (bf16[2,55,16,128]{3,2,1,0:T(8,128)(2,1)S(1)}, bf16[2,55,16,128]{3,2,1,0:T(8,128)(2,1)S(1)}, u32[]{:S(2)}, u32[]{:S(2)}) collective-permute-start(bf16[2,55,16,128]{3,2,1,0:T(8,128)(2,1)S(1)} %slice.8), channel_id=1, source_target_pairs={{0,16},{1,3},{2,18},{3,5},{4,20},{5,7},{6,22},{7,1},{16,8},{17,19}... | collective-permute-start | bytes 1351688 | tf_op jit(solution)/shard_map/ppermute | solution.py:346
  71.7 4.6 %collective-permute-start.3 = (bf16[2,55,16,128]{3,2,1,0:T(8,128)(2,1)S(1)}, bf16[2,55,16,128]{3,2,1,0:T(8,128)(2,1)S(1)}, u32[]{:S(2)}, u32[]{:S(2)}) collective-permute-start(bf16[2,55,16,128]{3,2,1,0:T(8,128)(2,1)S(1)} %slice.9), channel_id=1, source_target_pairs={{0,24},{1,7},{2,26},{3,1},{4,28},{5,3},{6,30},{7,5},{16,0},{17,23}... | collective-permute-start | bytes 1351688 | tf_op jit(solution)/shard_map/ppermute | solution.py:347
  76.3 5.2 %collective-permute-start.5 = (bf16[4,55,16,128]{3,2,1,0:T(8,128)(2,1)S(1)}, bf16[4,55,16,128]{3,2,1,0:T(8,128)(2,1)S(1)}, u32[]{:S(2)}, u32[]{:S(2)}) collective-permute-start(bf16[4,55,16,128]{3,2,1,0:T(8,128)(2,1)S(1)} %collective-permute-done.m1), channel_id=1, source_target_pairs={{0,1},{1,0},{2,3},{3,2},{4,5},{5,4},{6,7},{7,6},{16,17},{17,16},{1... | collective-permute-start | bytes 2703368 | tf_op jit(solution)/shard_map/ppermute | solution.py:349
  81.6 1.9 %collective-permute-start.6 = (bf16[4,55,16,128]{3,2,1,0:T(8,128)(2,1)S(1)}, bf16[4,55,16,128]{3,2,1,0:T(8,128)(2,1)S(1)}, u32[]{:S(2)}, u32[]{:S(2)}) collective-permute-start(bf16[4,55,16,128]{3,2,1,0:T(8,128)(2,1)S(1)} %collective-permute-done.1.m2), channel_id=1, source_target_pairs={{0,1},{1,0},{2,3},{3,2},{4,5},{5,4},{6,7},{7,6},{16,17},{17,16},{1... | collective-permute-start | bytes 2703368 | tf_op jit(solution)/shard_map/ppermute | solution.py:349
  83.5 2.4 %collective-permute-start.7 = (bf16[2,55,16,128]{3,2,1,0:T(8,128)(2,1)S(1)}, bf16[2,55,16,128]{3,2,1,0:T(8,128)(2,1)S(1)}, u32[]{:S(2)}, u32[]{:S(2)}) collective-permute-start(bf16[2,55,16,128]{3,2,1,0:T(8,128)(2,1)S(1)} %collective-permute-done.2.m3), channel_id=1, source_target_pairs={{0,1},{1,0},{2,3},{3,2},{4,5},{5,4},{6,7},{7,6},{16,17},{17,16},{1... | collective-permute-start | bytes 1351688 | tf_op jit(solution)/shard_map/ppermute | solution.py:349
  85.9 1.9 %collective-permute-start.8 = (bf16[2,55,16,128]{3,2,1,0:T(8,128)(2,1)S(1)}, bf16[2,55,16,128]{3,2,1,0:T(8,128)(2,1)S(1)}, u32[]{:S(2)}, u32[]{:S(2)}) collective-permute-start(bf16[2,55,16,128]{3,2,1,0:T(8,128)(2,1)S(1)} %collective-permute-done.3.m4), channel_id=1, source_target_pairs={{0,1},{1,0},{2,3},{3,2},{4,5},{5,4},{6,7},{7,6},{16,17},{17,16},{1... | collective-permute-start | bytes 1351688 | tf_op jit(solution)/shard_map/ppermute | solution.py:349
  89.2 1.6 %pick.1 = (bf16[352,512]{1,0:T(8,128)(2,1)S(1)}, s32[1,512]{1,0:T(1,128)S(1)}) custom-call(bf16[4,8,2880]{2,1,0:T(8,128)(2,1)S(1)} %bitcast.7, s32[1,512]{1,0:T(1,128)S(1)} %bitcast.8), custom_call_target="tpu_custom_call" | custom-call | tf_op jit(solution)/shard_map/pick/pallas_call | solution.py:350
  90.9 0.8 copy-done.6
  92.3 10.5 %tail.1 = bf16[4,8,2880]{2,1,0:T(8,128)(2,1)} custom-call(s32[1]{0:T(128)S(6)} %copy.11.limit_ref, bf16[352,512]{1,0:T(8,128)(2,1)S(1)} %get-tuple-element.7.xg_ref, s32[1,512]{1,0:T(1,128)S(1)} %get-tuple-element.8.place_ref, bf16[4,55,16,128]{3,2,1,0:T(8,128)(2,1)S(1)} %all-to-all-done.1.m0, bf16[4,55,16,128]{3,2,1,0:T(8,128)(2,1)S(1)} %collective-permute-done.m1, ...), custom_call_target="tpu_custom_call" | custom-call | tf_op jit(solution)/shard_map/tail/pallas_call | solution.py:362
  (40 shorter events, 3.0 us)
Async XLA Ops:
  1.6 15.9 %copy-start.9 = (bf16[1,512,128]{2,1,0:T(8,128)(2,1)S(1)}, bf16[1,512,128]{2,1,0:T(8,128)(2,1)}, u32[]{:S(2)}) copy-start(bf16[1,512,128]{2,1,0:T(8,128)(2,1)} %param.7) | copy-start | bytes 393220
  1.6 35.2 %all-to-all-start = ((bf16[16,56,128]{2,1,0:T(8,128)(2,1)}), bf16[16,56,128]{2,1,0:T(8,128)(2,1)S(1)}, u32[]{:S(2)}, u32[]{:S(2)}) async-start(bf16[16,56,128]{2,1,0:T(8,128)(2,1)} %form.1), calls=%async_computation | async-start | bytes 458752 | tf_op jit(solution)/shard_map/all_to_all | solution.py:334
  17.5 7.2 %collective-permute-start.9 = (bf16[512,128]{1,0:T(8,128)(2,1)S(1)}, bf16[512,128]{1,0:T(8,128)(2,1)S(1)}, u32[]{:S(2)}, u32[]{:S(2)}) collective-permute-start(bf16[512,128]{1,0:T(8,128)(2,1)S(1)} %bitcast.9), channel_id=1, source_target_pairs={{0,2},{1,3},{2,4},{3,5},{4,6},{5,7},{6,0},{7,1},{16,18},{17,19},{1... | collective-permute-start | bytes 393224 | tf_op jit(solution)/shard_map/ppermute | solution.py:318
  20.6 6.0 %collective-permute-start.10 = (bf16[512,128]{1,0:T(8,128)(2,1)S(1)}, bf16[512,128]{1,0:T(8,128)(2,1)S(1)}, u32[]{:S(2)}, u32[]{:S(2)}) collective-permute-start(bf16[512,128]{1,0:T(8,128)(2,1)S(1)} %bitcast.10), channel_id=1, source_target_pairs={{0,6},{1,7},{2,0},{3,1},{4,2},{5,3},{6,4},{7,5},{16,22},{17,23},{1... | collective-permute-start | bytes 393224 | tf_op jit(solution)/shard_map/ppermute | solution.py:319
  24.7 7.2 %collective-permute-start.11 = (bf16[512,128]{1,0:T(8,128)(2,1)S(1)}, bf16[512,128]{1,0:T(8,128)(2,1)S(1)}, u32[]{:S(2)}, u32[]{:S(2)}) collective-permute-start(bf16[512,128]{1,0:T(8,128)(2,1)S(1)} %collective-permute-done.9), channel_id=1, source_target_pairs={{0,2},{1,3},{2,4},{3,5},{4,6},{5,7},{6,0},{7,1},{16,18},{17,19},{1... | collective-permute-start | bytes 393224 | tf_op jit(solution)/shard_map/ppermute | solution.py:320
  31.9 14.1 %collective-permute-start.12 = (bf16[2048,128]{1,0:T(8,128)(2,1)S(1)}, bf16[2048,128]{1,0:T(8,128)(2,1)S(1)}, u32[]{:S(2)}, u32[]{:S(2)}) collective-permute-start(bf16[2048,128]{1,0:T(8,128)(2,1)S(1)} %pad_maximum_fusion), channel_id=1, source_target_pairs={{0,8},{1,9},{2,10},{3,11},{4,12},{5,13},{6,14},{7,15},{16,24},{17,... | collective-permute-start | bytes 1572872 | tf_op jit(solution)/shard_map/ppermute | solution.py:322
  39.5 14.6 %all-to-all-start.1 = ((bf16[4,55,16,128]{3,2,1,0:T(8,128)(2,1)}), bf16[4,55,16,128]{3,2,1,0:T(8,128)(2,1)S(1)}, u32[]{:S(2)}, u32[]{:S(2)}) async-start(bf16[4,55,16,128]{3,2,1,0:T(8,128)(2,1)} %merge.1), calls=%async_computation.1 | async-start | bytes 1802240 | tf_op jit(solution)/shard_map/all_to_all | solution.py:343
  46.2 44.7 %copy-start.3 = (bf16[4096,128]{1,0:T(8,128)(2,1)}, bf16[4096,128]{1,0:T(8,128)(2,1)S(1)}, u32[]{:S(2)}) copy-start(bf16[4096,128]{1,0:T(8,128)(2,1)S(1)} %constant_dynamic-update-slice_fusion.near_ref) | copy-start | bytes 3145732
  46.2 35.4 %collective-permute-start.13 = (bf16[4096,128]{1,0:T(8,128)(2,1)S(1)}, bf16[4096,128]{1,0:T(8,128)(2,1)S(1)}, u32[]{:S(2)}, u32[]{:S(2)}) collective-permute-start(bf16[4096,128]{1,0:T(8,128)(2,1)S(1)} %constant_dynamic-update-slice_fusion.near_ref), channel_id=1, source_target_pairs={{0,1},{1,0},{2,3},{3,2},{4,5},{5,4},{6,7},{7,6},{16,17},{17,16},{1... | collective-permute-start | bytes 3145736 | tf_op jit(solution)/shard_map/ppermute | solution.py:324
  54.1 15.5 %collective-permute-start = (bf16[4,55,16,128]{3,2,1,0:T(8,128)(2,1)S(1)}, bf16[4,55,16,128]{3,2,1,0:T(8,128)(2,1)S(1)}, u32[]{:S(2)}, u32[]{:S(2)}) collective-permute-start(bf16[4,55,16,128]{3,2,1,0:T(8,128)(2,1)S(1)} %all-to-all-done.1.m0), channel_id=1, source_target_pairs={{0,16},{1,3},{2,18},{3,5},{4,20},{5,7},{6,22},{7,1},{16,8},{17,19}... | collective-permute-start | bytes 2703368 | tf_op jit(solution)/shard_map/ppermute | solution.py:344
  56.0 15.6 %collective-permute-start.1 = (bf16[4,55,16,128]{3,2,1,0:T(8,128)(2,1)S(1)}, bf16[4,55,16,128]{3,2,1,0:T(8,128)(2,1)S(1)}, u32[]{:S(2)}, u32[]{:S(2)}) collective-permute-start(bf16[4,55,16,128]{3,2,1,0:T(8,128)(2,1)S(1)} %all-to-all-done.1.m0), channel_id=1, source_target_pairs={{0,24},{1,7},{2,26},{3,1},{4,28},{5,3},{6,30},{7,5},{16,0},{17,23}... | collective-permute-start | bytes 2703368 | tf_op jit(solution)/shard_map/ppermute | solution.py:345
  60.6 30.2 %collective-permute-start.4 = (bf16[4,55,16,128]{3,2,1,0:T(8,128)(2,1)S(1)}, bf16[4,55,16,128]{3,2,1,0:T(8,128)(2,1)S(1)}, u32[]{:S(2)}, u32[]{:S(2)}) collective-permute-start(bf16[4,55,16,128]{3,2,1,0:T(8,128)(2,1)S(1)} %all-to-all-done.1.m0), channel_id=1, source_target_pairs={{0,1},{1,0},{2,3},{3,2},{4,5},{5,4},{6,7},{7,6},{16,17},{17,16},{1... | collective-permute-start | bytes 2703368 | tf_op jit(solution)/shard_map/ppermute | solution.py:349
  69.6 18.9 %copy-start = (bf16[4,1,8,2880]{3,2,1,0:T(8,128)(2,1)S(1)}, bf16[4,1,8,2880]{3,2,1,0:T(8,128)(2,1)}, u32[]{:S(2)}) copy-start(bf16[4,1,8,2880]{3,2,1,0:T(8,128)(2,1)} %param.9) | copy-start | bytes 552964
  69.6 13.9 %collective-permute-start.2 = (bf16[2,55,16,128]{3,2,1,0:T(8,128)(2,1)S(1)}, bf16[2,55,16,128]{3,2,1,0:T(8,128)(2,1)S(1)}, u32[]{:S(2)}, u32[]{:S(2)}) collective-permute-start(bf16[2,55,16,128]{3,2,1,0:T(8,128)(2,1)S(1)} %slice.8), channel_id=1, source_target_pairs={{0,16},{1,3},{2,18},{3,5},{4,20},{5,7},{6,22},{7,1},{16,8},{17,19}... | collective-permute-start | bytes 1351688 | tf_op jit(solution)/shard_map/ppermute | solution.py:346
  71.7 19.2 %copy-start.2 = (bf16[4,55,16,128]{3,2,1,0:T(8,128)(2,1)}, bf16[4,55,16,128]{3,2,1,0:T(8,128)(2,1)S(1)}, u32[]{:S(2)}) copy-start(bf16[4,55,16,128]{3,2,1,0:T(8,128)(2,1)S(1)} %collective-permute-done.1.m2) | copy-start | bytes 2703364
  71.7 14.2 %collective-permute-start.3 = (bf16[2,55,16,128]{3,2,1,0:T(8,128)(2,1)S(1)}, bf16[2,55,16,128]{3,2,1,0:T(8,128)(2,1)S(1)}, u32[]{:S(2)}, u32[]{:S(2)}) collective-permute-start(bf16[2,55,16,128]{3,2,1,0:T(8,128)(2,1)S(1)} %slice.9), channel_id=1, source_target_pairs={{0,24},{1,7},{2,26},{3,1},{4,28},{5,3},{6,30},{7,5},{16,0},{17,23}... | collective-permute-start | bytes 1351688 | tf_op jit(solution)/shard_map/ppermute | solution.py:347
  76.3 14.5 %collective-permute-start.5 = (bf16[4,55,16,128]{3,2,1,0:T(8,128)(2,1)S(1)}, bf16[4,55,16,128]{3,2,1,0:T(8,128)(2,1)S(1)}, u32[]{:S(2)}, u32[]{:S(2)}) collective-permute-start(bf16[4,55,16,128]{3,2,1,0:T(8,128)(2,1)S(1)} %collective-permute-done.m1), channel_id=1, source_target_pairs={{0,1},{1,0},{2,3},{3,2},{4,5},{5,4},{6,7},{7,6},{16,17},{17,16},{1... | collective-permute-start | bytes 2703368 | tf_op jit(solution)/shard_map/ppermute | solution.py:349
  81.6 9.3 %copy-start.4 = (bf16[4096,128]{1,0:T(8,128)(2,1)}, bf16[4096,128]{1,0:T(8,128)(2,1)S(1)}, u32[]{:S(2)}) copy-start(bf16[4096,128]{1,0:T(8,128)(2,1)S(1)} %collective-permute-done.13.far_ref) | copy-start | bytes 3145732
  81.6 9.3 %collective-permute-start.6 = (bf16[4,55,16,128]{3,2,1,0:T(8,128)(2,1)S(1)}, bf16[4,55,16,128]{3,2,1,0:T(8,128)(2,1)S(1)}, u32[]{:S(2)}, u32[]{:S(2)}) collective-permute-start(bf16[4,55,16,128]{3,2,1,0:T(8,128)(2,1)S(1)} %collective-permute-done.1.m2), channel_id=1, source_target_pairs={{0,1},{1,0},{2,3},{3,2},{4,5},{5,4},{6,7},{7,6},{16,17},{17,16},{1... | collective-permute-start | bytes 2703368 | tf_op jit(solution)/shard_map/ppermute | solution.py:349
  83.5 7.3 %collective-permute-start.7 = (bf16[2,55,16,128]{3,2,1,0:T(8,128)(2,1)S(1)}, bf16[2,55,16,128]{3,2,1,0:T(8,128)(2,1)S(1)}, u32[]{:S(2)}, u32[]{:S(2)}) collective-permute-start(bf16[2,55,16,128]{3,2,1,0:T(8,128)(2,1)S(1)} %collective-permute-done.2.m3), channel_id=1, source_target_pairs={{0,1},{1,0},{2,3},{3,2},{4,5},{5,4},{6,7},{7,6},{16,17},{17,16},{1... | collective-permute-start | bytes 1351688 | tf_op jit(solution)/shard_map/ppermute | solution.py:349
  85.9 4.9 %collective-permute-start.8 = (bf16[2,55,16,128]{3,2,1,0:T(8,128)(2,1)S(1)}, bf16[2,55,16,128]{3,2,1,0:T(8,128)(2,1)S(1)}, u32[]{:S(2)}, u32[]{:S(2)}) collective-permute-start(bf16[2,55,16,128]{3,2,1,0:T(8,128)(2,1)S(1)} %collective-permute-done.3.m4), channel_id=1, source_target_pairs={{0,1},{1,0},{2,3},{3,2},{4,5},{5,4},{6,7},{7,6},{16,17},{17,16},{1... | collective-permute-start | bytes 1351688 | tf_op jit(solution)/shard_map/ppermute | solution.py:349
  90.8 0.9 copy-start.6
  90.8 1.2 %copy-start.7 = (bf16[4,55,16,128]{3,2,1,0:T(8,128)(2,1)}, bf16[4,55,16,128]{3,2,1,0:T(8,128)(2,1)S(1)}, u32[]{:S(2)}) copy-start(bf16[4,55,16,128]{3,2,1,0:T(8,128)(2,1)S(1)} %collective-permute-done.5.o1) | copy-start | bytes 2703364
  90.9 1.5 %copy-start.8 = (bf16[4,55,16,128]{3,2,1,0:T(8,128)(2,1)}, bf16[4,55,16,128]{3,2,1,0:T(8,128)(2,1)S(1)}, u32[]{:S(2)}) copy-start(bf16[4,55,16,128]{3,2,1,0:T(8,128)(2,1)S(1)} %collective-permute-done.6.o2) | copy-start | bytes 2703364
  (2 other events, 1.4 us)

commit v2 on v1

--- a/solution.py
+++ b/solution.py
@@ -52,8 +52,8 @@
 
 
 CORE_SWAP = moves(lambda y, x, c: (y, x, 1 - c))
-X_UP = moves(lambda y, x, c: (y, x + 1, c))
-X_DOWN = moves(lambda y, x, c: (y, x - 1, c))
+X_OUT = moves(lambda y, x, c: (y, x - 1 if c else x + 1, c))
+X_BACK = moves(lambda y, x, c: (y, x + 1 if c else x - 1, c))
 Y_FAR = moves(lambda y, x, c: (y + 2, x, c))
 RING_UP = moves(lambda y, x, c: (y, x + 1, c) if c else (y + 1, x, c))
 RING_DOWN = moves(lambda y, x, c: (y, x - 1, c) if c else (y - 1, x, c))
@@ -187,10 +187,10 @@
 
 
 def tail_kernel(
-    limit_ref, xg_ref, place_ref, m0, m1, m2, m3, m4, o0, o1, o2, o3, o4, near_ref, far_ref, out_ref,
+    limit_ref, xg_ref, place_ref, m0, m1, m2, m3, o0, o1, o2, o3, near_ref, far_ref, out_ref,
     s_ref, w_ref, og_ref, acc_ref,
 ):
-    halves = ((m0, m1, m2, m3, m4), (o0, o1, o2, o3, o4))
+    halves = ((m0, m1, m2, m3), (o0, o1, o2, o3))
     projected = project(xg_ref, halves)
     y0, x0, core0 = chip_place()
     rounded = projected.astype(jnp.bfloat16)
@@ -224,8 +224,9 @@
         )
         bias = []
         for n in range(CHUNK // SHARD * k, CHUNK // SHARD * (k + 1)):
-            x = (x0 + (0, 3, 1, 2)[n & 3]) & 3
-            shard = ((y0 >> 1) ^ ((n >> 2) & 1)) * 8 + x * 2 + (core0 ^ (n >> 3))
+            core = core0 ^ (n >> 3)
+            offset = (0, 3 - 2 * core, 1 + 2 * core, 2)[(n >> 1) & 3]
+            shard = ((y0 >> 1) ^ (n & 1)) * 8 + ((x0 + offset) & 3) * 2 + core
             keys = lax.broadcasted_iota(jnp.int32, (1, SHARD), 1)
             bias.append(jnp.where(keys < limit - SHARD * shard, 0.0, -1e30))
         scores = scores + jnp.concatenate(bias, 1)
@@ -315,13 +316,11 @@
     x = inputs[:, 0]
     x = inputs[:, 0]
     prefix = prefix_kv[0]
-    below = lax.ppermute(prefix, AXES, X_UP)
-    above = lax.ppermute(prefix, AXES, X_DOWN)
-    across = lax.ppermute(below, AXES, X_UP)
-    line_keys = lax.concatenate([prefix, below, above, across], 0)
-    far_keys = lax.ppermute(line_keys, AXES, Y_FAR)
-    core_keys = lax.concatenate([line_keys, far_keys], 0)
-    other_keys = lax.ppermute(core_keys, AXES, CORE_SWAP)
+    pair = lax.concatenate([prefix, lax.ppermute(prefix, AXES, Y_FAR)], 0)
+    behind = lax.ppermute(pair, AXES, X_OUT)
+    ahead = lax.ppermute(pair, AXES, X_BACK)
+    across = lax.ppermute(behind, AXES, X_OUT)
+    core_keys = lax.concatenate([pair, behind, ahead, across], 0)
 
     formed = pl.pallas_call(
         form_kernel,
@@ -338,15 +337,15 @@
         in_specs=[VMEM],
         out_specs=VMEM,
         scratch_shapes=[pltpu.VMEM((16 * SLOT, 128), f32)],
+        compiler_params=pltpu.CompilerParams(vmem_limit_bytes=8 * MIB),
         name="merge",
     )(along_z)
     lines = lax.all_to_all(merged, AXES, 0, 0, tiled=True, axis_index_groups=line_groups(0))
+    lines, core_keys = lax.optimization_barrier((lines, core_keys))
     low = lax.ppermute(lines, AXES, RING_UP)
     high = lax.ppermute(lines, AXES, RING_DOWN)
-    end0 = lax.ppermute(low[:2], AXES, RING_UP)
-    end1 = lax.ppermute(high[2:], AXES, RING_DOWN)
-    mine = [lines, low, high, end0, end1]
-    other = [lax.ppermute(piece, AXES, CORE_SWAP) for piece in mine]
+    other_lines = lax.ppermute(lines, AXES, CORE_SWAP)
+    other_keys = lax.ppermute(core_keys, AXES, CORE_SWAP)
     gathered, places = pl.pallas_call(
         pick_kernel,
         out_shape=(
@@ -356,13 +355,23 @@
         in_specs=[VMEM] * 2,
         out_specs=(VMEM, VMEM),
         scratch_shapes=[pltpu.VMEM((ROWS, 3072), f32), pltpu.VMEM((11 * ROWS, 3072), bf16)],
-        compiler_params=pltpu.CompilerParams(vmem_limit_bytes=40 * MIB),
+        compiler_params=pltpu.CompilerParams(vmem_limit_bytes=12 * MIB),
         name="pick",
     )(x, matching.reshape(1, 512))
+    low, gathered = lax.optimization_barrier((low, gathered))
+    end0 = lax.ppermute(low[:2], AXES, RING_UP)
+    end1 = lax.ppermute(high[2:], AXES, RING_DOWN)
+    side, other_keys, other_lines = lax.optimization_barrier((low, other_keys, other_lines))
+    other_low = lax.ppermute(side, AXES, CORE_SWAP)
+    other_high = lax.ppermute(high, AXES, CORE_SWAP)
+    ends = lax.concatenate([end0, end1], 0)
+    other_ends = lax.ppermute(ends, AXES, CORE_SWAP)
+    mine = [lines, low, high, ends]
+    other = [other_lines, other_low, other_high, other_ends]
     output = pl.pallas_call(
         tail_kernel,
         out_shape=jax.ShapeDtypeStruct(x.shape, bf16),
-        in_specs=[SMEM] + [VMEM] * 14,
+        in_specs=[SMEM] + [VMEM] * 12,
         out_specs=VMEM,
         scratch_shapes=[
             pltpu.VMEM((QHEADS * ROWS, 16 * SHARD), f32),
@@ -370,7 +379,7 @@
             pltpu.VMEM((ROWS, 768), f32),
             pltpu.VMEM((ROWS, 3072), f32),
         ],
-        compiler_params=pltpu.CompilerParams(vmem_limit_bytes=50 * MIB),
+        compiler_params=pltpu.CompilerParams(vmem_limit_bytes=20 * MIB),
         name="tail",
     )(prefix_blocks, gathered, places, *mine, *other, core_keys, other_keys)
     return output[:, None]

time: 104 us -> 96.1 us (0.924)
  Pallas kernels: 15.7 us -> 12.1 us
  local copies, waits for them, and re-layouts: 3.01 us -> 0.31 us
  waiting for transfers between devices: 13.6 us -> 12 us
    ppermute x1, waiting for transfers between devices: 4.58 us -> 0.01 us  [shards(): low = lax.ppermute(lines, AXES, RING_UP)]
    ppermute x9 -> x8, waiting for transfers between devices: 9.01 us -> 12 us  [the longest x1 7.93 us: shards(): across = lax.ppermute(behind, AXES, X_OUT)]
    unnamed x24 -> x11, local copies, waits for them, and re-layouts: 2.88 us -> 0.15 us
    pallas_call x1, Pallas kernels: 10.5 us -> 7.92 us  [shards(): pl.pallas_call(tail_kernel, out_shape=jax.ShapeDtypeStruct(x.shape, bf16)...]
    ppermute x1, starting transfers between devices: 7.89 us -> 6.29 us  [shards(): other_keys = lax.ppermute(core_keys, AXES, CORE_SWAP)]
    ppermute x9 -> x8, starting transfers between devices: 29.1 us -> 29.7 us  [the longest x1 6.24 us: shards(): other_high = lax.ppermute(high, AXES, CORE_SWAP)]
  transfers between devices with their start and end apart: 16 -> 15, of which waited for: 4 -> 3; matrix products, arithmetic and copies ran while one was open for 0% -> 0% of each run, Pallas kernels for 3% -> 3%
where the time goes in v2:
time: 96.1 us; the launch traced here: 95.1 us
  starting transfers between devices  69.7 us (73%)
  Pallas kernels  12.1 us (13%)
  waiting for transfers between devices  12 us (12%)
  between operations  0.97 us (1%)
    all_to_all x1, starting transfers between devices, shards(): lax.all_to_all(formed, AXES, 0, 0, tiled=True, axis_index_groups=Z_GROUPS)  15.9 us
    ppermute x1, waiting for transfers between devices, shards(): across = lax.ppermute(behind, AXES, X_OUT)  7.93 us
    pallas_call x1, Pallas kernels, shards(): pl.pallas_call(tail_kernel, out_shape=jax.ShapeDtypeStruct(x.shape, bf16)...  7.92 us
    ppermute x1, starting transfers between devices, shards(): other_keys = lax.ppermute(core_keys, AXES, CORE_SWAP)  6.29 us
    ppermute x1, starting transfers between devices, shards(): other_high = lax.ppermute(high, AXES, CORE_SWAP)  6.24 us
    ppermute x1, starting transfers between devices, shards(): high = lax.ppermute(lines, AXES, RING_DOWN)  5.27 us
    ppermute x1, starting transfers between devices, shards(): pair = lax.concatenate([prefix, lax.ppermute(prefix, AXES, Y_FAR)], 0)  4.82 us
    ppermute x1, starting transfers between devices, shards(): across = lax.ppermute(behind, AXES, X_OUT)  4.57 us
  transfers between devices with their start and end apart: 15, of which 3 were waited for; matrix products, arithmetic and copies ran while one was open for 0% of the time, Pallas kernels for 3%

profile of v2, /device:TPU:1, one launch (start us, length us, event | category | flops | bytes accessed | tf_op | source)
XLA Modules:
  0.0 95.1 jit_solution(17720300631442607176)
XLA Ops:
  0.0 1.6 %form.1 = bf16[16,56,128]{2,1,0:T(8,128)(2,1)} custom-call(s32[512]{0:T(512)} %matching_ref.1, bf16[1,6480]{1,0:T(2,128)(2,1)} %tile_ref.1), custom_call_target="tpu_custom_call" | custom-call | tf_op jit(solution)/shard_map/form/pallas_call | solution.py:325
  1.6 15.9 %all-to-all-start = ((bf16[16,56,128]{2,1,0:T(8,128)(2,1)}), bf16[16,56,128]{2,1,0:T(8,128)(2,1)S(1)}, u32[]{:S(2)}, u32[]{:S(2)}) async-start(bf16[16,56,128]{2,1,0:T(8,128)(2,1)} %form.1), calls=%async_computation | async-start | bytes 458752 | tf_op jit(solution)/shard_map/all_to_all | solution.py:333
  17.5 4.8 %collective-permute-start = (bf16[512,128]{1,0:T(8,128)(2,1)S(1)}, bf16[512,128]{1,0:T(8,128)(2,1)S(1)}, u32[]{:S(2)}, u32[]{:S(2)}) collective-permute-start(bf16[512,128]{1,0:T(8,128)(2,1)S(1)} %bitcast.9), channel_id=1, source_target_pairs={{0,8},{1,9},{2,10},{3,11},{4,12},{5,13},{6,14},{7,15},{16,24},{17,... | collective-permute-start | bytes 393224 | tf_op jit(solution)/shard_map/ppermute | solution.py:319
  22.3 2.7 %collective-permute-done = bf16[512,128]{1,0:T(8,128)(2,1)S(1)} collective-permute-done((bf16[512,128]{1,0:T(8,128)(2,1)S(1)}, bf16[512,128]{1,0:T(8,128)(2,1)S(1)}, u32[]{:S(2)}, u32[]{:S(2)}) %collective-permute-start) | collective-permute-done | bytes 131104 | tf_op jit(solution)/shard_map/ppermute | solution.py:319
  25.0 4.4 %collective-permute-start.1 = (bf16[1024,128]{1,0:T(8,128)(2,1)S(1)}, bf16[1024,128]{1,0:T(8,128)(2,1)S(1)}, u32[]{:S(2)}, u32[]{:S(2)}) collective-permute-start(bf16[1024,128]{1,0:T(8,128)(2,1)S(1)} %pad_maximum_fusion), channel_id=1, source_target_pairs={{0,2},{1,7},{2,4},{3,1},{4,6},{5,3},{6,0},{7,5},{16,18},{17,23},{1... | collective-permute-start | bytes 786440 | tf_op jit(solution)/shard_map/ppermute | solution.py:320
  29.4 1.9 %collective-permute-start.2 = (bf16[1024,128]{1,0:T(8,128)(2,1)S(1)}, bf16[1024,128]{1,0:T(8,128)(2,1)S(1)}, u32[]{:S(2)}, u32[]{:S(2)}) collective-permute-start(bf16[1024,128]{1,0:T(8,128)(2,1)S(1)} %pad_maximum_fusion), channel_id=1, source_target_pairs={{0,6},{1,3},{2,0},{3,5},{4,2},{5,7},{6,4},{7,1},{16,22},{17,19},{1... | collective-permute-start | bytes 786440 | tf_op jit(solution)/shard_map/ppermute | solution.py:321
  31.3 1.0 %merge.1 = bf16[4,55,16,128]{3,2,1,0:T(8,128)(2,1)} custom-call(bf16[16,56,128]{2,1,0:T(8,128)(2,1)S(1)} %all-to-all-done.in_ref), custom_call_target="tpu_custom_call" | custom-call | tf_op jit(solution)/shard_map/merge/pallas_call | solution.py:334
  32.4 4.2 %all-to-all-start.1 = ((bf16[4,55,16,128]{3,2,1,0:T(8,128)(2,1)}), bf16[4,55,16,128]{3,2,1,0:T(8,128)(2,1)S(1)}, u32[]{:S(2)}, u32[]{:S(2)}) async-start(bf16[4,55,16,128]{3,2,1,0:T(8,128)(2,1)} %merge.1), calls=%async_computation.1 | async-start | bytes 1802240 | tf_op jit(solution)/shard_map/all_to_all | solution.py:343
  36.6 4.6 %collective-permute-start.3 = (bf16[1024,128]{1,0:T(8,128)(2,1)S(1)}, bf16[1024,128]{1,0:T(8,128)(2,1)S(1)}, u32[]{:S(2)}, u32[]{:S(2)}) collective-permute-start(bf16[1024,128]{1,0:T(8,128)(2,1)S(1)} %collective-permute-done.1), channel_id=1, source_target_pairs={{0,2},{1,7},{2,4},{3,1},{4,6},{5,3},{6,0},{7,5},{16,18},{17,23},{1... | collective-permute-start | bytes 786440 | tf_op jit(solution)/shard_map/ppermute | solution.py:322
  41.3 0.0 copy-start
  41.3 7.9 %collective-permute-done.3 = bf16[1024,128]{1,0:T(8,128)(2,1)S(1)} collective-permute-done((bf16[1024,128]{1,0:T(8,128)(2,1)S(1)}, bf16[1024,128]{1,0:T(8,128)(2,1)S(1)}, u32[]{:S(2)}, u32[]{:S(2)}) %collective-permute-start.3) | collective-permute-done | bytes 262176 | tf_op jit(solution)/shard_map/ppermute | solution.py:322
  49.3 1.9 %collective-permute-start.4 = (bf16[4,55,16,128]{3,2,1,0:T(8,128)(2,1)S(1)}, bf16[4,55,16,128]{3,2,1,0:T(8,128)(2,1)S(1)}, u32[]{:S(2)}, u32[]{:S(2)}) collective-permute-start(bf16[4,55,16,128]{3,2,1,0:T(8,128)(2,1)S(1)} %all-to-all-done.1.m0), channel_id=1, source_target_pairs={{0,16},{1,3},{2,18},{3,5},{4,20},{5,7},{6,22},{7,1},{16,8},{17,19}... | collective-permute-start | bytes 2703368 | tf_op jit(solution)/shard_map/ppermute | solution.py:345
  51.2 5.3 %collective-permute-start.5 = (bf16[4,55,16,128]{3,2,1,0:T(8,128)(2,1)S(1)}, bf16[4,55,16,128]{3,2,1,0:T(8,128)(2,1)S(1)}, u32[]{:S(2)}, u32[]{:S(2)}) collective-permute-start(bf16[4,55,16,128]{3,2,1,0:T(8,128)(2,1)S(1)} %all-to-all-done.1.m0), channel_id=1, source_target_pairs={{0,24},{1,7},{2,26},{3,1},{4,28},{5,3},{6,30},{7,5},{16,0},{17,23}... | collective-permute-start | bytes 2703368 | tf_op jit(solution)/shard_map/ppermute | solution.py:346
  56.5 6.3 %collective-permute-start.8 = (bf16[4096,128]{1,0:T(8,128)(2,1)S(1)}, bf16[4096,128]{1,0:T(8,128)(2,1)S(1)}, u32[]{:S(2)}, u32[]{:S(2)}) collective-permute-start(bf16[4096,128]{1,0:T(8,128)(2,1)S(1)} %constant_dynamic-update-slice_fusion.near_ref), channel_id=1, source_target_pairs={{0,1},{1,0},{2,3},{3,2},{4,5},{5,4},{6,7},{7,6},{16,17},{17,16},{1... | collective-permute-start | bytes 3145736 | tf_op jit(solution)/shard_map/ppermute | solution.py:348
  62.8 1.9 %collective-permute-start.9 = (bf16[4,55,16,128]{3,2,1,0:T(8,128)(2,1)S(1)}, bf16[4,55,16,128]{3,2,1,0:T(8,128)(2,1)S(1)}, u32[]{:S(2)}, u32[]{:S(2)}) collective-permute-start(bf16[4,55,16,128]{3,2,1,0:T(8,128)(2,1)S(1)} %all-to-all-done.1.m0), channel_id=1, source_target_pairs={{0,1},{1,0},{2,3},{3,2},{4,5},{5,4},{6,7},{7,6},{16,17},{17,16},{1... | collective-permute-start | bytes 2703368 | tf_op jit(solution)/shard_map/ppermute | solution.py:347
  64.7 1.6 %pick.1 = (bf16[352,512]{1,0:T(8,128)(2,1)S(1)}, s32[1,512]{1,0:T(1,128)S(1)}) custom-call(bf16[4,8,2880]{2,1,0:T(8,128)(2,1)S(1)} %bitcast.7, s32[1,512]{1,0:T(1,128)S(1)} %bitcast.8), custom_call_target="tpu_custom_call" | custom-call | tf_op jit(solution)/shard_map/pick/pallas_call | solution.py:349
  66.4 2.6 %collective-permute-start.6 = (bf16[2,55,16,128]{3,2,1,0:T(8,128)(2,1)S(1)}, bf16[2,55,16,128]{3,2,1,0:T(8,128)(2,1)S(1)}, u32[]{:S(2)}, u32[]{:S(2)}) collective-permute-start(bf16[2,55,16,128]{3,2,1,0:T(8,128)(2,1)S(1)} %slice.6), channel_id=1, source_target_pairs={{0,16},{1,3},{2,18},{3,5},{4,20},{5,7},{6,22},{7,1},{16,8},{17,19}... | collective-permute-start | bytes 1351688 | tf_op jit(solution)/shard_map/ppermute | solution.py:362
  69.1 3.9 %collective-permute-start.7 = (bf16[2,55,16,128]{3,2,1,0:T(8,128)(2,1)S(1)}, bf16[2,55,16,128]{3,2,1,0:T(8,128)(2,1)S(1)}, u32[]{:S(2)}, u32[]{:S(2)}) collective-permute-start(bf16[2,55,16,128]{3,2,1,0:T(8,128)(2,1)S(1)} %slice.8), channel_id=1, source_target_pairs={{0,24},{1,7},{2,26},{3,1},{4,28},{5,3},{6,30},{7,5},{16,0},{17,23}... | collective-permute-start | bytes 1351688 | tf_op jit(solution)/shard_map/ppermute | solution.py:363
  72.9 6.2 %collective-permute-start.11 = (bf16[4,55,16,128]{3,2,1,0:T(8,128)(2,1)S(1)}, bf16[4,55,16,128]{3,2,1,0:T(8,128)(2,1)S(1)}, u32[]{:S(2)}, u32[]{:S(2)}) collective-permute-start(bf16[4,55,16,128]{3,2,1,0:T(8,128)(2,1)S(1)} %collective-permute-done.5.m2), channel_id=1, source_target_pairs={{0,1},{1,0},{2,3},{3,2},{4,5},{5,4},{6,7},{7,6},{16,17},{17,16},{1... | collective-permute-start | bytes 2703368 | tf_op jit(solution)/shard_map/ppermute | solution.py:366
  79.2 1.9 %collective-permute-start.10 = (bf16[4,55,16,128]{3,2,1,0:T(8,128)(2,1)S(1)}, bf16[4,55,16,128]{3,2,1,0:T(8,128)(2,1)S(1)}, u32[]{:S(2)}, u32[]{:S(2)}) collective-permute-start(bf16[4,55,16,128]{3,2,1,0:T(8,128)(2,1)S(1)} %collective-permute-done.4.m1), channel_id=1, source_target_pairs={{0,1},{1,0},{2,3},{3,2},{4,5},{5,4},{6,7},{7,6},{16,17},{17,16},{1... | collective-permute-start | bytes 2703368 | tf_op jit(solution)/shard_map/ppermute | solution.py:365
  81.2 0.1 constant_dynamic-update-slice_fusion.5.m3
  81.3 3.9 %collective-permute-start.12 = (bf16[4,55,16,128]{3,2,1,0:T(8,128)(2,1)S(1)}, bf16[4,55,16,128]{3,2,1,0:T(8,128)(2,1)S(1)}, u32[]{:S(2)}, u32[]{:S(2)}) collective-permute-start(bf16[4,55,16,128]{3,2,1,0:T(8,128)(2,1)S(1)} %constant_dynamic-update-slice_fusion.5.m3), channel_id=1, source_target_pairs={{0,1},{1,0},{2,3},{3,2},{4,5},{5,4},{6,7},{7,6},{16,17},{17,16},{1... | collective-permute-start | bytes 2703368 | tf_op jit(solution)/shard_map/ppermute | solution.py:368
  85.8 1.4 %collective-permute-done.12.o3 = bf16[4,55,16,128]{3,2,1,0:T(8,128)(2,1)S(1)} collective-permute-done((bf16[4,55,16,128]{3,2,1,0:T(8,128)(2,1)S(1)}, bf16[4,55,16,128]{3,2,1,0:T(8,128)(2,1)S(1)}, u32[]{:S(2)}, u32[]{:S(2)}) %collective-permute-start.12) | collective-permute-done | bytes 901152 | tf_op jit(solution)/shard_map/ppermute | solution.py:368
  87.2 7.9 %tail.1 = bf16[4,8,2880]{2,1,0:T(8,128)(2,1)} custom-call(s32[1]{0:T(128)S(6)} %copy.12.limit_ref, bf16[352,512]{1,0:T(8,128)(2,1)S(1)} %get-tuple-element.16.xg_ref, s32[1,512]{1,0:T(1,128)S(1)} %get-tuple-element.17.place_ref, bf16[4,55,16,128]{3,2,1,0:T(8,128)(2,1)S(1)} %all-to-all-done.1.m0, bf16[4,55,16,128]{3,2,1,0:T(8,128)(2,1)S(1)} %collective-permute-done.4.m1, ...), custom_call_target="tpu_custom_call" | custom-call | tf_op jit(solution)/shard_map/tail/pallas_call | solution.py:371
  (26 shorter events, 0.3 us)
Async XLA Ops:
  1.6 15.9 %copy-start.2 = (bf16[1,512,128]{2,1,0:T(8,128)(2,1)S(1)}, bf16[1,512,128]{2,1,0:T(8,128)(2,1)}, u32[]{:S(2)}) copy-start(bf16[1,512,128]{2,1,0:T(8,128)(2,1)} %param.7) | copy-start | bytes 393220
  1.6 29.8 %all-to-all-start = ((bf16[16,56,128]{2,1,0:T(8,128)(2,1)}), bf16[16,56,128]{2,1,0:T(8,128)(2,1)S(1)}, u32[]{:S(2)}, u32[]{:S(2)}) async-start(bf16[16,56,128]{2,1,0:T(8,128)(2,1)} %form.1), calls=%async_computation | async-start | bytes 458752 | tf_op jit(solution)/shard_map/all_to_all | solution.py:333
  17.5 7.5 %collective-permute-start = (bf16[512,128]{1,0:T(8,128)(2,1)S(1)}, bf16[512,128]{1,0:T(8,128)(2,1)S(1)}, u32[]{:S(2)}, u32[]{:S(2)}) collective-permute-start(bf16[512,128]{1,0:T(8,128)(2,1)S(1)} %bitcast.9), channel_id=1, source_target_pairs={{0,8},{1,9},{2,10},{3,11},{4,12},{5,13},{6,14},{7,15},{16,24},{17,... | collective-permute-start | bytes 393224 | tf_op jit(solution)/shard_map/ppermute | solution.py:319
  25.0 11.6 %collective-permute-start.1 = (bf16[1024,128]{1,0:T(8,128)(2,1)S(1)}, bf16[1024,128]{1,0:T(8,128)(2,1)S(1)}, u32[]{:S(2)}, u32[]{:S(2)}) collective-permute-start(bf16[1024,128]{1,0:T(8,128)(2,1)S(1)} %pad_maximum_fusion), channel_id=1, source_target_pairs={{0,2},{1,7},{2,4},{3,1},{4,6},{5,3},{6,0},{7,5},{16,18},{17,23},{1... | collective-permute-start | bytes 786440 | tf_op jit(solution)/shard_map/ppermute | solution.py:320
  29.4 11.8 %collective-permute-start.2 = (bf16[1024,128]{1,0:T(8,128)(2,1)S(1)}, bf16[1024,128]{1,0:T(8,128)(2,1)S(1)}, u32[]{:S(2)}, u32[]{:S(2)}) collective-permute-start(bf16[1024,128]{1,0:T(8,128)(2,1)S(1)} %pad_maximum_fusion), channel_id=1, source_target_pairs={{0,6},{1,3},{2,0},{3,5},{4,2},{5,7},{6,4},{7,1},{16,22},{17,19},{1... | collective-permute-start | bytes 786440 | tf_op jit(solution)/shard_map/ppermute | solution.py:321
  32.4 16.9 %all-to-all-start.1 = ((bf16[4,55,16,128]{3,2,1,0:T(8,128)(2,1)}), bf16[4,55,16,128]{3,2,1,0:T(8,128)(2,1)S(1)}, u32[]{:S(2)}, u32[]{:S(2)}) async-start(bf16[4,55,16,128]{3,2,1,0:T(8,128)(2,1)} %merge.1), calls=%async_computation.1 | async-start | bytes 1802240 | tf_op jit(solution)/shard_map/all_to_all | solution.py:343
  36.6 12.7 %collective-permute-start.3 = (bf16[1024,128]{1,0:T(8,128)(2,1)S(1)}, bf16[1024,128]{1,0:T(8,128)(2,1)S(1)}, u32[]{:S(2)}, u32[]{:S(2)}) collective-permute-start(bf16[1024,128]{1,0:T(8,128)(2,1)S(1)} %collective-permute-done.1), channel_id=1, source_target_pairs={{0,2},{1,7},{2,4},{3,1},{4,6},{5,3},{6,0},{7,5},{16,18},{17,23},{1... | collective-permute-start | bytes 786440 | tf_op jit(solution)/shard_map/ppermute | solution.py:322
  41.3 23.4 %copy-start = (bf16[4,1,8,2880]{3,2,1,0:T(8,128)(2,1)S(1)}, bf16[4,1,8,2880]{3,2,1,0:T(8,128)(2,1)}, u32[]{:S(2)}) copy-start(bf16[4,1,8,2880]{3,2,1,0:T(8,128)(2,1)} %param.9) | copy-start | bytes 552964
  49.3 15.5 %copy-start.1 = (s32[512]{0:T(512)S(1)}, s32[512]{0:T(512)}, u32[]{:S(2)}) copy-start(s32[512]{0:T(512)} %matching_ref.1) | copy-start | bytes 6148
  49.3 17.1 %collective-permute-start.4 = (bf16[4,55,16,128]{3,2,1,0:T(8,128)(2,1)S(1)}, bf16[4,55,16,128]{3,2,1,0:T(8,128)(2,1)S(1)}, u32[]{:S(2)}, u32[]{:S(2)}) collective-permute-start(bf16[4,55,16,128]{3,2,1,0:T(8,128)(2,1)S(1)} %all-to-all-done.1.m0), channel_id=1, source_target_pairs={{0,16},{1,3},{2,18},{3,5},{4,20},{5,7},{6,22},{7,1},{16,8},{17,19}... | collective-permute-start | bytes 2703368 | tf_op jit(solution)/shard_map/ppermute | solution.py:345
  51.2 17.8 %collective-permute-start.5 = (bf16[4,55,16,128]{3,2,1,0:T(8,128)(2,1)S(1)}, bf16[4,55,16,128]{3,2,1,0:T(8,128)(2,1)S(1)}, u32[]{:S(2)}, u32[]{:S(2)}) collective-permute-start(bf16[4,55,16,128]{3,2,1,0:T(8,128)(2,1)S(1)} %all-to-all-done.1.m0), channel_id=1, source_target_pairs={{0,24},{1,7},{2,26},{3,1},{4,28},{5,3},{6,30},{7,5},{16,0},{17,23}... | collective-permute-start | bytes 2703368 | tf_op jit(solution)/shard_map/ppermute | solution.py:346
  56.5 22.7 %collective-permute-start.8 = (bf16[4096,128]{1,0:T(8,128)(2,1)S(1)}, bf16[4096,128]{1,0:T(8,128)(2,1)S(1)}, u32[]{:S(2)}, u32[]{:S(2)}) collective-permute-start(bf16[4096,128]{1,0:T(8,128)(2,1)S(1)} %constant_dynamic-update-slice_fusion.near_ref), channel_id=1, source_target_pairs={{0,1},{1,0},{2,3},{3,2},{4,5},{5,4},{6,7},{7,6},{16,17},{17,16},{1... | collective-permute-start | bytes 3145736 | tf_op jit(solution)/shard_map/ppermute | solution.py:348
  62.8 16.4 %collective-permute-start.9 = (bf16[4,55,16,128]{3,2,1,0:T(8,128)(2,1)S(1)}, bf16[4,55,16,128]{3,2,1,0:T(8,128)(2,1)S(1)}, u32[]{:S(2)}, u32[]{:S(2)}) collective-permute-start(bf16[4,55,16,128]{3,2,1,0:T(8,128)(2,1)S(1)} %all-to-all-done.1.m0), channel_id=1, source_target_pairs={{0,1},{1,0},{2,3},{3,2},{4,5},{5,4},{6,7},{7,6},{16,17},{17,16},{1... | collective-permute-start | bytes 2703368 | tf_op jit(solution)/shard_map/ppermute | solution.py:347
  66.4 14.8 %collective-permute-start.6 = (bf16[2,55,16,128]{3,2,1,0:T(8,128)(2,1)S(1)}, bf16[2,55,16,128]{3,2,1,0:T(8,128)(2,1)S(1)}, u32[]{:S(2)}, u32[]{:S(2)}) collective-permute-start(bf16[2,55,16,128]{3,2,1,0:T(8,128)(2,1)S(1)} %slice.6), channel_id=1, source_target_pairs={{0,16},{1,3},{2,18},{3,5},{4,20},{5,7},{6,22},{7,1},{16,8},{17,19}... | collective-permute-start | bytes 1351688 | tf_op jit(solution)/shard_map/ppermute | solution.py:362
  69.1 12.1 %collective-permute-start.7 = (bf16[2,55,16,128]{3,2,1,0:T(8,128)(2,1)S(1)}, bf16[2,55,16,128]{3,2,1,0:T(8,128)(2,1)S(1)}, u32[]{:S(2)}, u32[]{:S(2)}) collective-permute-start(bf16[2,55,16,128]{3,2,1,0:T(8,128)(2,1)S(1)} %slice.8), channel_id=1, source_target_pairs={{0,24},{1,7},{2,26},{3,1},{4,28},{5,3},{6,30},{7,5},{16,0},{17,23}... | collective-permute-start | bytes 1351688 | tf_op jit(solution)/shard_map/ppermute | solution.py:363
  72.9 12.8 %collective-permute-start.11 = (bf16[4,55,16,128]{3,2,1,0:T(8,128)(2,1)S(1)}, bf16[4,55,16,128]{3,2,1,0:T(8,128)(2,1)S(1)}, u32[]{:S(2)}, u32[]{:S(2)}) collective-permute-start(bf16[4,55,16,128]{3,2,1,0:T(8,128)(2,1)S(1)} %collective-permute-done.5.m2), channel_id=1, source_target_pairs={{0,1},{1,0},{2,3},{3,2},{4,5},{5,4},{6,7},{7,6},{16,17},{17,16},{1... | collective-permute-start | bytes 2703368 | tf_op jit(solution)/shard_map/ppermute | solution.py:366
  79.2 6.6 %collective-permute-start.10 = (bf16[4,55,16,128]{3,2,1,0:T(8,128)(2,1)S(1)}, bf16[4,55,16,128]{3,2,1,0:T(8,128)(2,1)S(1)}, u32[]{:S(2)}, u32[]{:S(2)}) collective-permute-start(bf16[4,55,16,128]{3,2,1,0:T(8,128)(2,1)S(1)} %collective-permute-done.4.m1), channel_id=1, source_target_pairs={{0,1},{1,0},{2,3},{3,2},{4,5},{5,4},{6,7},{7,6},{16,17},{17,16},{1... | collective-permute-start | bytes 2703368 | tf_op jit(solution)/shard_map/ppermute | solution.py:365
  81.3 5.9 %collective-permute-start.12 = (bf16[4,55,16,128]{3,2,1,0:T(8,128)(2,1)S(1)}, bf16[4,55,16,128]{3,2,1,0:T(8,128)(2,1)S(1)}, u32[]{:S(2)}, u32[]{:S(2)}) collective-permute-start(bf16[4,55,16,128]{3,2,1,0:T(8,128)(2,1)S(1)} %constant_dynamic-update-slice_fusion.5.m3), channel_id=1, source_target_pairs={{0,1},{1,0},{2,3},{3,2},{4,5},{5,4},{6,7},{7,6},{16,17},{17,16},{1... | collective-permute-start | bytes 2703368 | tf_op jit(solution)/shard_map/ppermute | solution.py:368

commit v3 on v2

--- a/solution.py
+++ b/solution.py
@@ -56,6 +56,7 @@
 X_BACK = moves(lambda y, x, c: (y, x + 1 if c else x - 1, c))
 Y_FAR = moves(lambda y, x, c: (y + 2, x, c))
 RING_UP = moves(lambda y, x, c: (y, x + 1, c) if c else (y + 1, x, c))
+RING_FAR = moves(lambda y, x, c: (y, x + 2, c) if c else (y + 2, x, c))
 RING_DOWN = moves(lambda y, x, c: (y, x - 1, c) if c else (y - 1, x, c))
 
 
@@ -145,9 +146,13 @@
     return picked[0:1] * 16 + picked[1:2]
 
 
-def pick_kernel(x_ref, matching_ref, xg_ref, place_ref, xs_ref, a_ref):
+def pick_kernel(x_ref, matching_ref, xg_ref, place_ref, row_ref, xs_ref, a_ref):
     place = slot_places(matching_ref[...])
     place_ref[...] = place
+    row = jnp.where(place >= 284, ((9 * place - 2560) >> 2) + 1, -1)
+    row_ref[...] = jnp.where(
+        lax.broadcasted_iota(jnp.int32, (512, 512), 0) == row, 1.0, 0.0
+    ).astype(jnp.bfloat16)
     xs_ref[:, 2816:] = jnp.zeros((ROWS, 256), jnp.float32)
     xs_ref[:, :D] = x_ref[...].astype(jnp.float32).reshape(ROWS, D)
     xs = xs_ref[...]
@@ -187,7 +192,7 @@
 
 
 def tail_kernel(
-    limit_ref, xg_ref, place_ref, m0, m1, m2, m3, o0, o1, o2, o3, near_ref, far_ref, out_ref,
+    limit_ref, xg_ref, place_ref, row_ref, m0, m1, m2, m3, o0, o1, o2, o3, near_ref, far_ref, out_ref,
     s_ref, w_ref, og_ref, acc_ref,
 ):
     halves = ((m0, m1, m2, m3), (o0, o1, o2, o3))
@@ -236,18 +241,20 @@
     top = jnp.maximum(jnp.max(peak, 1, keepdims=True), jnp.max(own, 1, keepdims=True))
     floor = top * scale
 
-    ones = jnp.float32(1)
+    lane = lax.broadcasted_iota(jnp.int32, (1, 128), 1)
+    kept = jnp.where(lane < HEAD, 0.0, 1.0).astype(jnp.bfloat16)
+    ones = jnp.where(lane < HEAD, 1.0, 0.0).astype(jnp.bfloat16)
 
     def with_ones(piece):
-        lane = lax.broadcasted_iota(jnp.int32, piece.shape, 1)
-        return jnp.where(lane < HEAD, ones, piece.astype(jnp.float32)).astype(jnp.bfloat16)
+        return piece * kept + ones
 
     weights = jnp.where(allowed, jnp.exp2(own * scale - floor), 0.0).astype(jnp.bfloat16)
     summed = jnp.dot(weights, with_ones(own_kv), preferred_element_type=jnp.float32)
     for k in range(chunks):
-        weights = jnp.exp2(s_ref[:, CHUNK * k : CHUNK * k + CHUNK] * scale - floor)
+        powers = s_ref[:, CHUNK * k : CHUNK * k + CHUNK] * scale - floor
+        weights = jnp.exp2(powers.astype(jnp.bfloat16))
         summed = summed + jnp.dot(
-            weights.astype(jnp.bfloat16),
+            weights,
             with_ones(read_keys(k)),
             preferred_element_type=jnp.float32,
         )
@@ -258,8 +265,6 @@
 
     place = place_ref[...]
     unit = 9 * place - 2560
-    base = (unit >> 2) + 1
-    shown = jnp.where(place >= 284, base, -1)
     padded = og_ref[...]
     moved = [
         pltpu.roll(padded, 1, 1)[:, 128:640],
@@ -267,10 +272,7 @@
         pltpu.roll(padded, 767, 1)[:, 128:640],
     ]
     stacked = jnp.concatenate(moved, 0).astype(jnp.bfloat16)
-    chosen = jnp.where(
-        lax.broadcasted_iota(jnp.int32, (512, 512), 0) == shown, 1.0, 0.0
-    ).astype(jnp.bfloat16)
-    picked = jnp.dot(stacked, chosen, preferred_element_type=jnp.float32)
+    picked = jnp.dot(stacked, row_ref[...], preferred_element_type=jnp.float32)
     phase = unit & 3
     for i in range(9):
         for c in range(4):
@@ -314,7 +316,6 @@
         core == 0, jnp.concatenate([half0, half1], 1), jnp.concatenate([half1, half0], 1)
     )
     x = inputs[:, 0]
-    x = inputs[:, 0]
     prefix = prefix_kv[0]
     pair = lax.concatenate([prefix, lax.ppermute(prefix, AXES, Y_FAR)], 0)
     behind = lax.ppermute(pair, AXES, X_OUT)
@@ -344,25 +345,28 @@
     lines, core_keys = lax.optimization_barrier((lines, core_keys))
     low = lax.ppermute(lines, AXES, RING_UP)
     high = lax.ppermute(lines, AXES, RING_DOWN)
-    other_lines = lax.ppermute(lines, AXES, CORE_SWAP)
-    other_keys = lax.ppermute(core_keys, AXES, CORE_SWAP)
-    gathered, places = pl.pallas_call(
+    end1 = lax.ppermute(lines[2:], AXES, RING_FAR)
+    x, _ = lax.optimization_barrier((inputs[:, 0], lines))
+    gathered, places, out_rows = pl.pallas_call(
         pick_kernel,
         out_shape=(
             jax.ShapeDtypeStruct((11 * ROWS, 512), bf16),
             jax.ShapeDtypeStruct((1, 512), jnp.int32),
+            jax.ShapeDtypeStruct((512, 512), bf16),
         ),
         in_specs=[VMEM] * 2,
-        out_specs=(VMEM, VMEM),
+        out_specs=(VMEM, VMEM, VMEM),
         scratch_shapes=[pltpu.VMEM((ROWS, 3072), f32), pltpu.VMEM((11 * ROWS, 3072), bf16)],
         compiler_params=pltpu.CompilerParams(vmem_limit_bytes=12 * MIB),
         name="pick",
     )(x, matching.reshape(1, 512))
+    swapped, core_keys, _ = lax.optimization_barrier((lines, core_keys, gathered))
+    other_lines = lax.ppermute(swapped, AXES, CORE_SWAP)
+    other_keys = lax.ppermute(core_keys, AXES, CORE_SWAP)
     low, gathered = lax.optimization_barrier((low, gathered))
     end0 = lax.ppermute(low[:2], AXES, RING_UP)
-    end1 = lax.ppermute(high[2:], AXES, RING_DOWN)
-    side, other_keys, other_lines = lax.optimization_barrier((low, other_keys, other_lines))
-    other_low = lax.ppermute(side, AXES, CORE_SWAP)
+    low, end1 = lax.optimization_barrier((low, end1))
+    other_low = lax.ppermute(low, AXES, CORE_SWAP)
     other_high = lax.ppermute(high, AXES, CORE_SWAP)
     ends = lax.concatenate([end0, end1], 0)
     other_ends = lax.ppermute(ends, AXES, CORE_SWAP)
@@ -371,7 +375,7 @@
     output = pl.pallas_call(
         tail_kernel,
         out_shape=jax.ShapeDtypeStruct(x.shape, bf16),
-        in_specs=[SMEM] + [VMEM] * 12,
+        in_specs=[SMEM] + [VMEM] * 13,
         out_specs=VMEM,
         scratch_shapes=[
             pltpu.VMEM((QHEADS * ROWS, 16 * SHARD), f32),
@@ -381,7 +385,7 @@
         ],
         compiler_params=pltpu.CompilerParams(vmem_limit_bytes=20 * MIB),
         name="tail",
-    )(prefix_blocks, gathered, places, *mine, *other, core_keys, other_keys)
+    )(prefix_blocks, gathered, places, out_rows, *mine, *other, core_keys, other_keys)
     return output[:, None]
 
 

time: 96.1 us -> 97.8 us (1.018)
  the two profiles are of different devices: /device:TPU:1 before, /device:TPU:13 now
where the time goes in v3:
time: 97.8 us; the launch traced here: 97.1 us
  starting transfers between devices  70.8 us (72%)
  waiting for transfers between devices  13.4 us (14%)
  Pallas kernels  11.7 us (12%)
    all_to_all x1, starting transfers between devices, shards(): lax.all_to_all(formed, AXES, 0, 0, tiled=True, axis_index_groups=Z_GROUPS)  15 us
    ppermute x1, starting transfers between devices, shards(): other_lines = lax.ppermute(swapped, AXES, CORE_SWAP)  12.3 us
    ppermute x1, starting transfers between devices, shards(): low = lax.ppermute(lines, AXES, RING_UP)  9.35 us
    pallas_call x1, Pallas kernels, shards(): pl.pallas_call(tail_kernel, out_shape=jax.ShapeDtypeStruct(x.shape, bf16)...  7.31 us
    ppermute x1, waiting for transfers between devices, shards(): across = lax.ppermute(behind, AXES, X_OUT)  5.79 us
    all_to_all x1, starting transfers between devices, shards(): lax.all_to_all(merged, AXES, 0, 0, tiled=True, axis_index_groups=line_gro...  4.35 us
    ppermute x1, starting transfers between devices, shards(): end0 = lax.ppermute(low[:2], AXES, RING_UP)  4.11 us
    ppermute x1, starting transfers between devices, shards(): pair = lax.concatenate([prefix, lax.ppermute(prefix, AXES, Y_FAR)], 0)  3.92 us
  transfers between devices with their start and end apart: 15, of which 4 were waited for; matrix products, arithmetic and copies ran while one was open for 0% of the time, Pallas kernels for 3%

profile of v3, /device:TPU:13, one launch (start us, length us, event | category | flops | bytes accessed | tf_op | source)
XLA Modules:
  0.0 97.1 jit_solution(2777609126046825224)
XLA Ops:
  0.0 1.6 %form.1 = bf16[16,56,128]{2,1,0:T(8,128)(2,1)} custom-call(s32[512]{0:T(512)} %matching_ref.1, bf16[1,6480]{1,0:T(2,128)(2,1)} %tile_ref.1), custom_call_target="tpu_custom_call" | custom-call | tf_op jit(solution)/shard_map/form/pallas_call | solution.py:326
  1.6 15.0 %all-to-all-start = ((bf16[16,56,128]{2,1,0:T(8,128)(2,1)}), bf16[16,56,128]{2,1,0:T(8,128)(2,1)S(1)}, u32[]{:S(2)}, u32[]{:S(2)}) async-start(bf16[16,56,128]{2,1,0:T(8,128)(2,1)} %form.1), calls=%async_computation | async-start | bytes 458752 | tf_op jit(solution)/shard_map/all_to_all | solution.py:334
  16.6 3.9 %collective-permute-start = (bf16[512,128]{1,0:T(8,128)(2,1)S(1)}, bf16[512,128]{1,0:T(8,128)(2,1)S(1)}, u32[]{:S(2)}, u32[]{:S(2)}) collective-permute-start(bf16[512,128]{1,0:T(8,128)(2,1)S(1)} %bitcast.9), channel_id=1, source_target_pairs={{0,8},{1,9},{2,10},{3,11},{4,12},{5,13},{6,14},{7,15},{16,24},{17,... | collective-permute-start | bytes 393224 | tf_op jit(solution)/shard_map/ppermute | solution.py:320
  20.6 3.6 %collective-permute-done = bf16[512,128]{1,0:T(8,128)(2,1)S(1)} collective-permute-done((bf16[512,128]{1,0:T(8,128)(2,1)S(1)}, bf16[512,128]{1,0:T(8,128)(2,1)S(1)}, u32[]{:S(2)}, u32[]{:S(2)}) %collective-permute-start) | collective-permute-done | bytes 131104 | tf_op jit(solution)/shard_map/ppermute | solution.py:320
  24.2 2.2 %collective-permute-start.1 = (bf16[1024,128]{1,0:T(8,128)(2,1)S(1)}, bf16[1024,128]{1,0:T(8,128)(2,1)S(1)}, u32[]{:S(2)}, u32[]{:S(2)}) collective-permute-start(bf16[1024,128]{1,0:T(8,128)(2,1)S(1)} %pad_maximum_fusion), channel_id=1, source_target_pairs={{0,2},{1,7},{2,4},{3,1},{4,6},{5,3},{6,0},{7,5},{16,18},{17,23},{1... | collective-permute-start | bytes 786440 | tf_op jit(solution)/shard_map/ppermute | solution.py:321
  26.3 3.1 %collective-permute-start.2 = (bf16[1024,128]{1,0:T(8,128)(2,1)S(1)}, bf16[1024,128]{1,0:T(8,128)(2,1)S(1)}, u32[]{:S(2)}, u32[]{:S(2)}) collective-permute-start(bf16[1024,128]{1,0:T(8,128)(2,1)S(1)} %pad_maximum_fusion), channel_id=1, source_target_pairs={{0,6},{1,3},{2,0},{3,5},{4,2},{5,7},{6,4},{7,1},{16,22},{17,19},{1... | collective-permute-start | bytes 786440 | tf_op jit(solution)/shard_map/ppermute | solution.py:322
  29.5 1.0 %merge.1 = bf16[4,55,16,128]{3,2,1,0:T(8,128)(2,1)} custom-call(bf16[16,56,128]{2,1,0:T(8,128)(2,1)S(1)} %all-to-all-done.in_ref), custom_call_target="tpu_custom_call" | custom-call | tf_op jit(solution)/shard_map/merge/pallas_call | solution.py:335
  30.5 4.3 %all-to-all-start.1 = ((bf16[4,55,16,128]{3,2,1,0:T(8,128)(2,1)}), bf16[4,55,16,128]{3,2,1,0:T(8,128)(2,1)S(1)}, u32[]{:S(2)}, u32[]{:S(2)}) async-start(bf16[4,55,16,128]{3,2,1,0:T(8,128)(2,1)} %merge.1), calls=%async_computation.1 | async-start | bytes 1802240 | tf_op jit(solution)/shard_map/all_to_all | solution.py:344
  34.9 2.2 %collective-permute-start.3 = (bf16[1024,128]{1,0:T(8,128)(2,1)S(1)}, bf16[1024,128]{1,0:T(8,128)(2,1)S(1)}, u32[]{:S(2)}, u32[]{:S(2)}) collective-permute-start(bf16[1024,128]{1,0:T(8,128)(2,1)S(1)} %collective-permute-done.1), channel_id=1, source_target_pairs={{0,2},{1,7},{2,4},{3,1},{4,6},{5,3},{6,0},{7,5},{16,18},{17,23},{1... | collective-permute-start | bytes 786440 | tf_op jit(solution)/shard_map/ppermute | solution.py:323
  37.2 5.8 %collective-permute-done.3 = bf16[1024,128]{1,0:T(8,128)(2,1)S(1)} collective-permute-done((bf16[1024,128]{1,0:T(8,128)(2,1)S(1)}, bf16[1024,128]{1,0:T(8,128)(2,1)S(1)}, u32[]{:S(2)}, u32[]{:S(2)}) %collective-permute-start.3) | collective-permute-done | bytes 262176 | tf_op jit(solution)/shard_map/ppermute | solution.py:323
  43.0 9.4 %collective-permute-start.4 = (bf16[4,55,16,128]{3,2,1,0:T(8,128)(2,1)S(1)}, bf16[4,55,16,128]{3,2,1,0:T(8,128)(2,1)S(1)}, u32[]{:S(2)}, u32[]{:S(2)}) collective-permute-start(bf16[4,55,16,128]{3,2,1,0:T(8,128)(2,1)S(1)} %all-to-all-done.1.m0), channel_id=1, source_target_pairs={{0,16},{1,3},{2,18},{3,5},{4,20},{5,7},{6,22},{7,1},{16,8},{17,19}... | collective-permute-start | bytes 2703368 | tf_op jit(solution)/shard_map/ppermute | solution.py:346
  52.4 1.9 %collective-permute-start.6 = (bf16[4,55,16,128]{3,2,1,0:T(8,128)(2,1)S(1)}, bf16[4,55,16,128]{3,2,1,0:T(8,128)(2,1)S(1)}, u32[]{:S(2)}, u32[]{:S(2)}) collective-permute-start(bf16[4,55,16,128]{3,2,1,0:T(8,128)(2,1)S(1)} %all-to-all-done.1.m0), channel_id=1, source_target_pairs={{0,24},{1,7},{2,26},{3,1},{4,28},{5,3},{6,30},{7,5},{16,0},{17,23}... | collective-permute-start | bytes 2703368 | tf_op jit(solution)/shard_map/ppermute | solution.py:347
  54.4 3.7 %collective-permute-start.5 = (bf16[2,55,16,128]{3,2,1,0:T(8,128)(2,1)S(1)}, bf16[2,55,16,128]{3,2,1,0:T(8,128)(2,1)S(1)}, u32[]{:S(2)}, u32[]{:S(2)}) collective-permute-start(bf16[2,55,16,128]{3,2,1,0:T(8,128)(2,1)S(1)} %slice.6), channel_id=1, source_target_pairs={{0,8},{1,5},{2,10},{3,7},{4,12},{5,1},{6,14},{7,3},{16,24},{17,21}... | collective-permute-start | bytes 1351688 | tf_op jit(solution)/shard_map/ppermute | solution.py:348
  58.1 1.8 %pick.1 = (bf16[352,512]{1,0:T(8,128)(2,1)S(1)}, s32[1,512]{1,0:T(1,128)S(1)}, bf16[512,512]{1,0:T(8,128)(2,1)S(1)}) custom-call(bf16[4,8,2880]{2,1,0:T(8,128)(2,1)S(1)} %bitcast.7, s32[1,512]{1,0:T(1,128)S(1)} %bitcast.8), custom_call_target="tpu_custom_call" | custom-call | tf_op jit(solution)/shard_map/pick/pallas_call | solution.py:350
  59.9 2.6 %collective-permute-done.4.m1 = bf16[4,55,16,128]{3,2,1,0:T(8,128)(2,1)S(1)} collective-permute-done((bf16[4,55,16,128]{3,2,1,0:T(8,128)(2,1)S(1)}, bf16[4,55,16,128]{3,2,1,0:T(8,128)(2,1)S(1)}, u32[]{:S(2)}, u32[]{:S(2)}) %collective-permute-start.4) | collective-permute-done | bytes 901152 | tf_op jit(solution)/shard_map/ppermute | solution.py:346
  62.6 4.1 %collective-permute-start.7 = (bf16[2,55,16,128]{3,2,1,0:T(8,128)(2,1)S(1)}, bf16[2,55,16,128]{3,2,1,0:T(8,128)(2,1)S(1)}, u32[]{:S(2)}, u32[]{:S(2)}) collective-permute-start(bf16[2,55,16,128]{3,2,1,0:T(8,128)(2,1)S(1)} %slice.7), channel_id=1, source_target_pairs={{0,16},{1,3},{2,18},{3,5},{4,20},{5,7},{6,22},{7,1},{16,8},{17,19}... | collective-permute-start | bytes 1351688 | tf_op jit(solution)/shard_map/ppermute | solution.py:367
  66.7 12.3 %collective-permute-start.8 = (bf16[4,55,16,128]{3,2,1,0:T(8,128)(2,1)S(1)}, bf16[4,55,16,128]{3,2,1,0:T(8,128)(2,1)S(1)}, u32[]{:S(2)}, u32[]{:S(2)}) collective-permute-start(bf16[4,55,16,128]{3,2,1,0:T(8,128)(2,1)S(1)} %all-to-all-done.1.m0), channel_id=1, source_target_pairs={{0,1},{1,0},{2,3},{3,2},{4,5},{5,4},{6,7},{7,6},{16,17},{17,16},{1... | collective-permute-start | bytes 2703368 | tf_op jit(solution)/shard_map/ppermute | solution.py:364
  78.9 1.9 %collective-permute-start.12 = (bf16[4096,128]{1,0:T(8,128)(2,1)S(1)}, bf16[4096,128]{1,0:T(8,128)(2,1)S(1)}, u32[]{:S(2)}, u32[]{:S(2)}) collective-permute-start(bf16[4096,128]{1,0:T(8,128)(2,1)S(1)} %constant_dynamic-update-slice_fusion.near_ref), channel_id=1, source_target_pairs={{0,1},{1,0},{2,3},{3,2},{4,5},{5,4},{6,7},{7,6},{16,17},{17,16},{1... | collective-permute-start | bytes 3145736 | tf_op jit(solution)/shard_map/ppermute | solution.py:365
  80.9 2.4 %collective-permute-start.9 = (bf16[4,55,16,128]{3,2,1,0:T(8,128)(2,1)S(1)}, bf16[4,55,16,128]{3,2,1,0:T(8,128)(2,1)S(1)}, u32[]{:S(2)}, u32[]{:S(2)}) collective-permute-start(bf16[4,55,16,128]{3,2,1,0:T(8,128)(2,1)S(1)} %collective-permute-done.4.m1), channel_id=1, source_target_pairs={{0,1},{1,0},{2,3},{3,2},{4,5},{5,4},{6,7},{7,6},{16,17},{17,16},{1... | collective-permute-start | bytes 2703368 | tf_op jit(solution)/shard_map/ppermute | solution.py:369
  83.3 1.9 %collective-permute-start.10 = (bf16[4,55,16,128]{3,2,1,0:T(8,128)(2,1)S(1)}, bf16[4,55,16,128]{3,2,1,0:T(8,128)(2,1)S(1)}, u32[]{:S(2)}, u32[]{:S(2)}) collective-permute-start(bf16[4,55,16,128]{3,2,1,0:T(8,128)(2,1)S(1)} %collective-permute-done.6.m2), channel_id=1, source_target_pairs={{0,1},{1,0},{2,3},{3,2},{4,5},{5,4},{6,7},{7,6},{16,17},{17,16},{1... | collective-permute-start | bytes 2703368 | tf_op jit(solution)/shard_map/ppermute | solution.py:370
  85.3 0.1 constant_dynamic-update-slice_fusion.5.m3
  85.4 2.4 %collective-permute-start.11 = (bf16[4,55,16,128]{3,2,1,0:T(8,128)(2,1)S(1)}, bf16[4,55,16,128]{3,2,1,0:T(8,128)(2,1)S(1)}, u32[]{:S(2)}, u32[]{:S(2)}) collective-permute-start(bf16[4,55,16,128]{3,2,1,0:T(8,128)(2,1)S(1)} %constant_dynamic-update-slice_fusion.5.m3), channel_id=1, source_target_pairs={{0,1},{1,0},{2,3},{3,2},{4,5},{5,4},{6,7},{7,6},{16,17},{17,16},{1... | collective-permute-start | bytes 2703368 | tf_op jit(solution)/shard_map/ppermute | solution.py:372
  88.5 1.4 %collective-permute-done.11.o3 = bf16[4,55,16,128]{3,2,1,0:T(8,128)(2,1)S(1)} collective-permute-done((bf16[4,55,16,128]{3,2,1,0:T(8,128)(2,1)S(1)}, bf16[4,55,16,128]{3,2,1,0:T(8,128)(2,1)S(1)}, u32[]{:S(2)}, u32[]{:S(2)}) %collective-permute-start.11) | collective-permute-done | bytes 901152 | tf_op jit(solution)/shard_map/ppermute | solution.py:372
  89.8 7.3 %tail.1 = bf16[4,8,2880]{2,1,0:T(8,128)(2,1)} custom-call(s32[1]{0:T(128)S(6)} %copy.12.limit_ref, bf16[352,512]{1,0:T(8,128)(2,1)S(1)} %get-tuple-element.20.xg_ref, s32[1,512]{1,0:T(1,128)S(1)} %get-tuple-element.21.place_ref, bf16[512,512]{1,0:T(8,128)(2,1)S(1)} %get-tuple-element.22.row_ref, bf16[4,55,16,128]{3,2,1,0:T(8,128)(2,1)S(1)} %all-to-all-done.1.m0, ...), custom_call_target="tpu_custom_call" | custom-call | tf_op jit(solution)/shard_map/tail/pallas_call | solution.py:375
  (26 shorter events, 0.3 us)
Async XLA Ops:
  1.6 15.1 %copy-start.2 = (bf16[1,512,128]{2,1,0:T(8,128)(2,1)S(1)}, bf16[1,512,128]{2,1,0:T(8,128)(2,1)}, u32[]{:S(2)}) copy-start(bf16[1,512,128]{2,1,0:T(8,128)(2,1)} %param.7) | copy-start | bytes 393220
  1.6 27.9 %all-to-all-start = ((bf16[16,56,128]{2,1,0:T(8,128)(2,1)}), bf16[16,56,128]{2,1,0:T(8,128)(2,1)S(1)}, u32[]{:S(2)}, u32[]{:S(2)}) async-start(bf16[16,56,128]{2,1,0:T(8,128)(2,1)} %form.1), calls=%async_computation | async-start | bytes 458752 | tf_op jit(solution)/shard_map/all_to_all | solution.py:334
  16.6 7.5 %collective-permute-start = (bf16[512,128]{1,0:T(8,128)(2,1)S(1)}, bf16[512,128]{1,0:T(8,128)(2,1)S(1)}, u32[]{:S(2)}, u32[]{:S(2)}) collective-permute-start(bf16[512,128]{1,0:T(8,128)(2,1)S(1)} %bitcast.9), channel_id=1, source_target_pairs={{0,8},{1,9},{2,10},{3,11},{4,12},{5,13},{6,14},{7,15},{16,24},{17,... | collective-permute-start | bytes 393224 | tf_op jit(solution)/shard_map/ppermute | solution.py:320
  24.2 10.7 %collective-permute-start.1 = (bf16[1024,128]{1,0:T(8,128)(2,1)S(1)}, bf16[1024,128]{1,0:T(8,128)(2,1)S(1)}, u32[]{:S(2)}, u32[]{:S(2)}) collective-permute-start(bf16[1024,128]{1,0:T(8,128)(2,1)S(1)} %pad_maximum_fusion), channel_id=1, source_target_pairs={{0,2},{1,7},{2,4},{3,1},{4,6},{5,3},{6,0},{7,5},{16,18},{17,23},{1... | collective-permute-start | bytes 786440 | tf_op jit(solution)/shard_map/ppermute | solution.py:321
  26.3 10.8 %collective-permute-start.2 = (bf16[1024,128]{1,0:T(8,128)(2,1)S(1)}, bf16[1024,128]{1,0:T(8,128)(2,1)S(1)}, u32[]{:S(2)}, u32[]{:S(2)}) collective-permute-start(bf16[1024,128]{1,0:T(8,128)(2,1)S(1)} %pad_maximum_fusion), channel_id=1, source_target_pairs={{0,6},{1,3},{2,0},{3,5},{4,2},{5,7},{6,4},{7,1},{16,22},{17,19},{1... | collective-permute-start | bytes 786440 | tf_op jit(solution)/shard_map/ppermute | solution.py:322
  30.5 12.5 %all-to-all-start.1 = ((bf16[4,55,16,128]{3,2,1,0:T(8,128)(2,1)}), bf16[4,55,16,128]{3,2,1,0:T(8,128)(2,1)S(1)}, u32[]{:S(2)}, u32[]{:S(2)}) async-start(bf16[4,55,16,128]{3,2,1,0:T(8,128)(2,1)} %merge.1), calls=%async_computation.1 | async-start | bytes 1802240 | tf_op jit(solution)/shard_map/all_to_all | solution.py:344
  34.9 8.1 %collective-permute-start.3 = (bf16[1024,128]{1,0:T(8,128)(2,1)S(1)}, bf16[1024,128]{1,0:T(8,128)(2,1)S(1)}, u32[]{:S(2)}, u32[]{:S(2)}) collective-permute-start(bf16[1024,128]{1,0:T(8,128)(2,1)S(1)} %collective-permute-done.1), channel_id=1, source_target_pairs={{0,2},{1,7},{2,4},{3,1},{4,6},{5,3},{6,0},{7,5},{16,18},{17,23},{1... | collective-permute-start | bytes 786440 | tf_op jit(solution)/shard_map/ppermute | solution.py:323
  43.0 15.1 %copy-start = (bf16[4,1,8,2880]{3,2,1,0:T(8,128)(2,1)S(1)}, bf16[4,1,8,2880]{3,2,1,0:T(8,128)(2,1)}, u32[]{:S(2)}) copy-start(bf16[4,1,8,2880]{3,2,1,0:T(8,128)(2,1)} %param.9) | copy-start | bytes 552964
  43.0 19.5 %collective-permute-start.4 = (bf16[4,55,16,128]{3,2,1,0:T(8,128)(2,1)S(1)}, bf16[4,55,16,128]{3,2,1,0:T(8,128)(2,1)S(1)}, u32[]{:S(2)}, u32[]{:S(2)}) collective-permute-start(bf16[4,55,16,128]{3,2,1,0:T(8,128)(2,1)S(1)} %all-to-all-done.1.m0), channel_id=1, source_target_pairs={{0,16},{1,3},{2,18},{3,5},{4,20},{5,7},{6,22},{7,1},{16,8},{17,19}... | collective-permute-start | bytes 2703368 | tf_op jit(solution)/shard_map/ppermute | solution.py:346
  52.4 30.9 %collective-permute-start.6 = (bf16[4,55,16,128]{3,2,1,0:T(8,128)(2,1)S(1)}, bf16[4,55,16,128]{3,2,1,0:T(8,128)(2,1)S(1)}, u32[]{:S(2)}, u32[]{:S(2)}) collective-permute-start(bf16[4,55,16,128]{3,2,1,0:T(8,128)(2,1)S(1)} %all-to-all-done.1.m0), channel_id=1, source_target_pairs={{0,24},{1,7},{2,26},{3,1},{4,28},{5,3},{6,30},{7,5},{16,0},{17,23}... | collective-permute-start | bytes 2703368 | tf_op jit(solution)/shard_map/ppermute | solution.py:347
  54.4 3.7 %copy-start.1 = (s32[512]{0:T(512)S(1)}, s32[512]{0:T(512)}, u32[]{:S(2)}) copy-start(s32[512]{0:T(512)} %matching_ref.1) | copy-start | bytes 6148
  54.4 26.5 %collective-permute-start.5 = (bf16[2,55,16,128]{3,2,1,0:T(8,128)(2,1)S(1)}, bf16[2,55,16,128]{3,2,1,0:T(8,128)(2,1)S(1)}, u32[]{:S(2)}, u32[]{:S(2)}) collective-permute-start(bf16[2,55,16,128]{3,2,1,0:T(8,128)(2,1)S(1)} %slice.6), channel_id=1, source_target_pairs={{0,8},{1,5},{2,10},{3,7},{4,12},{5,1},{6,14},{7,3},{16,24},{17,21}... | collective-permute-start | bytes 1351688 | tf_op jit(solution)/shard_map/ppermute | solution.py:348
  62.6 22.7 %collective-permute-start.7 = (bf16[2,55,16,128]{3,2,1,0:T(8,128)(2,1)S(1)}, bf16[2,55,16,128]{3,2,1,0:T(8,128)(2,1)S(1)}, u32[]{:S(2)}, u32[]{:S(2)}) collective-permute-start(bf16[2,55,16,128]{3,2,1,0:T(8,128)(2,1)S(1)} %slice.7), channel_id=1, source_target_pairs={{0,16},{1,3},{2,18},{3,5},{4,20},{5,7},{6,22},{7,1},{16,8},{17,19}... | collective-permute-start | bytes 1351688 | tf_op jit(solution)/shard_map/ppermute | solution.py:367
  66.7 21.7 %collective-permute-start.8 = (bf16[4,55,16,128]{3,2,1,0:T(8,128)(2,1)S(1)}, bf16[4,55,16,128]{3,2,1,0:T(8,128)(2,1)S(1)}, u32[]{:S(2)}, u32[]{:S(2)}) collective-permute-start(bf16[4,55,16,128]{3,2,1,0:T(8,128)(2,1)S(1)} %all-to-all-done.1.m0), channel_id=1, source_target_pairs={{0,1},{1,0},{2,3},{3,2},{4,5},{5,4},{6,7},{7,6},{16,17},{17,16},{1... | collective-permute-start | bytes 2703368 | tf_op jit(solution)/shard_map/ppermute | solution.py:364
  78.9 9.5 %collective-permute-start.12 = (bf16[4096,128]{1,0:T(8,128)(2,1)S(1)}, bf16[4096,128]{1,0:T(8,128)(2,1)S(1)}, u32[]{:S(2)}, u32[]{:S(2)}) collective-permute-start(bf16[4096,128]{1,0:T(8,128)(2,1)S(1)} %constant_dynamic-update-slice_fusion.near_ref), channel_id=1, source_target_pairs={{0,1},{1,0},{2,3},{3,2},{4,5},{5,4},{6,7},{7,6},{16,17},{17,16},{1... | collective-permute-start | bytes 3145736 | tf_op jit(solution)/shard_map/ppermute | solution.py:365
  80.9 7.6 %collective-permute-start.9 = (bf16[4,55,16,128]{3,2,1,0:T(8,128)(2,1)S(1)}, bf16[4,55,16,128]{3,2,1,0:T(8,128)(2,1)S(1)}, u32[]{:S(2)}, u32[]{:S(2)}) collective-permute-start(bf16[4,55,16,128]{3,2,1,0:T(8,128)(2,1)S(1)} %collective-permute-done.4.m1), channel_id=1, source_target_pairs={{0,1},{1,0},{2,3},{3,2},{4,5},{5,4},{6,7},{7,6},{16,17},{17,16},{1... | collective-permute-start | bytes 2703368 | tf_op jit(solution)/shard_map/ppermute | solution.py:369
  83.3 5.1 %collective-permute-start.10 = (bf16[4,55,16,128]{3,2,1,0:T(8,128)(2,1)S(1)}, bf16[4,55,16,128]{3,2,1,0:T(8,128)(2,1)S(1)}, u32[]{:S(2)}, u32[]{:S(2)}) collective-permute-start(bf16[4,55,16,128]{3,2,1,0:T(8,128)(2,1)S(1)} %collective-permute-done.6.m2), channel_id=1, source_target_pairs={{0,1},{1,0},{2,3},{3,2},{4,5},{5,4},{6,7},{7,6},{16,17},{17,16},{1... | collective-permute-start | bytes 2703368 | tf_op jit(solution)/shard_map/ppermute | solution.py:370
  85.4 4.5 %collective-permute-start.11 = (bf16[4,55,16,128]{3,2,1,0:T(8,128)(2,1)S(1)}, bf16[4,55,16,128]{3,2,1,0:T(8,128)(2,1)S(1)}, u32[]{:S(2)}, u32[]{:S(2)}) collective-permute-start(bf16[4,55,16,128]{3,2,1,0:T(8,128)(2,1)S(1)} %constant_dynamic-update-slice_fusion.5.m3), channel_id=1, source_target_pairs={{0,1},{1,0},{2,3},{3,2},{4,5},{5,4},{6,7},{7,6},{16,17},{17,16},{1... | collective-permute-start | bytes 2703368 | tf_op jit(solution)/shard_map/ppermute | solution.py:372

commit v4 on v3

--- a/solution.py
+++ b/solution.py
@@ -308,13 +308,6 @@
 
 def shards(trainer_flat, matching, prefix_kv, prefix_blocks, inputs):
     bf16, f32 = jnp.bfloat16, jnp.float32
-    core = lax.axis_index("sample") % 2
-    by_place = matching.reshape(16, 2, 2, 4, 2)
-    half0 = by_place[..., 0].transpose(2, 1, 3, 0).reshape(1, 256)
-    half1 = by_place[..., 1].transpose(3, 2, 1, 0).reshape(1, 256)
-    places = jnp.where(
-        core == 0, jnp.concatenate([half0, half1], 1), jnp.concatenate([half1, half0], 1)
-    )
     x = inputs[:, 0]
     prefix = prefix_kv[0]
     pair = lax.concatenate([prefix, lax.ppermute(prefix, AXES, Y_FAR)], 0)
@@ -345,7 +338,7 @@
     lines, core_keys = lax.optimization_barrier((lines, core_keys))
     low = lax.ppermute(lines, AXES, RING_UP)
     high = lax.ppermute(lines, AXES, RING_DOWN)
-    end1 = lax.ppermute(lines[2:], AXES, RING_FAR)
+    ends = lax.ppermute(lines, AXES, RING_FAR)
     x, _ = lax.optimization_barrier((inputs[:, 0], lines))
     gathered, places, out_rows = pl.pallas_call(
         pick_kernel,
@@ -363,12 +356,8 @@
     swapped, core_keys, _ = lax.optimization_barrier((lines, core_keys, gathered))
     other_lines = lax.ppermute(swapped, AXES, CORE_SWAP)
     other_keys = lax.ppermute(core_keys, AXES, CORE_SWAP)
-    low, gathered = lax.optimization_barrier((low, gathered))
-    end0 = lax.ppermute(low[:2], AXES, RING_UP)
-    low, end1 = lax.optimization_barrier((low, end1))
     other_low = lax.ppermute(low, AXES, CORE_SWAP)
     other_high = lax.ppermute(high, AXES, CORE_SWAP)
-    ends = lax.concatenate([end0, end1], 0)
     other_ends = lax.ppermute(ends, AXES, CORE_SWAP)
     mine = [lines, low, high, ends]
     other = [other_lines, other_low, other_high, other_ends]

time: 97.8 us -> 94.7 us (0.968)
  the two profiles are of different devices: /device:TPU:13 before, /device:TPU:1 now
where the time goes in v4:
time: 94.7 us; the launch traced here: 94 us
  starting transfers between devices  66 us (70%)
  waiting for transfers between devices  15.2 us (16%)
  Pallas kernels  11.7 us (12%)
    all_to_all x1, starting transfers between devices, shards(): lax.all_to_all(formed, AXES, 0, 0, tiled=True, axis_index_groups=Z_GROUPS)  15.9 us
    ppermute x1, waiting for transfers between devices, shards(): across = lax.ppermute(behind, AXES, X_OUT)  7.93 us
    ppermute x1, starting transfers between devices, shards(): other_keys = lax.ppermute(core_keys, AXES, CORE_SWAP)  7.7 us
    pallas_call x1, Pallas kernels, shards(): pl.pallas_call(tail_kernel, out_shape=jax.ShapeDtypeStruct(x.shape, bf16)...  7.32 us
    ppermute x1, starting transfers between devices, shards(): other_high = lax.ppermute(high, AXES, CORE_SWAP)  6.64 us
    ppermute x1, starting transfers between devices, shards(): high = lax.ppermute(lines, AXES, RING_DOWN)  5.27 us
    ppermute x1, starting transfers between devices, shards(): pair = lax.concatenate([prefix, lax.ppermute(prefix, AXES, Y_FAR)], 0)  4.82 us
    ppermute x1, starting transfers between devices, shards(): across = lax.ppermute(behind, AXES, X_OUT)  4.57 us
  transfers between devices with their start and end apart: 14, of which 4 were waited for; matrix products, arithmetic and copies ran while one was open for 0% of the time, Pallas kernels for 3%

profile of v4, /device:TPU:1, one launch (start us, length us, event | category | flops | bytes accessed | tf_op | source)
XLA Modules:
  0.0 94.0 jit_solution(5432339029988359621)
XLA Ops:
  0.0 1.6 %form.1 = bf16[16,56,128]{2,1,0:T(8,128)(2,1)} custom-call(s32[512]{0:T(512)} %matching_ref.1, bf16[1,6480]{1,0:T(2,128)(2,1)} %tile_ref.1), custom_call_target="tpu_custom_call" | custom-call | tf_op jit(solution)/shard_map/form/pallas_call | solution.py:319
  1.6 15.9 %all-to-all-start = ((bf16[16,56,128]{2,1,0:T(8,128)(2,1)}), bf16[16,56,128]{2,1,0:T(8,128)(2,1)S(1)}, u32[]{:S(2)}, u32[]{:S(2)}) async-start(bf16[16,56,128]{2,1,0:T(8,128)(2,1)} %form.1), calls=%async_computation | async-start | bytes 458752 | tf_op jit(solution)/shard_map/all_to_all | solution.py:327
  17.4 4.8 %collective-permute-start = (bf16[512,128]{1,0:T(8,128)(2,1)S(1)}, bf16[512,128]{1,0:T(8,128)(2,1)S(1)}, u32[]{:S(2)}, u32[]{:S(2)}) collective-permute-start(bf16[512,128]{1,0:T(8,128)(2,1)S(1)} %bitcast.9), channel_id=1, source_target_pairs={{0,8},{1,9},{2,10},{3,11},{4,12},{5,13},{6,14},{7,15},{16,24},{17,... | collective-permute-start | bytes 393224 | tf_op jit(solution)/shard_map/ppermute | solution.py:313
  22.3 2.7 %collective-permute-done = bf16[512,128]{1,0:T(8,128)(2,1)S(1)} collective-permute-done((bf16[512,128]{1,0:T(8,128)(2,1)S(1)}, bf16[512,128]{1,0:T(8,128)(2,1)S(1)}, u32[]{:S(2)}, u32[]{:S(2)}) %collective-permute-start) | collective-permute-done | bytes 131104 | tf_op jit(solution)/shard_map/ppermute | solution.py:313
  25.0 4.4 %collective-permute-start.1 = (bf16[1024,128]{1,0:T(8,128)(2,1)S(1)}, bf16[1024,128]{1,0:T(8,128)(2,1)S(1)}, u32[]{:S(2)}, u32[]{:S(2)}) collective-permute-start(bf16[1024,128]{1,0:T(8,128)(2,1)S(1)} %pad_maximum_fusion), channel_id=1, source_target_pairs={{0,2},{1,7},{2,4},{3,1},{4,6},{5,3},{6,0},{7,5},{16,18},{17,23},{1... | collective-permute-start | bytes 786440 | tf_op jit(solution)/shard_map/ppermute | solution.py:314
  29.4 1.9 %collective-permute-start.2 = (bf16[1024,128]{1,0:T(8,128)(2,1)S(1)}, bf16[1024,128]{1,0:T(8,128)(2,1)S(1)}, u32[]{:S(2)}, u32[]{:S(2)}) collective-permute-start(bf16[1024,128]{1,0:T(8,128)(2,1)S(1)} %pad_maximum_fusion), channel_id=1, source_target_pairs={{0,6},{1,3},{2,0},{3,5},{4,2},{5,7},{6,4},{7,1},{16,22},{17,19},{1... | collective-permute-start | bytes 786440 | tf_op jit(solution)/shard_map/ppermute | solution.py:315
  31.3 1.0 %merge.1 = bf16[4,55,16,128]{3,2,1,0:T(8,128)(2,1)} custom-call(bf16[16,56,128]{2,1,0:T(8,128)(2,1)S(1)} %all-to-all-done.in_ref), custom_call_target="tpu_custom_call" | custom-call | tf_op jit(solution)/shard_map/merge/pallas_call | solution.py:328
  32.4 4.2 %all-to-all-start.1 = ((bf16[4,55,16,128]{3,2,1,0:T(8,128)(2,1)}), bf16[4,55,16,128]{3,2,1,0:T(8,128)(2,1)S(1)}, u32[]{:S(2)}, u32[]{:S(2)}) async-start(bf16[4,55,16,128]{3,2,1,0:T(8,128)(2,1)} %merge.1), calls=%async_computation.1 | async-start | bytes 1802240 | tf_op jit(solution)/shard_map/all_to_all | solution.py:337
  36.6 4.6 %collective-permute-start.3 = (bf16[1024,128]{1,0:T(8,128)(2,1)S(1)}, bf16[1024,128]{1,0:T(8,128)(2,1)S(1)}, u32[]{:S(2)}, u32[]{:S(2)}) collective-permute-start(bf16[1024,128]{1,0:T(8,128)(2,1)S(1)} %collective-permute-done.1), channel_id=1, source_target_pairs={{0,2},{1,7},{2,4},{3,1},{4,6},{5,3},{6,0},{7,5},{16,18},{17,23},{1... | collective-permute-start | bytes 786440 | tf_op jit(solution)/shard_map/ppermute | solution.py:316
  41.3 0.0 copy-start
  41.3 7.9 %collective-permute-done.3 = bf16[1024,128]{1,0:T(8,128)(2,1)S(1)} collective-permute-done((bf16[1024,128]{1,0:T(8,128)(2,1)S(1)}, bf16[1024,128]{1,0:T(8,128)(2,1)S(1)}, u32[]{:S(2)}, u32[]{:S(2)}) %collective-permute-start.3) | collective-permute-done | bytes 262176 | tf_op jit(solution)/shard_map/ppermute | solution.py:316
  49.3 0.0 copy-start.1
  49.3 1.9 %collective-permute-start.6 = (bf16[4,55,16,128]{3,2,1,0:T(8,128)(2,1)S(1)}, bf16[4,55,16,128]{3,2,1,0:T(8,128)(2,1)S(1)}, u32[]{:S(2)}, u32[]{:S(2)}) collective-permute-start(bf16[4,55,16,128]{3,2,1,0:T(8,128)(2,1)S(1)} %all-to-all-done.1.m0), channel_id=1, source_target_pairs={{0,8},{1,5},{2,10},{3,7},{4,12},{5,1},{6,14},{7,3},{16,24},{17,21}... | collective-permute-start | bytes 2703368 | tf_op jit(solution)/shard_map/ppermute | solution.py:341
  51.2 5.3 %collective-permute-start.5 = (bf16[4,55,16,128]{3,2,1,0:T(8,128)(2,1)S(1)}, bf16[4,55,16,128]{3,2,1,0:T(8,128)(2,1)S(1)}, u32[]{:S(2)}, u32[]{:S(2)}) collective-permute-start(bf16[4,55,16,128]{3,2,1,0:T(8,128)(2,1)S(1)} %all-to-all-done.1.m0), channel_id=1, source_target_pairs={{0,24},{1,7},{2,26},{3,1},{4,28},{5,3},{6,30},{7,5},{16,0},{17,23}... | collective-permute-start | bytes 2703368 | tf_op jit(solution)/shard_map/ppermute | solution.py:340
  56.5 2.5 %collective-permute-start.4 = (bf16[4,55,16,128]{3,2,1,0:T(8,128)(2,1)S(1)}, bf16[4,55,16,128]{3,2,1,0:T(8,128)(2,1)S(1)}, u32[]{:S(2)}, u32[]{:S(2)}) collective-permute-start(bf16[4,55,16,128]{3,2,1,0:T(8,128)(2,1)S(1)} %all-to-all-done.1.m0), channel_id=1, source_target_pairs={{0,16},{1,3},{2,18},{3,5},{4,20},{5,7},{6,22},{7,1},{16,8},{17,19}... | collective-permute-start | bytes 2703368 | tf_op jit(solution)/shard_map/ppermute | solution.py:339
  59.0 1.8 %pick.1 = (bf16[352,512]{1,0:T(8,128)(2,1)S(1)}, s32[1,512]{1,0:T(1,128)S(1)}, bf16[512,512]{1,0:T(8,128)(2,1)S(1)}) custom-call(bf16[4,8,2880]{2,1,0:T(8,128)(2,1)S(1)} %bitcast.7, s32[1,512]{1,0:T(1,128)S(1)} %bitcast.8), custom_call_target="tpu_custom_call" | custom-call | tf_op jit(solution)/shard_map/pick/pallas_call | solution.py:343
  60.8 7.7 %collective-permute-start.11 = (bf16[4096,128]{1,0:T(8,128)(2,1)S(1)}, bf16[4096,128]{1,0:T(8,128)(2,1)S(1)}, u32[]{:S(2)}, u32[]{:S(2)}) collective-permute-start(bf16[4096,128]{1,0:T(8,128)(2,1)S(1)} %constant_dynamic-update-slice_fusion.near_ref), channel_id=1, source_target_pairs={{0,1},{1,0},{2,3},{3,2},{4,5},{5,4},{6,7},{7,6},{16,17},{17,16},{1... | collective-permute-start | bytes 3145736 | tf_op jit(solution)/shard_map/ppermute | solution.py:358
  68.5 1.9 %collective-permute-start.7 = (bf16[4,55,16,128]{3,2,1,0:T(8,128)(2,1)S(1)}, bf16[4,55,16,128]{3,2,1,0:T(8,128)(2,1)S(1)}, u32[]{:S(2)}, u32[]{:S(2)}) collective-permute-start(bf16[4,55,16,128]{3,2,1,0:T(8,128)(2,1)S(1)} %all-to-all-done.1.m0), channel_id=1, source_target_pairs={{0,1},{1,0},{2,3},{3,2},{4,5},{5,4},{6,7},{7,6},{16,17},{17,16},{1... | collective-permute-start | bytes 2703368 | tf_op jit(solution)/shard_map/ppermute | solution.py:357
  70.5 2.4 %collective-permute-start.10 = (bf16[4,55,16,128]{3,2,1,0:T(8,128)(2,1)S(1)}, bf16[4,55,16,128]{3,2,1,0:T(8,128)(2,1)S(1)}, u32[]{:S(2)}, u32[]{:S(2)}) collective-permute-start(bf16[4,55,16,128]{3,2,1,0:T(8,128)(2,1)S(1)} %collective-permute-done.6.m3), channel_id=1, source_target_pairs={{0,1},{1,0},{2,3},{3,2},{4,5},{5,4},{6,7},{7,6},{16,17},{17,16},{1... | collective-permute-start | bytes 2703368 | tf_op jit(solution)/shard_map/ppermute | solution.py:361
  72.9 2.8 %collective-permute-done.5.m2 = bf16[4,55,16,128]{3,2,1,0:T(8,128)(2,1)S(1)} collective-permute-done((bf16[4,55,16,128]{3,2,1,0:T(8,128)(2,1)S(1)}, bf16[4,55,16,128]{3,2,1,0:T(8,128)(2,1)S(1)}, u32[]{:S(2)}, u32[]{:S(2)}) %collective-permute-start.5) | collective-permute-done | bytes 901152 | tf_op jit(solution)/shard_map/ppermute | solution.py:340
  75.7 6.6 %collective-permute-start.9 = (bf16[4,55,16,128]{3,2,1,0:T(8,128)(2,1)S(1)}, bf16[4,55,16,128]{3,2,1,0:T(8,128)(2,1)S(1)}, u32[]{:S(2)}, u32[]{:S(2)}) collective-permute-start(bf16[4,55,16,128]{3,2,1,0:T(8,128)(2,1)S(1)} %collective-permute-done.5.m2), channel_id=1, source_target_pairs={{0,1},{1,0},{2,3},{3,2},{4,5},{5,4},{6,7},{7,6},{16,17},{17,16},{1... | collective-permute-start | bytes 2703368 | tf_op jit(solution)/shard_map/ppermute | solution.py:360
  82.4 1.9 %collective-permute-start.8 = (bf16[4,55,16,128]{3,2,1,0:T(8,128)(2,1)S(1)}, bf16[4,55,16,128]{3,2,1,0:T(8,128)(2,1)S(1)}, u32[]{:S(2)}, u32[]{:S(2)}) collective-permute-start(bf16[4,55,16,128]{3,2,1,0:T(8,128)(2,1)S(1)} %collective-permute-done.4.m1), channel_id=1, source_target_pairs={{0,1},{1,0},{2,3},{3,2},{4,5},{5,4},{6,7},{7,6},{16,17},{17,16},{1... | collective-permute-start | bytes 2703368 | tf_op jit(solution)/shard_map/ppermute | solution.py:359
  85.0 1.7 %collective-permute-done.8.o1 = bf16[4,55,16,128]{3,2,1,0:T(8,128)(2,1)S(1)} collective-permute-done((bf16[4,55,16,128]{3,2,1,0:T(8,128)(2,1)S(1)}, bf16[4,55,16,128]{3,2,1,0:T(8,128)(2,1)S(1)}, u32[]{:S(2)}, u32[]{:S(2)}) %collective-permute-start.8) | collective-permute-done | bytes 901152 | tf_op jit(solution)/shard_map/ppermute | solution.py:359
  86.7 7.3 %tail.1 = bf16[4,8,2880]{2,1,0:T(8,128)(2,1)} custom-call(s32[1]{0:T(128)S(6)} %copy.11.limit_ref, bf16[352,512]{1,0:T(8,128)(2,1)S(1)} %get-tuple-element.15.xg_ref, s32[1,512]{1,0:T(1,128)S(1)} %get-tuple-element.16.place_ref, bf16[512,512]{1,0:T(8,128)(2,1)S(1)} %get-tuple-element.17.row_ref, bf16[4,55,16,128]{3,2,1,0:T(8,128)(2,1)S(1)} %all-to-all-done.1.m0, ...), custom_call_target="tpu_custom_call" | custom-call | tf_op jit(solution)/shard_map/tail/pallas_call | solution.py:364
  (20 shorter events, 0.2 us)
Async XLA Ops:
  1.6 15.9 %copy-start.2 = (bf16[1,512,128]{2,1,0:T(8,128)(2,1)S(1)}, bf16[1,512,128]{2,1,0:T(8,128)(2,1)}, u32[]{:S(2)}) copy-start(bf16[1,512,128]{2,1,0:T(8,128)(2,1)} %param.7) | copy-start | bytes 393220
  1.6 29.8 %all-to-all-start = ((bf16[16,56,128]{2,1,0:T(8,128)(2,1)}), bf16[16,56,128]{2,1,0:T(8,128)(2,1)S(1)}, u32[]{:S(2)}, u32[]{:S(2)}) async-start(bf16[16,56,128]{2,1,0:T(8,128)(2,1)} %form.1), calls=%async_computation | async-start | bytes 458752 | tf_op jit(solution)/shard_map/all_to_all | solution.py:327
  17.4 7.5 %collective-permute-start = (bf16[512,128]{1,0:T(8,128)(2,1)S(1)}, bf16[512,128]{1,0:T(8,128)(2,1)S(1)}, u32[]{:S(2)}, u32[]{:S(2)}) collective-permute-start(bf16[512,128]{1,0:T(8,128)(2,1)S(1)} %bitcast.9), channel_id=1, source_target_pairs={{0,8},{1,9},{2,10},{3,11},{4,12},{5,13},{6,14},{7,15},{16,24},{17,... | collective-permute-start | bytes 393224 | tf_op jit(solution)/shard_map/ppermute | solution.py:313
  25.0 11.6 %collective-permute-start.1 = (bf16[1024,128]{1,0:T(8,128)(2,1)S(1)}, bf16[1024,128]{1,0:T(8,128)(2,1)S(1)}, u32[]{:S(2)}, u32[]{:S(2)}) collective-permute-start(bf16[1024,128]{1,0:T(8,128)(2,1)S(1)} %pad_maximum_fusion), channel_id=1, source_target_pairs={{0,2},{1,7},{2,4},{3,1},{4,6},{5,3},{6,0},{7,5},{16,18},{17,23},{1... | collective-permute-start | bytes 786440 | tf_op jit(solution)/shard_map/ppermute | solution.py:314
  29.4 11.8 %collective-permute-start.2 = (bf16[1024,128]{1,0:T(8,128)(2,1)S(1)}, bf16[1024,128]{1,0:T(8,128)(2,1)S(1)}, u32[]{:S(2)}, u32[]{:S(2)}) collective-permute-start(bf16[1024,128]{1,0:T(8,128)(2,1)S(1)} %pad_maximum_fusion), channel_id=1, source_target_pairs={{0,6},{1,3},{2,0},{3,5},{4,2},{5,7},{6,4},{7,1},{16,22},{17,19},{1... | collective-permute-start | bytes 786440 | tf_op jit(solution)/shard_map/ppermute | solution.py:315
  32.4 16.9 %all-to-all-start.1 = ((bf16[4,55,16,128]{3,2,1,0:T(8,128)(2,1)}), bf16[4,55,16,128]{3,2,1,0:T(8,128)(2,1)S(1)}, u32[]{:S(2)}, u32[]{:S(2)}) async-start(bf16[4,55,16,128]{3,2,1,0:T(8,128)(2,1)} %merge.1), calls=%async_computation.1 | async-start | bytes 1802240 | tf_op jit(solution)/shard_map/all_to_all | solution.py:337
  36.6 12.7 %collective-permute-start.3 = (bf16[1024,128]{1,0:T(8,128)(2,1)S(1)}, bf16[1024,128]{1,0:T(8,128)(2,1)S(1)}, u32[]{:S(2)}, u32[]{:S(2)}) collective-permute-start(bf16[1024,128]{1,0:T(8,128)(2,1)S(1)} %collective-permute-done.1), channel_id=1, source_target_pairs={{0,2},{1,7},{2,4},{3,1},{4,6},{5,3},{6,0},{7,5},{16,18},{17,23},{1... | collective-permute-start | bytes 786440 | tf_op jit(solution)/shard_map/ppermute | solution.py:316
  41.3 17.7 %copy-start = (bf16[4,1,8,2880]{3,2,1,0:T(8,128)(2,1)S(1)}, bf16[4,1,8,2880]{3,2,1,0:T(8,128)(2,1)}, u32[]{:S(2)}) copy-start(bf16[4,1,8,2880]{3,2,1,0:T(8,128)(2,1)} %param.9) | copy-start | bytes 552964
  49.3 9.7 %copy-start.1 = (s32[512]{0:T(512)S(1)}, s32[512]{0:T(512)}, u32[]{:S(2)}) copy-start(s32[512]{0:T(512)} %matching_ref.1) | copy-start | bytes 6148
  49.3 21.2 %collective-permute-start.6 = (bf16[4,55,16,128]{3,2,1,0:T(8,128)(2,1)S(1)}, bf16[4,55,16,128]{3,2,1,0:T(8,128)(2,1)S(1)}, u32[]{:S(2)}, u32[]{:S(2)}) collective-permute-start(bf16[4,55,16,128]{3,2,1,0:T(8,128)(2,1)S(1)} %all-to-all-done.1.m0), channel_id=1, source_target_pairs={{0,8},{1,5},{2,10},{3,7},{4,12},{5,1},{6,14},{7,3},{16,24},{17,21}... | collective-permute-start | bytes 2703368 | tf_op jit(solution)/shard_map/ppermute | solution.py:341
  51.2 24.5 %collective-permute-start.5 = (bf16[4,55,16,128]{3,2,1,0:T(8,128)(2,1)S(1)}, bf16[4,55,16,128]{3,2,1,0:T(8,128)(2,1)S(1)}, u32[]{:S(2)}, u32[]{:S(2)}) collective-permute-start(bf16[4,55,16,128]{3,2,1,0:T(8,128)(2,1)S(1)} %all-to-all-done.1.m0), channel_id=1, source_target_pairs={{0,24},{1,7},{2,26},{3,1},{4,28},{5,3},{6,30},{7,5},{16,0},{17,23}... | collective-permute-start | bytes 2703368 | tf_op jit(solution)/shard_map/ppermute | solution.py:340
  56.5 25.9 %collective-permute-start.4 = (bf16[4,55,16,128]{3,2,1,0:T(8,128)(2,1)S(1)}, bf16[4,55,16,128]{3,2,1,0:T(8,128)(2,1)S(1)}, u32[]{:S(2)}, u32[]{:S(2)}) collective-permute-start(bf16[4,55,16,128]{3,2,1,0:T(8,128)(2,1)S(1)} %all-to-all-done.1.m0), channel_id=1, source_target_pairs={{0,16},{1,3},{2,18},{3,5},{4,20},{5,7},{6,22},{7,1},{16,8},{17,19}... | collective-permute-start | bytes 2703368 | tf_op jit(solution)/shard_map/ppermute | solution.py:339
  60.8 24.2 %collective-permute-start.11 = (bf16[4096,128]{1,0:T(8,128)(2,1)S(1)}, bf16[4096,128]{1,0:T(8,128)(2,1)S(1)}, u32[]{:S(2)}, u32[]{:S(2)}) collective-permute-start(bf16[4096,128]{1,0:T(8,128)(2,1)S(1)} %constant_dynamic-update-slice_fusion.near_ref), channel_id=1, source_target_pairs={{0,1},{1,0},{2,3},{3,2},{4,5},{5,4},{6,7},{7,6},{16,17},{17,16},{1... | collective-permute-start | bytes 3145736 | tf_op jit(solution)/shard_map/ppermute | solution.py:358
  68.5 16.4 %collective-permute-start.7 = (bf16[4,55,16,128]{3,2,1,0:T(8,128)(2,1)S(1)}, bf16[4,55,16,128]{3,2,1,0:T(8,128)(2,1)S(1)}, u32[]{:S(2)}, u32[]{:S(2)}) collective-permute-start(bf16[4,55,16,128]{3,2,1,0:T(8,128)(2,1)S(1)} %all-to-all-done.1.m0), channel_id=1, source_target_pairs={{0,1},{1,0},{2,3},{3,2},{4,5},{5,4},{6,7},{7,6},{16,17},{17,16},{1... | collective-permute-start | bytes 2703368 | tf_op jit(solution)/shard_map/ppermute | solution.py:357
  70.5 14.5 %collective-permute-start.10 = (bf16[4,55,16,128]{3,2,1,0:T(8,128)(2,1)S(1)}, bf16[4,55,16,128]{3,2,1,0:T(8,128)(2,1)S(1)}, u32[]{:S(2)}, u32[]{:S(2)}) collective-permute-start(bf16[4,55,16,128]{3,2,1,0:T(8,128)(2,1)S(1)} %collective-permute-done.6.m3), channel_id=1, source_target_pairs={{0,1},{1,0},{2,3},{3,2},{4,5},{5,4},{6,7},{7,6},{16,17},{17,16},{1... | collective-permute-start | bytes 2703368 | tf_op jit(solution)/shard_map/ppermute | solution.py:361
  75.7 9.3 %collective-permute-start.9 = (bf16[4,55,16,128]{3,2,1,0:T(8,128)(2,1)S(1)}, bf16[4,55,16,128]{3,2,1,0:T(8,128)(2,1)S(1)}, u32[]{:S(2)}, u32[]{:S(2)}) collective-permute-start(bf16[4,55,16,128]{3,2,1,0:T(8,128)(2,1)S(1)} %collective-permute-done.5.m2), channel_id=1, source_target_pairs={{0,1},{1,0},{2,3},{3,2},{4,5},{5,4},{6,7},{7,6},{16,17},{17,16},{1... | collective-permute-start | bytes 2703368 | tf_op jit(solution)/shard_map/ppermute | solution.py:360
  82.4 4.3 %collective-permute-start.8 = (bf16[4,55,16,128]{3,2,1,0:T(8,128)(2,1)S(1)}, bf16[4,55,16,128]{3,2,1,0:T(8,128)(2,1)S(1)}, u32[]{:S(2)}, u32[]{:S(2)}) collective-permute-start(bf16[4,55,16,128]{3,2,1,0:T(8,128)(2,1)S(1)} %collective-permute-done.4.m1), channel_id=1, source_target_pairs={{0,1},{1,0},{2,3},{3,2},{4,5},{5,4},{6,7},{7,6},{16,17},{17,16},{1... | collective-permute-start | bytes 2703368 | tf_op jit(solution)/shard_map/ppermute | solution.py:359

commit v5 on v4

--- a/solution.py
+++ b/solution.py
@@ -124,7 +124,7 @@
 
 
 def ring_offset(piece):
-    return jnp.where(piece == 0, 0, jnp.where(piece == 1, 3, piece - 1))
+    return jnp.where(piece == 0, 0, jnp.where(piece == 3, 1, piece + 1))
 
 
 def slot_places(matching_row):
@@ -171,14 +171,15 @@
     xg_ref[...] = total.astype(jnp.bfloat16)
 
 
-def project(xg_ref, halves):
+def project(xg_ref, halves, first):
     blocks = []
     for cols in ((0, 1), (2, 3), (4,)):
         total = None
         for half in range(2):
+            slots = slice(256 * half + first, 256 * half + first + 128)
             for i in range(11):
                 term = jnp.dot(
-                    xg_ref[ROWS * i : ROWS * i + ROWS, 256 * half : 256 * half + 256],
+                    xg_ref[ROWS * i : ROWS * i + ROWS, slots],
                     read_weights(halves[half], [5 * i + b for b in cols]),
                     preferred_element_type=jnp.float32,
                 )
@@ -187,16 +188,20 @@
     return jnp.concatenate(blocks, 1)
 
 
+def early_kernel(xg_ref, m0, m1, o0, o1, out_ref):
+    out_ref[...] = project(xg_ref, ((m0, m1), (o0, o1)), 0)
+
+
 CHUNK = 1024
 SHARD = 512
 
 
 def tail_kernel(
-    limit_ref, xg_ref, place_ref, row_ref, m0, m1, m2, m3, o0, o1, o2, o3, near_ref, far_ref, out_ref,
+    limit_ref, part_ref, xg_ref, place_ref, row_ref, m0, m1, m2, m3, o0, o1, o2, o3, near_ref, far_ref, out_ref,
     s_ref, w_ref, og_ref, acc_ref,
 ):
     halves = ((m0, m1, m2, m3), (o0, o1, o2, o3))
-    projected = project(xg_ref, halves)
+    projected = part_ref[...] + project(xg_ref, ((m2, m3), (o2, o3)), 128)
     y0, x0, core0 = chip_place()
     rounded = projected.astype(jnp.bfloat16)
     own_kv = rounded[:, 512:640]
@@ -357,14 +362,22 @@
     other_lines = lax.ppermute(swapped, AXES, CORE_SWAP)
     other_keys = lax.ppermute(core_keys, AXES, CORE_SWAP)
     other_low = lax.ppermute(low, AXES, CORE_SWAP)
+    other_ends = lax.ppermute(ends, AXES, CORE_SWAP)
+    part = pl.pallas_call(
+        early_kernel,
+        out_shape=jax.ShapeDtypeStruct((ROWS, 640), f32),
+        in_specs=[VMEM] * 5,
+        out_specs=VMEM,
+        compiler_params=pltpu.CompilerParams(vmem_limit_bytes=8 * MIB),
+        name="early",
+    )(gathered, lines, ends, other_lines, other_ends)
     other_high = lax.ppermute(high, AXES, CORE_SWAP)
-    other_ends = lax.ppermute(ends, AXES, CORE_SWAP)
-    mine = [lines, low, high, ends]
-    other = [other_lines, other_low, other_high, other_ends]
+    mine = [lines, ends, low, high]
+    other = [other_lines, other_ends, other_low, other_high]
     output = pl.pallas_call(
         tail_kernel,
         out_shape=jax.ShapeDtypeStruct(x.shape, bf16),
-        in_specs=[SMEM] + [VMEM] * 13,
+        in_specs=[SMEM] + [VMEM] * 14,
         out_specs=VMEM,
         scratch_shapes=[
             pltpu.VMEM((QHEADS * ROWS, 16 * SHARD), f32),
@@ -374,7 +387,7 @@
         ],
         compiler_params=pltpu.CompilerParams(vmem_limit_bytes=20 * MIB),
         name="tail",
-    )(prefix_blocks, gathered, places, out_rows, *mine, *other, core_keys, other_keys)
+    )(prefix_blocks, part, gathered, places, out_rows, *mine, *other, core_keys, other_keys)
     return output[:, None]
 
 

time: 94.7 us -> 94.8 us (level)
  transfers between devices with their start and end apart: 14 -> 14, of which waited for: 4 -> 4; matrix products, arithmetic and copies ran while one was open for 0% -> 0% of each run, Pallas kernels for 3% -> 4%
where the time goes in v5:
time: 94.8 us; the launch traced here: 94.1 us
  starting transfers between devices  66 us (70%)
  waiting for transfers between devices  14.5 us (15%)
  Pallas kernels  12.5 us (13%)
    all_to_all x1, starting transfers between devices, shards(): lax.all_to_all(formed, AXES, 0, 0, tiled=True, axis_index_groups=Z_GROUPS)  15.9 us
    ppermute x1, waiting for transfers between devices, shards(): across = lax.ppermute(behind, AXES, X_OUT)  7.93 us
    ppermute x1, starting transfers between devices, shards(): other_keys = lax.ppermute(core_keys, AXES, CORE_SWAP)  7.7 us
    pallas_call x1, Pallas kernels, shards(): pl.pallas_call(tail_kernel, out_shape=jax.ShapeDtypeStruct(x.shape, bf16)...  7.42 us
    ppermute x1, starting transfers between devices, shards(): other_high = lax.ppermute(high, AXES, CORE_SWAP)  6.64 us
    ppermute x1, starting transfers between devices, shards(): high = lax.ppermute(lines, AXES, RING_DOWN)  5.27 us
    ppermute x1, starting transfers between devices, shards(): pair = lax.concatenate([prefix, lax.ppermute(prefix, AXES, Y_FAR)], 0)  4.82 us
    ppermute x1, starting transfers between devices, shards(): across = lax.ppermute(behind, AXES, X_OUT)  4.57 us
  transfers between devices with their start and end apart: 14, of which 4 were waited for; matrix products, arithmetic and copies ran while one was open for 0% of the time, Pallas kernels for 4%

profile of v5, /device:TPU:1, one launch (start us, length us, event | category | flops | bytes accessed | tf_op | source)
XLA Modules:
  0.0 94.1 jit_solution(17387045283151806111)
XLA Ops:
  0.0 1.6 %form.1 = bf16[16,56,128]{2,1,0:T(8,128)(2,1)} custom-call(s32[512]{0:T(512)} %matching_ref.1, bf16[1,6480]{1,0:T(2,128)(2,1)} %tile_ref.1), custom_call_target="tpu_custom_call" | custom-call | tf_op jit(solution)/shard_map/form/pallas_call | solution.py:324
  1.6 15.9 %all-to-all-start = ((bf16[16,56,128]{2,1,0:T(8,128)(2,1)}), bf16[16,56,128]{2,1,0:T(8,128)(2,1)S(1)}, u32[]{:S(2)}, u32[]{:S(2)}) async-start(bf16[16,56,128]{2,1,0:T(8,128)(2,1)} %form.1), calls=%async_computation | async-start | bytes 458752 | tf_op jit(solution)/shard_map/all_to_all | solution.py:332
  17.4 4.8 %collective-permute-start = (bf16[512,128]{1,0:T(8,128)(2,1)S(1)}, bf16[512,128]{1,0:T(8,128)(2,1)S(1)}, u32[]{:S(2)}, u32[]{:S(2)}) collective-permute-start(bf16[512,128]{1,0:T(8,128)(2,1)S(1)} %bitcast.9), channel_id=1, source_target_pairs={{0,8},{1,9},{2,10},{3,11},{4,12},{5,13},{6,14},{7,15},{16,24},{17,... | collective-permute-start | bytes 393224 | tf_op jit(solution)/shard_map/ppermute | solution.py:318
  22.3 2.7 %collective-permute-done = bf16[512,128]{1,0:T(8,128)(2,1)S(1)} collective-permute-done((bf16[512,128]{1,0:T(8,128)(2,1)S(1)}, bf16[512,128]{1,0:T(8,128)(2,1)S(1)}, u32[]{:S(2)}, u32[]{:S(2)}) %collective-permute-start) | collective-permute-done | bytes 131104 | tf_op jit(solution)/shard_map/ppermute | solution.py:318
  25.0 4.4 %collective-permute-start.1 = (bf16[1024,128]{1,0:T(8,128)(2,1)S(1)}, bf16[1024,128]{1,0:T(8,128)(2,1)S(1)}, u32[]{:S(2)}, u32[]{:S(2)}) collective-permute-start(bf16[1024,128]{1,0:T(8,128)(2,1)S(1)} %pad_maximum_fusion), channel_id=1, source_target_pairs={{0,2},{1,7},{2,4},{3,1},{4,6},{5,3},{6,0},{7,5},{16,18},{17,23},{1... | collective-permute-start | bytes 786440 | tf_op jit(solution)/shard_map/ppermute | solution.py:319
  29.4 1.9 %collective-permute-start.2 = (bf16[1024,128]{1,0:T(8,128)(2,1)S(1)}, bf16[1024,128]{1,0:T(8,128)(2,1)S(1)}, u32[]{:S(2)}, u32[]{:S(2)}) collective-permute-start(bf16[1024,128]{1,0:T(8,128)(2,1)S(1)} %pad_maximum_fusion), channel_id=1, source_target_pairs={{0,6},{1,3},{2,0},{3,5},{4,2},{5,7},{6,4},{7,1},{16,22},{17,19},{1... | collective-permute-start | bytes 786440 | tf_op jit(solution)/shard_map/ppermute | solution.py:320
  31.3 1.0 %merge.1 = bf16[4,55,16,128]{3,2,1,0:T(8,128)(2,1)} custom-call(bf16[16,56,128]{2,1,0:T(8,128)(2,1)S(1)} %all-to-all-done.in_ref), custom_call_target="tpu_custom_call" | custom-call | tf_op jit(solution)/shard_map/merge/pallas_call | solution.py:333
  32.4 4.2 %all-to-all-start.1 = ((bf16[4,55,16,128]{3,2,1,0:T(8,128)(2,1)}), bf16[4,55,16,128]{3,2,1,0:T(8,128)(2,1)S(1)}, u32[]{:S(2)}, u32[]{:S(2)}) async-start(bf16[4,55,16,128]{3,2,1,0:T(8,128)(2,1)} %merge.1), calls=%async_computation.1 | async-start | bytes 1802240 | tf_op jit(solution)/shard_map/all_to_all | solution.py:342
  36.6 4.6 %collective-permute-start.3 = (bf16[1024,128]{1,0:T(8,128)(2,1)S(1)}, bf16[1024,128]{1,0:T(8,128)(2,1)S(1)}, u32[]{:S(2)}, u32[]{:S(2)}) collective-permute-start(bf16[1024,128]{1,0:T(8,128)(2,1)S(1)} %collective-permute-done.1), channel_id=1, source_target_pairs={{0,2},{1,7},{2,4},{3,1},{4,6},{5,3},{6,0},{7,5},{16,18},{17,23},{1... | collective-permute-start | bytes 786440 | tf_op jit(solution)/shard_map/ppermute | solution.py:321
  41.3 7.9 %collective-permute-done.3 = bf16[1024,128]{1,0:T(8,128)(2,1)S(1)} collective-permute-done((bf16[1024,128]{1,0:T(8,128)(2,1)S(1)}, bf16[1024,128]{1,0:T(8,128)(2,1)S(1)}, u32[]{:S(2)}, u32[]{:S(2)}) %collective-permute-start.3) | collective-permute-done | bytes 262176 | tf_op jit(solution)/shard_map/ppermute | solution.py:321
  49.3 1.9 %collective-permute-start.4 = (bf16[4,55,16,128]{3,2,1,0:T(8,128)(2,1)S(1)}, bf16[4,55,16,128]{3,2,1,0:T(8,128)(2,1)S(1)}, u32[]{:S(2)}, u32[]{:S(2)}) collective-permute-start(bf16[4,55,16,128]{3,2,1,0:T(8,128)(2,1)S(1)} %all-to-all-done.1.m0), channel_id=1, source_target_pairs={{0,8},{1,5},{2,10},{3,7},{4,12},{5,1},{6,14},{7,3},{16,24},{17,21}... | collective-permute-start | bytes 2703368 | tf_op jit(solution)/shard_map/ppermute | solution.py:346
  51.2 5.3 %collective-permute-start.8 = (bf16[4,55,16,128]{3,2,1,0:T(8,128)(2,1)S(1)}, bf16[4,55,16,128]{3,2,1,0:T(8,128)(2,1)S(1)}, u32[]{:S(2)}, u32[]{:S(2)}) collective-permute-start(bf16[4,55,16,128]{3,2,1,0:T(8,128)(2,1)S(1)} %all-to-all-done.1.m0), channel_id=1, source_target_pairs={{0,24},{1,7},{2,26},{3,1},{4,28},{5,3},{6,30},{7,5},{16,0},{17,23}... | collective-permute-start | bytes 2703368 | tf_op jit(solution)/shard_map/ppermute | solution.py:345
  56.5 2.5 %collective-permute-start.7 = (bf16[4,55,16,128]{3,2,1,0:T(8,128)(2,1)S(1)}, bf16[4,55,16,128]{3,2,1,0:T(8,128)(2,1)S(1)}, u32[]{:S(2)}, u32[]{:S(2)}) collective-permute-start(bf16[4,55,16,128]{3,2,1,0:T(8,128)(2,1)S(1)} %all-to-all-done.1.m0), channel_id=1, source_target_pairs={{0,16},{1,3},{2,18},{3,5},{4,20},{5,7},{6,22},{7,1},{16,8},{17,19}... | collective-permute-start | bytes 2703368 | tf_op jit(solution)/shard_map/ppermute | solution.py:344
  59.0 1.8 %pick.1 = (bf16[352,512]{1,0:T(8,128)(2,1)S(1)}, s32[1,512]{1,0:T(1,128)S(1)}, bf16[512,512]{1,0:T(8,128)(2,1)S(1)}) custom-call(bf16[4,8,2880]{2,1,0:T(8,128)(2,1)S(1)} %bitcast.7, s32[1,512]{1,0:T(1,128)S(1)} %bitcast.8), custom_call_target="tpu_custom_call" | custom-call | tf_op jit(solution)/shard_map/pick/pallas_call | solution.py:348
  60.8 7.7 %collective-permute-start.11 = (bf16[4096,128]{1,0:T(8,128)(2,1)S(1)}, bf16[4096,128]{1,0:T(8,128)(2,1)S(1)}, u32[]{:S(2)}, u32[]{:S(2)}) collective-permute-start(bf16[4096,128]{1,0:T(8,128)(2,1)S(1)} %constant_dynamic-update-slice_fusion.near_ref), channel_id=1, source_target_pairs={{0,1},{1,0},{2,3},{3,2},{4,5},{5,4},{6,7},{7,6},{16,17},{17,16},{1... | collective-permute-start | bytes 3145736 | tf_op jit(solution)/shard_map/ppermute | solution.py:363
  68.5 1.9 %collective-permute-start.5 = (bf16[4,55,16,128]{3,2,1,0:T(8,128)(2,1)S(1)}, bf16[4,55,16,128]{3,2,1,0:T(8,128)(2,1)S(1)}, u32[]{:S(2)}, u32[]{:S(2)}) collective-permute-start(bf16[4,55,16,128]{3,2,1,0:T(8,128)(2,1)S(1)} %all-to-all-done.1.m0), channel_id=1, source_target_pairs={{0,1},{1,0},{2,3},{3,2},{4,5},{5,4},{6,7},{7,6},{16,17},{17,16},{1... | collective-permute-start | bytes 2703368 | tf_op jit(solution)/shard_map/ppermute | solution.py:362
  70.5 2.4 %collective-permute-start.6 = (bf16[4,55,16,128]{3,2,1,0:T(8,128)(2,1)S(1)}, bf16[4,55,16,128]{3,2,1,0:T(8,128)(2,1)S(1)}, u32[]{:S(2)}, u32[]{:S(2)}) collective-permute-start(bf16[4,55,16,128]{3,2,1,0:T(8,128)(2,1)S(1)} %collective-permute-done.4.m1), channel_id=1, source_target_pairs={{0,1},{1,0},{2,3},{3,2},{4,5},{5,4},{6,7},{7,6},{16,17},{17,16},{1... | collective-permute-start | bytes 2703368 | tf_op jit(solution)/shard_map/ppermute | solution.py:365
  72.9 2.8 %collective-permute-done.8.m3 = bf16[4,55,16,128]{3,2,1,0:T(8,128)(2,1)S(1)} collective-permute-done((bf16[4,55,16,128]{3,2,1,0:T(8,128)(2,1)S(1)}, bf16[4,55,16,128]{3,2,1,0:T(8,128)(2,1)S(1)}, u32[]{:S(2)}, u32[]{:S(2)}) %collective-permute-start.8) | collective-permute-done | bytes 901152 | tf_op jit(solution)/shard_map/ppermute | solution.py:345
  75.7 6.6 %collective-permute-start.10 = (bf16[4,55,16,128]{3,2,1,0:T(8,128)(2,1)S(1)}, bf16[4,55,16,128]{3,2,1,0:T(8,128)(2,1)S(1)}, u32[]{:S(2)}, u32[]{:S(2)}) collective-permute-start(bf16[4,55,16,128]{3,2,1,0:T(8,128)(2,1)S(1)} %collective-permute-done.8.m3), channel_id=1, source_target_pairs={{0,1},{1,0},{2,3},{3,2},{4,5},{5,4},{6,7},{7,6},{16,17},{17,16},{1... | collective-permute-start | bytes 2703368 | tf_op jit(solution)/shard_map/ppermute | solution.py:374
  82.4 1.9 %collective-permute-start.9 = (bf16[4,55,16,128]{3,2,1,0:T(8,128)(2,1)S(1)}, bf16[4,55,16,128]{3,2,1,0:T(8,128)(2,1)S(1)}, u32[]{:S(2)}, u32[]{:S(2)}) collective-permute-start(bf16[4,55,16,128]{3,2,1,0:T(8,128)(2,1)S(1)} %collective-permute-done.7.m2), channel_id=1, source_target_pairs={{0,1},{1,0},{2,3},{3,2},{4,5},{5,4},{6,7},{7,6},{16,17},{17,16},{1... | collective-permute-start | bytes 2703368 | tf_op jit(solution)/shard_map/ppermute | solution.py:364
  85.0 0.7 early.1.part_ref
  85.7 0.0 collective-permute-done.10.o3
  85.7 1.0 %collective-permute-done.9.o2 = bf16[4,55,16,128]{3,2,1,0:T(8,128)(2,1)S(1)} collective-permute-done((bf16[4,55,16,128]{3,2,1,0:T(8,128)(2,1)S(1)}, bf16[4,55,16,128]{3,2,1,0:T(8,128)(2,1)S(1)}, u32[]{:S(2)}, u32[]{:S(2)}) %collective-permute-start.9) | collective-permute-done | bytes 901152 | tf_op jit(solution)/shard_map/ppermute | solution.py:364
  86.7 7.4 %tail.1 = bf16[4,8,2880]{2,1,0:T(8,128)(2,1)} custom-call(s32[1]{0:T(128)S(6)} %copy.11.limit_ref, f32[32,640]{1,0:T(8,128)S(1)} %early.1.part_ref, bf16[352,512]{1,0:T(8,128)(2,1)S(1)} %get-tuple-element.15.xg_ref, s32[1,512]{1,0:T(1,128)S(1)} %get-tuple-element.18.place_ref, bf16[512,512]{1,0:T(8,128)(2,1)S(1)} %get-tuple-element.19.row_ref, ...), custom_call_target="tpu_custom_call" | custom-call | tf_op jit(solution)/shard_map/tail/pallas_call | solution.py:377
  (21 shorter events, 0.2 us)
Async XLA Ops:
  1.6 15.9 %copy-start.2 = (bf16[1,512,128]{2,1,0:T(8,128)(2,1)S(1)}, bf16[1,512,128]{2,1,0:T(8,128)(2,1)}, u32[]{:S(2)}) copy-start(bf16[1,512,128]{2,1,0:T(8,128)(2,1)} %param.7) | copy-start | bytes 393220
  1.6 29.8 %all-to-all-start = ((bf16[16,56,128]{2,1,0:T(8,128)(2,1)}), bf16[16,56,128]{2,1,0:T(8,128)(2,1)S(1)}, u32[]{:S(2)}, u32[]{:S(2)}) async-start(bf16[16,56,128]{2,1,0:T(8,128)(2,1)} %form.1), calls=%async_computation | async-start | bytes 458752 | tf_op jit(solution)/shard_map/all_to_all | solution.py:332
  17.4 7.5 %collective-permute-start = (bf16[512,128]{1,0:T(8,128)(2,1)S(1)}, bf16[512,128]{1,0:T(8,128)(2,1)S(1)}, u32[]{:S(2)}, u32[]{:S(2)}) collective-permute-start(bf16[512,128]{1,0:T(8,128)(2,1)S(1)} %bitcast.9), channel_id=1, source_target_pairs={{0,8},{1,9},{2,10},{3,11},{4,12},{5,13},{6,14},{7,15},{16,24},{17,... | collective-permute-start | bytes 393224 | tf_op jit(solution)/shard_map/ppermute | solution.py:318
  25.0 11.6 %collective-permute-start.1 = (bf16[1024,128]{1,0:T(8,128)(2,1)S(1)}, bf16[1024,128]{1,0:T(8,128)(2,1)S(1)}, u32[]{:S(2)}, u32[]{:S(2)}) collective-permute-start(bf16[1024,128]{1,0:T(8,128)(2,1)S(1)} %pad_maximum_fusion), channel_id=1, source_target_pairs={{0,2},{1,7},{2,4},{3,1},{4,6},{5,3},{6,0},{7,5},{16,18},{17,23},{1... | collective-permute-start | bytes 786440 | tf_op jit(solution)/shard_map/ppermute | solution.py:319
  29.4 11.8 %collective-permute-start.2 = (bf16[1024,128]{1,0:T(8,128)(2,1)S(1)}, bf16[1024,128]{1,0:T(8,128)(2,1)S(1)}, u32[]{:S(2)}, u32[]{:S(2)}) collective-permute-start(bf16[1024,128]{1,0:T(8,128)(2,1)S(1)} %pad_maximum_fusion), channel_id=1, source_target_pairs={{0,6},{1,3},{2,0},{3,5},{4,2},{5,7},{6,4},{7,1},{16,22},{17,19},{1... | collective-permute-start | bytes 786440 | tf_op jit(solution)/shard_map/ppermute | solution.py:320
  32.4 16.9 %all-to-all-start.1 = ((bf16[4,55,16,128]{3,2,1,0:T(8,128)(2,1)}), bf16[4,55,16,128]{3,2,1,0:T(8,128)(2,1)S(1)}, u32[]{:S(2)}, u32[]{:S(2)}) async-start(bf16[4,55,16,128]{3,2,1,0:T(8,128)(2,1)} %merge.1), calls=%async_computation.1 | async-start | bytes 1802240 | tf_op jit(solution)/shard_map/all_to_all | solution.py:342
  36.6 12.7 %collective-permute-start.3 = (bf16[1024,128]{1,0:T(8,128)(2,1)S(1)}, bf16[1024,128]{1,0:T(8,128)(2,1)S(1)}, u32[]{:S(2)}, u32[]{:S(2)}) collective-permute-start(bf16[1024,128]{1,0:T(8,128)(2,1)S(1)} %collective-permute-done.1), channel_id=1, source_target_pairs={{0,2},{1,7},{2,4},{3,1},{4,6},{5,3},{6,0},{7,5},{16,18},{17,23},{1... | collective-permute-start | bytes 786440 | tf_op jit(solution)/shard_map/ppermute | solution.py:321
  41.3 17.7 %copy-start = (bf16[4,1,8,2880]{3,2,1,0:T(8,128)(2,1)S(1)}, bf16[4,1,8,2880]{3,2,1,0:T(8,128)(2,1)}, u32[]{:S(2)}) copy-start(bf16[4,1,8,2880]{3,2,1,0:T(8,128)(2,1)} %param.9) | copy-start | bytes 552964
  49.3 9.7 %copy-start.1 = (s32[512]{0:T(512)S(1)}, s32[512]{0:T(512)}, u32[]{:S(2)}) copy-start(s32[512]{0:T(512)} %matching_ref.1) | copy-start | bytes 6148
  49.3 21.2 %collective-permute-start.4 = (bf16[4,55,16,128]{3,2,1,0:T(8,128)(2,1)S(1)}, bf16[4,55,16,128]{3,2,1,0:T(8,128)(2,1)S(1)}, u32[]{:S(2)}, u32[]{:S(2)}) collective-permute-start(bf16[4,55,16,128]{3,2,1,0:T(8,128)(2,1)S(1)} %all-to-all-done.1.m0), channel_id=1, source_target_pairs={{0,8},{1,5},{2,10},{3,7},{4,12},{5,1},{6,14},{7,3},{16,24},{17,21}... | collective-permute-start | bytes 2703368 | tf_op jit(solution)/shard_map/ppermute | solution.py:346
  51.2 24.5 %collective-permute-start.8 = (bf16[4,55,16,128]{3,2,1,0:T(8,128)(2,1)S(1)}, bf16[4,55,16,128]{3,2,1,0:T(8,128)(2,1)S(1)}, u32[]{:S(2)}, u32[]{:S(2)}) collective-permute-start(bf16[4,55,16,128]{3,2,1,0:T(8,128)(2,1)S(1)} %all-to-all-done.1.m0), channel_id=1, source_target_pairs={{0,24},{1,7},{2,26},{3,1},{4,28},{5,3},{6,30},{7,5},{16,0},{17,23}... | collective-permute-start | bytes 2703368 | tf_op jit(solution)/shard_map/ppermute | solution.py:345
  56.5 25.9 %collective-permute-start.7 = (bf16[4,55,16,128]{3,2,1,0:T(8,128)(2,1)S(1)}, bf16[4,55,16,128]{3,2,1,0:T(8,128)(2,1)S(1)}, u32[]{:S(2)}, u32[]{:S(2)}) collective-permute-start(bf16[4,55,16,128]{3,2,1,0:T(8,128)(2,1)S(1)} %all-to-all-done.1.m0), channel_id=1, source_target_pairs={{0,16},{1,3},{2,18},{3,5},{4,20},{5,7},{6,22},{7,1},{16,8},{17,19}... | collective-permute-start | bytes 2703368 | tf_op jit(solution)/shard_map/ppermute | solution.py:344
  60.8 24.9 %collective-permute-start.11 = (bf16[4096,128]{1,0:T(8,128)(2,1)S(1)}, bf16[4096,128]{1,0:T(8,128)(2,1)S(1)}, u32[]{:S(2)}, u32[]{:S(2)}) collective-permute-start(bf16[4096,128]{1,0:T(8,128)(2,1)S(1)} %constant_dynamic-update-slice_fusion.near_ref), channel_id=1, source_target_pairs={{0,1},{1,0},{2,3},{3,2},{4,5},{5,4},{6,7},{7,6},{16,17},{17,16},{1... | collective-permute-start | bytes 3145736 | tf_op jit(solution)/shard_map/ppermute | solution.py:363
  68.5 16.4 %collective-permute-start.5 = (bf16[4,55,16,128]{3,2,1,0:T(8,128)(2,1)S(1)}, bf16[4,55,16,128]{3,2,1,0:T(8,128)(2,1)S(1)}, u32[]{:S(2)}, u32[]{:S(2)}) collective-permute-start(bf16[4,55,16,128]{3,2,1,0:T(8,128)(2,1)S(1)} %all-to-all-done.1.m0), channel_id=1, source_target_pairs={{0,1},{1,0},{2,3},{3,2},{4,5},{5,4},{6,7},{7,6},{16,17},{17,16},{1... | collective-permute-start | bytes 2703368 | tf_op jit(solution)/shard_map/ppermute | solution.py:362
  70.5 14.5 %collective-permute-start.6 = (bf16[4,55,16,128]{3,2,1,0:T(8,128)(2,1)S(1)}, bf16[4,55,16,128]{3,2,1,0:T(8,128)(2,1)S(1)}, u32[]{:S(2)}, u32[]{:S(2)}) collective-permute-start(bf16[4,55,16,128]{3,2,1,0:T(8,128)(2,1)S(1)} %collective-permute-done.4.m1), channel_id=1, source_target_pairs={{0,1},{1,0},{2,3},{3,2},{4,5},{5,4},{6,7},{7,6},{16,17},{17,16},{1... | collective-permute-start | bytes 2703368 | tf_op jit(solution)/shard_map/ppermute | solution.py:365
  75.7 10.0 %collective-permute-start.10 = (bf16[4,55,16,128]{3,2,1,0:T(8,128)(2,1)S(1)}, bf16[4,55,16,128]{3,2,1,0:T(8,128)(2,1)S(1)}, u32[]{:S(2)}, u32[]{:S(2)}) collective-permute-start(bf16[4,55,16,128]{3,2,1,0:T(8,128)(2,1)S(1)} %collective-permute-done.8.m3), channel_id=1, source_target_pairs={{0,1},{1,0},{2,3},{3,2},{4,5},{5,4},{6,7},{7,6},{16,17},{17,16},{1... | collective-permute-start | bytes 2703368 | tf_op jit(solution)/shard_map/ppermute | solution.py:374
  82.4 4.3 %collective-permute-start.9 = (bf16[4,55,16,128]{3,2,1,0:T(8,128)(2,1)S(1)}, bf16[4,55,16,128]{3,2,1,0:T(8,128)(2,1)S(1)}, u32[]{:S(2)}, u32[]{:S(2)}) collective-permute-start(bf16[4,55,16,128]{3,2,1,0:T(8,128)(2,1)S(1)} %collective-permute-done.7.m2), channel_id=1, source_target_pairs={{0,1},{1,0},{2,3},{3,2},{4,5},{5,4},{6,7},{7,6},{16,17},{17,16},{1... | collective-permute-start | bytes 2703368 | tf_op jit(solution)/shard_map/ppermute | solution.py:364

commit v6 on v5

--- a/solution.py
+++ b/solution.py
@@ -171,16 +171,15 @@
     xg_ref[...] = total.astype(jnp.bfloat16)
 
 
-def project(xg_ref, halves, first):
+def project(xg_ref, groups):
     blocks = []
     for cols in ((0, 1), (2, 3), (4,)):
         total = None
-        for half in range(2):
-            slots = slice(256 * half + first, 256 * half + first + 128)
+        for refs, slots in groups:
             for i in range(11):
                 term = jnp.dot(
                     xg_ref[ROWS * i : ROWS * i + ROWS, slots],
-                    read_weights(halves[half], [5 * i + b for b in cols]),
+                    read_weights(refs, [5 * i + b for b in cols]),
                     preferred_element_type=jnp.float32,
                 )
                 total = term if total is None else total + term
@@ -188,8 +187,9 @@
     return jnp.concatenate(blocks, 1)
 
 
-def early_kernel(xg_ref, m0, m1, o0, o1, out_ref):
-    out_ref[...] = project(xg_ref, ((m0, m1), (o0, o1)), 0)
+def early_kernel(xg_ref, m0, m1, m2, m3, o0, o1, out_ref):
+    groups = (((m0, m1, m2, m3), slice(0, 256)), ((o0, o1), slice(256, 384)))
+    out_ref[...] = project(xg_ref, groups)
 
 
 CHUNK = 1024
@@ -201,7 +201,7 @@
     s_ref, w_ref, og_ref, acc_ref,
 ):
     halves = ((m0, m1, m2, m3), (o0, o1, o2, o3))
-    projected = part_ref[...] + project(xg_ref, ((m2, m3), (o2, o3)), 128)
+    projected = part_ref[...] + project(xg_ref, (((o2, o3), slice(384, 512)),))
     y0, x0, core0 = chip_place()
     rounded = projected.astype(jnp.bfloat16)
     own_kv = rounded[:, 512:640]
@@ -366,11 +366,11 @@
     part = pl.pallas_call(
         early_kernel,
         out_shape=jax.ShapeDtypeStruct((ROWS, 640), f32),
-        in_specs=[VMEM] * 5,
+        in_specs=[VMEM] * 7,
         out_specs=VMEM,
         compiler_params=pltpu.CompilerParams(vmem_limit_bytes=8 * MIB),
         name="early",
-    )(gathered, lines, ends, other_lines, other_ends)
+    )(gathered, lines, ends, low, high, other_lines, other_ends)
     other_high = lax.ppermute(high, AXES, CORE_SWAP)
     mine = [lines, ends, low, high]
     other = [other_lines, other_ends, other_low, other_high]

time: 94.8 us -> 93.9 us (level)
  no operation moved by 1% of the time
where the time goes in v6:
time: 93.9 us; the launch traced here: 93.2 us
  starting transfers between devices  66 us (70%)
  waiting for transfers between devices  14.2 us (15%)
  Pallas kernels  11.8 us (13%)
    all_to_all x1, starting transfers between devices, shards(): lax.all_to_all(formed, AXES, 0, 0, tiled=True, axis_index_groups=Z_GROUPS)  15.9 us
    ppermute x1, waiting for transfers between devices, shards(): across = lax.ppermute(behind, AXES, X_OUT)  7.93 us
    ppermute x1, starting transfers between devices, shards(): other_keys = lax.ppermute(core_keys, AXES, CORE_SWAP)  7.7 us
    ppermute x1, starting transfers between devices, shards(): other_high = lax.ppermute(high, AXES, CORE_SWAP)  6.64 us
    pallas_call x1, Pallas kernels, shards(): pl.pallas_call(tail_kernel, out_shape=jax.ShapeDtypeStruct(x.shape, bf16)...  6.49 us
    ppermute x1, starting transfers between devices, shards(): high = lax.ppermute(lines, AXES, RING_DOWN)  5.27 us
    ppermute x1, starting transfers between devices, shards(): pair = lax.concatenate([prefix, lax.ppermute(prefix, AXES, Y_FAR)], 0)  4.82 us
    ppermute x1, starting transfers between devices, shards(): across = lax.ppermute(behind, AXES, X_OUT)  4.57 us
  transfers between devices with their start and end apart: 14, of which 4 were waited for; matrix products, arithmetic and copies ran while one was open for 0% of the time, Pallas kernels for 4%

profile of v6, /device:TPU:1, one launch (start us, length us, event | category | flops | bytes accessed | tf_op | source)
XLA Modules:
  0.0 93.2 jit_solution(1693383086547651642)
XLA Ops:
  0.0 1.6 %form.1 = bf16[16,56,128]{2,1,0:T(8,128)(2,1)} custom-call(s32[512]{0:T(512)} %matching_ref.1, bf16[1,6480]{1,0:T(2,128)(2,1)} %tile_ref.1), custom_call_target="tpu_custom_call" | custom-call | tf_op jit(solution)/shard_map/form/pallas_call | solution.py:324
  1.6 15.9 %all-to-all-start = ((bf16[16,56,128]{2,1,0:T(8,128)(2,1)}), bf16[16,56,128]{2,1,0:T(8,128)(2,1)S(1)}, u32[]{:S(2)}, u32[]{:S(2)}) async-start(bf16[16,56,128]{2,1,0:T(8,128)(2,1)} %form.1), calls=%async_computation | async-start | bytes 458752 | tf_op jit(solution)/shard_map/all_to_all | solution.py:332
  17.4 4.8 %collective-permute-start = (bf16[512,128]{1,0:T(8,128)(2,1)S(1)}, bf16[512,128]{1,0:T(8,128)(2,1)S(1)}, u32[]{:S(2)}, u32[]{:S(2)}) collective-permute-start(bf16[512,128]{1,0:T(8,128)(2,1)S(1)} %bitcast.9), channel_id=1, source_target_pairs={{0,8},{1,9},{2,10},{3,11},{4,12},{5,13},{6,14},{7,15},{16,24},{17,... | collective-permute-start | bytes 393224 | tf_op jit(solution)/shard_map/ppermute | solution.py:318
  22.3 2.7 %collective-permute-done = bf16[512,128]{1,0:T(8,128)(2,1)S(1)} collective-permute-done((bf16[512,128]{1,0:T(8,128)(2,1)S(1)}, bf16[512,128]{1,0:T(8,128)(2,1)S(1)}, u32[]{:S(2)}, u32[]{:S(2)}) %collective-permute-start) | collective-permute-done | bytes 131104 | tf_op jit(solution)/shard_map/ppermute | solution.py:318
  25.0 4.4 %collective-permute-start.1 = (bf16[1024,128]{1,0:T(8,128)(2,1)S(1)}, bf16[1024,128]{1,0:T(8,128)(2,1)S(1)}, u32[]{:S(2)}, u32[]{:S(2)}) collective-permute-start(bf16[1024,128]{1,0:T(8,128)(2,1)S(1)} %pad_maximum_fusion), channel_id=1, source_target_pairs={{0,2},{1,7},{2,4},{3,1},{4,6},{5,3},{6,0},{7,5},{16,18},{17,23},{1... | collective-permute-start | bytes 786440 | tf_op jit(solution)/shard_map/ppermute | solution.py:319
  29.4 1.9 %collective-permute-start.2 = (bf16[1024,128]{1,0:T(8,128)(2,1)S(1)}, bf16[1024,128]{1,0:T(8,128)(2,1)S(1)}, u32[]{:S(2)}, u32[]{:S(2)}) collective-permute-start(bf16[1024,128]{1,0:T(8,128)(2,1)S(1)} %pad_maximum_fusion), channel_id=1, source_target_pairs={{0,6},{1,3},{2,0},{3,5},{4,2},{5,7},{6,4},{7,1},{16,22},{17,19},{1... | collective-permute-start | bytes 786440 | tf_op jit(solution)/shard_map/ppermute | solution.py:320
  31.3 1.0 %merge.1 = bf16[4,55,16,128]{3,2,1,0:T(8,128)(2,1)} custom-call(bf16[16,56,128]{2,1,0:T(8,128)(2,1)S(1)} %all-to-all-done.in_ref), custom_call_target="tpu_custom_call" | custom-call | tf_op jit(solution)/shard_map/merge/pallas_call | solution.py:333
  32.4 4.2 %all-to-all-start.1 = ((bf16[4,55,16,128]{3,2,1,0:T(8,128)(2,1)}), bf16[4,55,16,128]{3,2,1,0:T(8,128)(2,1)S(1)}, u32[]{:S(2)}, u32[]{:S(2)}) async-start(bf16[4,55,16,128]{3,2,1,0:T(8,128)(2,1)} %merge.1), calls=%async_computation.1 | async-start | bytes 1802240 | tf_op jit(solution)/shard_map/all_to_all | solution.py:342
  36.6 4.6 %collective-permute-start.3 = (bf16[1024,128]{1,0:T(8,128)(2,1)S(1)}, bf16[1024,128]{1,0:T(8,128)(2,1)S(1)}, u32[]{:S(2)}, u32[]{:S(2)}) collective-permute-start(bf16[1024,128]{1,0:T(8,128)(2,1)S(1)} %collective-permute-done.1), channel_id=1, source_target_pairs={{0,2},{1,7},{2,4},{3,1},{4,6},{5,3},{6,0},{7,5},{16,18},{17,23},{1... | collective-permute-start | bytes 786440 | tf_op jit(solution)/shard_map/ppermute | solution.py:321
  41.3 7.9 %collective-permute-done.3 = bf16[1024,128]{1,0:T(8,128)(2,1)S(1)} collective-permute-done((bf16[1024,128]{1,0:T(8,128)(2,1)S(1)}, bf16[1024,128]{1,0:T(8,128)(2,1)S(1)}, u32[]{:S(2)}, u32[]{:S(2)}) %collective-permute-start.3) | collective-permute-done | bytes 262176 | tf_op jit(solution)/shard_map/ppermute | solution.py:321
  49.3 0.0 copy-start.1
  49.3 1.9 %collective-permute-start.4 = (bf16[4,55,16,128]{3,2,1,0:T(8,128)(2,1)S(1)}, bf16[4,55,16,128]{3,2,1,0:T(8,128)(2,1)S(1)}, u32[]{:S(2)}, u32[]{:S(2)}) collective-permute-start(bf16[4,55,16,128]{3,2,1,0:T(8,128)(2,1)S(1)} %all-to-all-done.1.m0), channel_id=1, source_target_pairs={{0,8},{1,5},{2,10},{3,7},{4,12},{5,1},{6,14},{7,3},{16,24},{17,21}... | collective-permute-start | bytes 2703368 | tf_op jit(solution)/shard_map/ppermute | solution.py:346
  51.2 5.3 %collective-permute-start.6 = (bf16[4,55,16,128]{3,2,1,0:T(8,128)(2,1)S(1)}, bf16[4,55,16,128]{3,2,1,0:T(8,128)(2,1)S(1)}, u32[]{:S(2)}, u32[]{:S(2)}) collective-permute-start(bf16[4,55,16,128]{3,2,1,0:T(8,128)(2,1)S(1)} %all-to-all-done.1.m0), channel_id=1, source_target_pairs={{0,24},{1,7},{2,26},{3,1},{4,28},{5,3},{6,30},{7,5},{16,0},{17,23}... | collective-permute-start | bytes 2703368 | tf_op jit(solution)/shard_map/ppermute | solution.py:345
  56.5 2.5 %collective-permute-start.5 = (bf16[4,55,16,128]{3,2,1,0:T(8,128)(2,1)S(1)}, bf16[4,55,16,128]{3,2,1,0:T(8,128)(2,1)S(1)}, u32[]{:S(2)}, u32[]{:S(2)}) collective-permute-start(bf16[4,55,16,128]{3,2,1,0:T(8,128)(2,1)S(1)} %all-to-all-done.1.m0), channel_id=1, source_target_pairs={{0,16},{1,3},{2,18},{3,5},{4,20},{5,7},{6,22},{7,1},{16,8},{17,19}... | collective-permute-start | bytes 2703368 | tf_op jit(solution)/shard_map/ppermute | solution.py:344
  59.0 1.8 %pick.1 = (bf16[352,512]{1,0:T(8,128)(2,1)S(1)}, s32[1,512]{1,0:T(1,128)S(1)}, bf16[512,512]{1,0:T(8,128)(2,1)S(1)}) custom-call(bf16[4,8,2880]{2,1,0:T(8,128)(2,1)S(1)} %bitcast.7, s32[1,512]{1,0:T(1,128)S(1)} %bitcast.8), custom_call_target="tpu_custom_call" | custom-call | tf_op jit(solution)/shard_map/pick/pallas_call | solution.py:348
  60.8 7.7 %collective-permute-start.11 = (bf16[4096,128]{1,0:T(8,128)(2,1)S(1)}, bf16[4096,128]{1,0:T(8,128)(2,1)S(1)}, u32[]{:S(2)}, u32[]{:S(2)}) collective-permute-start(bf16[4096,128]{1,0:T(8,128)(2,1)S(1)} %constant_dynamic-update-slice_fusion.near_ref), channel_id=1, source_target_pairs={{0,1},{1,0},{2,3},{3,2},{4,5},{5,4},{6,7},{7,6},{16,17},{17,16},{1... | collective-permute-start | bytes 3145736 | tf_op jit(solution)/shard_map/ppermute | solution.py:363
  68.5 1.9 %collective-permute-start.7 = (bf16[4,55,16,128]{3,2,1,0:T(8,128)(2,1)S(1)}, bf16[4,55,16,128]{3,2,1,0:T(8,128)(2,1)S(1)}, u32[]{:S(2)}, u32[]{:S(2)}) collective-permute-start(bf16[4,55,16,128]{3,2,1,0:T(8,128)(2,1)S(1)} %all-to-all-done.1.m0), channel_id=1, source_target_pairs={{0,1},{1,0},{2,3},{3,2},{4,5},{5,4},{6,7},{7,6},{16,17},{17,16},{1... | collective-permute-start | bytes 2703368 | tf_op jit(solution)/shard_map/ppermute | solution.py:362
  70.5 2.4 %collective-permute-start.8 = (bf16[4,55,16,128]{3,2,1,0:T(8,128)(2,1)S(1)}, bf16[4,55,16,128]{3,2,1,0:T(8,128)(2,1)S(1)}, u32[]{:S(2)}, u32[]{:S(2)}) collective-permute-start(bf16[4,55,16,128]{3,2,1,0:T(8,128)(2,1)S(1)} %collective-permute-done.4.m1), channel_id=1, source_target_pairs={{0,1},{1,0},{2,3},{3,2},{4,5},{5,4},{6,7},{7,6},{16,17},{17,16},{1... | collective-permute-start | bytes 2703368 | tf_op jit(solution)/shard_map/ppermute | solution.py:365
  72.9 2.8 %collective-permute-done.6.m3 = bf16[4,55,16,128]{3,2,1,0:T(8,128)(2,1)S(1)} collective-permute-done((bf16[4,55,16,128]{3,2,1,0:T(8,128)(2,1)S(1)}, bf16[4,55,16,128]{3,2,1,0:T(8,128)(2,1)S(1)}, u32[]{:S(2)}, u32[]{:S(2)}) %collective-permute-start.6) | collective-permute-done | bytes 901152 | tf_op jit(solution)/shard_map/ppermute | solution.py:345
  75.7 6.6 %collective-permute-start.10 = (bf16[4,55,16,128]{3,2,1,0:T(8,128)(2,1)S(1)}, bf16[4,55,16,128]{3,2,1,0:T(8,128)(2,1)S(1)}, u32[]{:S(2)}, u32[]{:S(2)}) collective-permute-start(bf16[4,55,16,128]{3,2,1,0:T(8,128)(2,1)S(1)} %collective-permute-done.6.m3), channel_id=1, source_target_pairs={{0,1},{1,0},{2,3},{3,2},{4,5},{5,4},{6,7},{7,6},{16,17},{17,16},{1... | collective-permute-start | bytes 2703368 | tf_op jit(solution)/shard_map/ppermute | solution.py:374
  82.4 1.9 %collective-permute-start.9 = (bf16[4,55,16,128]{3,2,1,0:T(8,128)(2,1)S(1)}, bf16[4,55,16,128]{3,2,1,0:T(8,128)(2,1)S(1)}, u32[]{:S(2)}, u32[]{:S(2)}) collective-permute-start(bf16[4,55,16,128]{3,2,1,0:T(8,128)(2,1)S(1)} %collective-permute-done.5.m2), channel_id=1, source_target_pairs={{0,1},{1,0},{2,3},{3,2},{4,5},{5,4},{6,7},{7,6},{16,17},{17,16},{1... | collective-permute-start | bytes 2703368 | tf_op jit(solution)/shard_map/ppermute | solution.py:364
  85.0 1.0 %early.1.part_ref = f32[32,640]{1,0:T(8,128)S(1)} custom-call(bf16[352,512]{1,0:T(8,128)(2,1)S(1)} %get-tuple-element.15.xg_ref, bf16[4,55,16,128]{3,2,1,0:T(8,128)(2,1)S(1)} %all-to-all-done.1.m0, bf16[4,55,16,128]{3,2,1,0:T(8,128)(2,1)S(1)} %collective-permute-done.4.m1, bf16[4,55,16,128]{3,2,1,0:T(8,128)(2,1)S(1)} %collective-permute-done.5.m2, ...), custom_call_target="tpu_custom_call" | custom-call | tf_op jit(solution)/shard_map/early/pallas_call | solution.py:366
  86.0 0.8 collective-permute-done.9.o2
  86.7 6.5 %tail.1 = bf16[4,8,2880]{2,1,0:T(8,128)(2,1)} custom-call(s32[1]{0:T(128)S(6)} %copy.11.limit_ref, f32[32,640]{1,0:T(8,128)S(1)} %early.1.part_ref, bf16[352,512]{1,0:T(8,128)(2,1)S(1)} %get-tuple-element.15.xg_ref, s32[1,512]{1,0:T(1,128)S(1)} %get-tuple-element.18.place_ref, bf16[512,512]{1,0:T(8,128)(2,1)S(1)} %get-tuple-element.19.row_ref, ...), custom_call_target="tpu_custom_call" | custom-call | tf_op jit(solution)/shard_map/tail/pallas_call | solution.py:377
  (21 shorter events, 0.2 us)
Async XLA Ops:
  1.6 15.9 %copy-start.2 = (bf16[1,512,128]{2,1,0:T(8,128)(2,1)S(1)}, bf16[1,512,128]{2,1,0:T(8,128)(2,1)}, u32[]{:S(2)}) copy-start(bf16[1,512,128]{2,1,0:T(8,128)(2,1)} %param.7) | copy-start | bytes 393220
  1.6 29.8 %all-to-all-start = ((bf16[16,56,128]{2,1,0:T(8,128)(2,1)}), bf16[16,56,128]{2,1,0:T(8,128)(2,1)S(1)}, u32[]{:S(2)}, u32[]{:S(2)}) async-start(bf16[16,56,128]{2,1,0:T(8,128)(2,1)} %form.1), calls=%async_computation | async-start | bytes 458752 | tf_op jit(solution)/shard_map/all_to_all | solution.py:332
  17.4 7.5 %collective-permute-start = (bf16[512,128]{1,0:T(8,128)(2,1)S(1)}, bf16[512,128]{1,0:T(8,128)(2,1)S(1)}, u32[]{:S(2)}, u32[]{:S(2)}) collective-permute-start(bf16[512,128]{1,0:T(8,128)(2,1)S(1)} %bitcast.9), channel_id=1, source_target_pairs={{0,8},{1,9},{2,10},{3,11},{4,12},{5,13},{6,14},{7,15},{16,24},{17,... | collective-permute-start | bytes 393224 | tf_op jit(solution)/shard_map/ppermute | solution.py:318
  25.0 11.6 %collective-permute-start.1 = (bf16[1024,128]{1,0:T(8,128)(2,1)S(1)}, bf16[1024,128]{1,0:T(8,128)(2,1)S(1)}, u32[]{:S(2)}, u32[]{:S(2)}) collective-permute-start(bf16[1024,128]{1,0:T(8,128)(2,1)S(1)} %pad_maximum_fusion), channel_id=1, source_target_pairs={{0,2},{1,7},{2,4},{3,1},{4,6},{5,3},{6,0},{7,5},{16,18},{17,23},{1... | collective-permute-start | bytes 786440 | tf_op jit(solution)/shard_map/ppermute | solution.py:319
  29.4 11.8 %collective-permute-start.2 = (bf16[1024,128]{1,0:T(8,128)(2,1)S(1)}, bf16[1024,128]{1,0:T(8,128)(2,1)S(1)}, u32[]{:S(2)}, u32[]{:S(2)}) collective-permute-start(bf16[1024,128]{1,0:T(8,128)(2,1)S(1)} %pad_maximum_fusion), channel_id=1, source_target_pairs={{0,6},{1,3},{2,0},{3,5},{4,2},{5,7},{6,4},{7,1},{16,22},{17,19},{1... | collective-permute-start | bytes 786440 | tf_op jit(solution)/shard_map/ppermute | solution.py:320
  32.4 16.9 %all-to-all-start.1 = ((bf16[4,55,16,128]{3,2,1,0:T(8,128)(2,1)}), bf16[4,55,16,128]{3,2,1,0:T(8,128)(2,1)S(1)}, u32[]{:S(2)}, u32[]{:S(2)}) async-start(bf16[4,55,16,128]{3,2,1,0:T(8,128)(2,1)} %merge.1), calls=%async_computation.1 | async-start | bytes 1802240 | tf_op jit(solution)/shard_map/all_to_all | solution.py:342
  36.6 12.7 %collective-permute-start.3 = (bf16[1024,128]{1,0:T(8,128)(2,1)S(1)}, bf16[1024,128]{1,0:T(8,128)(2,1)S(1)}, u32[]{:S(2)}, u32[]{:S(2)}) collective-permute-start(bf16[1024,128]{1,0:T(8,128)(2,1)S(1)} %collective-permute-done.1), channel_id=1, source_target_pairs={{0,2},{1,7},{2,4},{3,1},{4,6},{5,3},{6,0},{7,5},{16,18},{17,23},{1... | collective-permute-start | bytes 786440 | tf_op jit(solution)/shard_map/ppermute | solution.py:321
  41.3 17.7 %copy-start = (bf16[4,1,8,2880]{3,2,1,0:T(8,128)(2,1)S(1)}, bf16[4,1,8,2880]{3,2,1,0:T(8,128)(2,1)}, u32[]{:S(2)}) copy-start(bf16[4,1,8,2880]{3,2,1,0:T(8,128)(2,1)} %param.9) | copy-start | bytes 552964
  49.3 9.7 %copy-start.1 = (s32[512]{0:T(512)S(1)}, s32[512]{0:T(512)}, u32[]{:S(2)}) copy-start(s32[512]{0:T(512)} %matching_ref.1) | copy-start | bytes 6148
  49.3 21.2 %collective-permute-start.4 = (bf16[4,55,16,128]{3,2,1,0:T(8,128)(2,1)S(1)}, bf16[4,55,16,128]{3,2,1,0:T(8,128)(2,1)S(1)}, u32[]{:S(2)}, u32[]{:S(2)}) collective-permute-start(bf16[4,55,16,128]{3,2,1,0:T(8,128)(2,1)S(1)} %all-to-all-done.1.m0), channel_id=1, source_target_pairs={{0,8},{1,5},{2,10},{3,7},{4,12},{5,1},{6,14},{7,3},{16,24},{17,21}... | collective-permute-start | bytes 2703368 | tf_op jit(solution)/shard_map/ppermute | solution.py:346
  51.2 24.5 %collective-permute-start.6 = (bf16[4,55,16,128]{3,2,1,0:T(8,128)(2,1)S(1)}, bf16[4,55,16,128]{3,2,1,0:T(8,128)(2,1)S(1)}, u32[]{:S(2)}, u32[]{:S(2)}) collective-permute-start(bf16[4,55,16,128]{3,2,1,0:T(8,128)(2,1)S(1)} %all-to-all-done.1.m0), channel_id=1, source_target_pairs={{0,24},{1,7},{2,26},{3,1},{4,28},{5,3},{6,30},{7,5},{16,0},{17,23}... | collective-permute-start | bytes 2703368 | tf_op jit(solution)/shard_map/ppermute | solution.py:345
  56.5 25.9 %collective-permute-start.5 = (bf16[4,55,16,128]{3,2,1,0:T(8,128)(2,1)S(1)}, bf16[4,55,16,128]{3,2,1,0:T(8,128)(2,1)S(1)}, u32[]{:S(2)}, u32[]{:S(2)}) collective-permute-start(bf16[4,55,16,128]{3,2,1,0:T(8,128)(2,1)S(1)} %all-to-all-done.1.m0), channel_id=1, source_target_pairs={{0,16},{1,3},{2,18},{3,5},{4,20},{5,7},{6,22},{7,1},{16,8},{17,19}... | collective-permute-start | bytes 2703368 | tf_op jit(solution)/shard_map/ppermute | solution.py:344
  60.8 25.1 %collective-permute-start.11 = (bf16[4096,128]{1,0:T(8,128)(2,1)S(1)}, bf16[4096,128]{1,0:T(8,128)(2,1)S(1)}, u32[]{:S(2)}, u32[]{:S(2)}) collective-permute-start(bf16[4096,128]{1,0:T(8,128)(2,1)S(1)} %constant_dynamic-update-slice_fusion.near_ref), channel_id=1, source_target_pairs={{0,1},{1,0},{2,3},{3,2},{4,5},{5,4},{6,7},{7,6},{16,17},{17,16},{1... | collective-permute-start | bytes 3145736 | tf_op jit(solution)/shard_map/ppermute | solution.py:363
  68.5 16.4 %collective-permute-start.7 = (bf16[4,55,16,128]{3,2,1,0:T(8,128)(2,1)S(1)}, bf16[4,55,16,128]{3,2,1,0:T(8,128)(2,1)S(1)}, u32[]{:S(2)}, u32[]{:S(2)}) collective-permute-start(bf16[4,55,16,128]{3,2,1,0:T(8,128)(2,1)S(1)} %all-to-all-done.1.m0), channel_id=1, source_target_pairs={{0,1},{1,0},{2,3},{3,2},{4,5},{5,4},{6,7},{7,6},{16,17},{17,16},{1... | collective-permute-start | bytes 2703368 | tf_op jit(solution)/shard_map/ppermute | solution.py:362
  70.5 14.5 %collective-permute-start.8 = (bf16[4,55,16,128]{3,2,1,0:T(8,128)(2,1)S(1)}, bf16[4,55,16,128]{3,2,1,0:T(8,128)(2,1)S(1)}, u32[]{:S(2)}, u32[]{:S(2)}) collective-permute-start(bf16[4,55,16,128]{3,2,1,0:T(8,128)(2,1)S(1)} %collective-permute-done.4.m1), channel_id=1, source_target_pairs={{0,1},{1,0},{2,3},{3,2},{4,5},{5,4},{6,7},{7,6},{16,17},{17,16},{1... | collective-permute-start | bytes 2703368 | tf_op jit(solution)/shard_map/ppermute | solution.py:365
  75.7 10.2 %collective-permute-start.10 = (bf16[4,55,16,128]{3,2,1,0:T(8,128)(2,1)S(1)}, bf16[4,55,16,128]{3,2,1,0:T(8,128)(2,1)S(1)}, u32[]{:S(2)}, u32[]{:S(2)}) collective-permute-start(bf16[4,55,16,128]{3,2,1,0:T(8,128)(2,1)S(1)} %collective-permute-done.6.m3), channel_id=1, source_target_pairs={{0,1},{1,0},{2,3},{3,2},{4,5},{5,4},{6,7},{7,6},{16,17},{17,16},{1... | collective-permute-start | bytes 2703368 | tf_op jit(solution)/shard_map/ppermute | solution.py:374
  82.4 4.3 %collective-permute-start.9 = (bf16[4,55,16,128]{3,2,1,0:T(8,128)(2,1)S(1)}, bf16[4,55,16,128]{3,2,1,0:T(8,128)(2,1)S(1)}, u32[]{:S(2)}, u32[]{:S(2)}) collective-permute-start(bf16[4,55,16,128]{3,2,1,0:T(8,128)(2,1)S(1)} %collective-permute-done.5.m2), channel_id=1, source_target_pairs={{0,1},{1,0},{2,3},{3,2},{4,5},{5,4},{6,7},{7,6},{16,17},{17,16},{1... | collective-permute-start | bytes 2703368 | tf_op jit(solution)/shard_map/ppermute | solution.py:364
